TPU v7x, 256 devices: a whole 4x4x8 slice. The times are simulated.
256 devices in a mesh: layer: 4 (over x_hi, core), feat: 64 (over z, y, x_lo).
Axes of the slice: x: 4 (x_hi: 2, x_lo: 2; x = x_hi * 2 + x_lo), y: 4, z: 8, core: 2. Of those that a mesh axis runs over, the one named last changes fastest.
Arguments:
- layer_acts: bfloat16 [4, 512, 576], P('layer', 'feat'), may hold values from -6 to 6
- enc_weight: bfloat16 [4, 576, 131072], P('layer', None, 'feat'), may hold values from -6 to 6
- dec_weight: bfloat16 [4, 131072, 576], P('layer', 'feat'), may hold values from -6 to 6
- enc_bias: float32 [131072], P('feat'), may hold values from -4 to 4
- dec_bias: float32 [4, 576], P('layer'), may hold values from -4 to 4
Outputs:
- enc_step: bfloat16 [4, 576, 131072], P('layer', None, 'feat')
- dec_step: bfloat16 [4, 131072, 576], P('layer', 'feat')
All inputs are finite; a program needn't handle non-finite values.
Results may differ from a plain program's by a relative error of at most 0.012.
Values may be sent and summed in bfloat16 or wider, within the bound.
No kernel may reach another device: no remote copies, remote signals or barrier semaphores. Data moves between devices by JAX's collectives and lax.ppermute only.
A program may use at most 64 MiB of HBM per device.

v0:
```python
import jax
import jax.numpy as jnp
from jax import lax
from jax.sharding import PartitionSpec as P

LEARN_RATE = 4.0


def contract_rows(left, right):
    return lax.dot_general(
        left, right, (((0,), (0,)), ((), ())), preferred_element_type=jnp.float32
    )


def body(layer_acts, enc_weight, dec_weight, enc_bias, dec_bias):
    tok_local = layer_acts[0]
    enc_local = enc_weight[0]
    dec_local = dec_weight[0]
    model_width = enc_local.shape[0]
    slab_width = enc_local.shape[1]
    enc_scale = (layer_acts.shape[0] * lax.axis_size("layer") * model_width) ** (-0.5)
    dec_scale = (slab_width * lax.axis_size("feat")) ** (-0.5)
    whole_tokens = lax.all_gather(tok_local, "feat", axis=0, tiled=True)
    partial_value = jnp.dot(whole_tokens, enc_local, preferred_element_type=jnp.float32)
    preact = enc_scale * lax.psum(partial_value, "layer") + enc_bias
    active_b = jnp.maximum(preact, 0.0).astype(jnp.bfloat16)
    recon = lax.psum_scatter(
        dec_scale * jnp.dot(active_b, dec_local, preferred_element_type=jnp.float32),
        "feat",
        scatter_dimension=0,
        tiled=True,
    )
    error_b = (recon + dec_bias[0] - tok_local.astype(jnp.float32)).astype(jnp.bfloat16)
    whole_errors = lax.all_gather(error_b, "feat", axis=0, tiled=True)
    grad_dec = contract_rows(active_b, whole_errors)
    act_terms = dec_scale * lax.dot_general(
        whole_errors, dec_local, (((1,), (1,)), ((), ())), preferred_element_type=jnp.float32
    )
    grad_act = lax.psum(act_terms, "layer")
    grad_pre = jnp.where(preact > 0.0, grad_act, 0.0).astype(jnp.bfloat16)
    tokens_later = lax.all_gather(tok_local, "feat", axis=0, tiled=True)
    grad_enc = contract_rows(tokens_later, grad_pre)
    enc_step = (-LEARN_RATE * enc_scale * grad_enc).astype(jnp.bfloat16)[None]
    dec_step = (-LEARN_RATE * dec_scale * grad_dec).astype(jnp.bfloat16)[None]
    return (enc_step, dec_step)


def solution(mesh):
    in_specs = (
        P("layer", "feat", None),
        P("layer", None, "feat"),
        P("layer", "feat", None),
        P("feat"),
        P("layer", None),
    )
    out_specs = (P("layer", None, "feat"), P("layer", "feat", None))
    return jax.shard_map(body, mesh=mesh, in_specs=in_specs, out_specs=out_specs, check_vma=False)
```

profile of v0, /device:TPU:1, one launch (start us, length us, event | category | flops | bytes accessed | tf_op | source)
XLA Modules:
  0.0 1121.1 jit_solution(10872791915528842918)
XLA Ops:
  7.2 0.0 copy-start
  7.2 0.0 all-reduce.5.cloned.1.call-start
  7.2 135.9 %all-gather = bf16[1,512,576]{2,1,0:T(8,128)(2,1)S(1)} all-gather(bf16[1,8,576]{2,1,0:T(8,128)(2,1)} %param.5), channel_id=2, replica_groups=mesh['layer'=4,'feat'=64] {'feat'}, dimensions={1}, use_global_device_ids=true | all-gather | bytes 599040 | tf_op jit(solution)/shard_map/all_gather | solution.py:41
  143.1 0.0 copy-start.6
  143.1 5.5 fusion.5
  148.5 0.0 all-reduce.5.cloned.1.call-update
  148.6 0.0 copy-start.7
  148.6 0.0 copy-start.4
  148.6 0.0 copy-start.3
  148.6 0.0 all-reduce.7.cloned.1.call-start
  148.7 120.8 %all-reduce.5.cloned.1.call-done = f32[512,2048]{1,0:T(8,128)} async-done(((f32[512,2048]{1,0:T(8,128)}), f32[512,2048]{1,0:T(8,128)}) %all-reduce.5.cloned.1.call-update) | async-done | bytes 4194320 | tf_op jit(solution)/shard_map/psum | solution.py:25
  269.5 0.0 copy-done
  269.5 0.0 copy-done.6
  269.5 5.1 fusion.10
  274.6 0.0 all-reduce.7.cloned.1.call-update
  274.6 0.0 copy-done.7
  274.6 0.6 dynamic-slice
  275.9 0.0 copy-done.4
  275.9 550.6 %all-reduce.7.cloned.1.call-done = f32[512,576]{1,0:T(8,128)} async-done(((f32[512,576]{1,0:T(8,128)}), f32[512,576]{1,0:T(8,128)}) %all-reduce.7.cloned.1.call-update) | async-done | bytes 1179664
  826.5 0.0 copy-done.3
  826.5 0.7 fusion.15
  827.2 129.8 %all_gather.8 = bf16[512,576]{1,0:T(8,128)(2,1)S(1)} all-gather(bf16[8,576]{1,0:T(8,128)(2,1)S(1)} %fusion.15), channel_id=1, replica_groups=mesh['layer'=4,'feat'=64] {'feat'}, dimensions={0}, use_global_device_ids=true | all-gather | bytes 599040 | tf_op jit(solution)/shard_map/all_gather | solution.py:34
  957.0 0.0 copy-start.2
  957.0 0.9 copy-done.2
  957.9 3.8 convolution_multiply_fusion
  961.7 144.2 %all-reduce.8 = bf16[512,2048]{1,0:T(8,128)(2,1)} all-reduce(f32[512,2048]{1,0:T(8,128)} %convolution_multiply_fusion), channel_id=1, replica_groups=mesh['layer'=4,'feat'=64] {'layer'}, use_global_device_ids=true, to_apply=%region_2.0 | all-reduce | flops 1048576 | bytes 6291456 | tf_op jit(solution)/shard_map/psum | solution.py:39
  1105.9 0.0 copy-start.1
  1105.9 0.0 copy-start.5
  1105.9 5.4 fusion.1
  1111.3 0.0 copy-done.1
  1111.3 0.0 copy-done.5
  1111.3 3.0 fusion
  (1 shorter events, 0.0 us)
Async XLA Ops:
  7.2 262.3 %copy-start = (bf16[1,2048,576]{1,2,0:T(8,128)(2,1)S(1)}, bf16[1,2048,576]{1,2,0:T(8,128)(2,1)}, u32[]{:S(2)}) copy-start(bf16[1,2048,576]{1,2,0:T(8,128)(2,1)} %param.7) | copy-start | bytes 7077892
  7.2 262.3 %all-reduce.5.cloned.1.call-start = ((), (), s32[]{:S(2)}) async-start(), calls=%async_computation | async-start | bytes 8388608 | tf_op jit(solution)/shard_map/psum | solution.py:25
  143.1 126.4 %copy-start.6 = (f32[2048]{0:T(1024)S(1)}, f32[2048]{0:T(1024)}, u32[]{:S(2)}) copy-start(f32[2048]{0:T(1024)} %param.8) | copy-start | bytes 24580
  148.6 126.0 %copy-start.7 = (u32[256]{0:T(256)S(1)}, u32[256]{0:T(256)}, u32[]{:S(2)}) copy-start(u32[256]{0:T(256)} %constant.18) | copy-start | bytes 3076
  148.6 127.3 %copy-start.4 = (f32[1,576]{1,0:T(1,128)S(1)}, f32[1,576]{1,0:T(1,128)}, u32[]{:S(2)}) copy-start(f32[1,576]{1,0:T(1,128)} %param.9) | copy-start | bytes 6916
  148.6 677.9 %copy-start.3 = (bf16[1,8,576]{2,1,0:T(8,128)(2,1)S(1)}, bf16[1,8,576]{2,1,0:T(8,128)(2,1)}, u32[]{:S(2)}) copy-start(bf16[1,8,576]{2,1,0:T(8,128)(2,1)} %param.5) | copy-start | bytes 27652
  148.6 677.9 %all-reduce.7.cloned.1.call-start = ((), (), s32[]{:S(2)}) async-start(), calls=%async_computation.1 | async-start | bytes 2621440
  957.0 0.9 copy-start.2
  1105.9 5.4 copy-start.1
  1105.9 5.4 copy-start.5
Sparse Core Ops, SparseCore 0:
  148.7 120.7 all-reduce.4
  274.7 551.7 all-reduce.6
where the time goes:
time: 1120 us
  waiting for transfers between devices  671 us (60%)
  blocking collectives  410 us (37%)
  matrix products  22.7 us (2%)
  between operations  14.8 us (1%)
    unnamed x3, waiting for transfers between devices  551 us
    psum x1, blocking collectives, body(): grad_act = lax.psum(act_terms, 'layer')  144 us
    all_gather x1, blocking collectives, body(): tokens_later = lax.all_gather(tok_local, 'feat', axis=0, tiled=True)  136 us
    all_gather x1, blocking collectives, body(): whole_errors = lax.all_gather(error_b, 'feat', axis=0, tiled=True)  130 us
    psum x1, waiting for transfers between devices, body(): preact = enc_scale * lax.psum(partial_value, 'layer') + enc_bias  121 us
  transfers between devices with their start and end apart: 2, of which 2 were waited for; matrix products, arithmetic and copies ran while one was open for 0% of the time, Pallas kernels for 0%

commit v1 on v0

v1 whole, which is shorter than its diff:
```python
import jax
import jax.numpy as jnp
from jax import lax
from jax.sharding import PartitionSpec as P

LEARN_RATE = 4.0
BF16 = jnp.bfloat16
F32 = jnp.float32
ACROSS_CORES = [(0, 1), (1, 0), (2, 3), (3, 2)]
ACROSS_CHIPS = [(0, 2), (1, 3), (2, 0), (3, 1)]


def to_core(value):
    return lax.ppermute(value, "layer", ACROSS_CORES)


def to_chip(value):
    return lax.ppermute(value, "layer", ACROSS_CHIPS)


def gather_tokens(value):
    blocks = lax.axis_size("feat")
    rows, width = value.shape
    copies = jnp.broadcast_to(value[None], (blocks, rows, width))
    return lax.all_to_all(copies, "feat", 0, 0, tiled=True).reshape(blocks * rows, width)


def rows_of(value, start, count):
    return lax.dynamic_slice_in_dim(value, start, count, axis=0)


def dot(left, right):
    return jnp.dot(left, right, preferred_element_type=F32)


def dot_transposed(left, right):
    return lax.dot_general(left, right, (((1,), (1,)), ((), ())), preferred_element_type=F32)


def contract_rows(left, right):
    return lax.dot_general(left, right, (((0,), (0,)), ((), ())), preferred_element_type=F32)


def body(layer_acts, enc_weight, dec_weight, enc_bias, dec_bias):
    tok_local = layer_acts[0]
    enc_local = enc_weight[0]
    dec_local = dec_weight[0]
    bias = enc_bias[None, :]
    model_width, slab_width = enc_local.shape
    blocks = lax.axis_size("feat")
    enc_scale = (layer_acts.shape[0] * lax.axis_size("layer") * model_width) ** (-0.5)
    dec_scale = (slab_width * blocks) ** (-0.5)
    tokens = tok_local.shape[0] * blocks
    half, quarter = tokens // 2, tokens // 4
    place = lax.axis_index("layer")
    chip, core = place // 2, place % 2

    def quarter_at(core_index, chip_index):
        return core_index * half + chip_index * quarter

    mine = quarter_at(core, chip)
    of_chip = quarter_at(core, 1 - chip)
    of_core = quarter_at(1 - core, chip)
    of_both = quarter_at(1 - core, 1 - chip)

    whole_tokens = gather_tokens(tok_local)

    def encode(start):
        return dot(rows_of(whole_tokens, start, quarter), enc_local)

    sum_of_chip = encode(of_chip) + to_core(encode(of_both))
    arrived = to_chip(sum_of_chip)
    sum_mine = encode(mine) + to_core(encode(of_core))
    preact = enc_scale * (sum_mine + arrived) + bias
    active_mine = jnp.maximum(preact, 0.0).astype(BF16)
    active_of_chip = to_chip(active_mine)
    active_of_core = to_core(active_mine)
    active_of_both = to_core(active_of_chip)

    pieces = (
        (mine, active_mine),
        (of_core, active_of_core),
        (of_chip, active_of_chip),
        (of_both, active_of_both),
    )
    recon_terms = jnp.zeros((tokens, model_width), BF16)
    for start, active in pieces:
        term = (dec_scale * dot(active, dec_local)).astype(BF16)
        recon_terms = lax.dynamic_update_slice_in_dim(recon_terms, term, start, axis=0)
    arrived_terms = lax.all_to_all(
        recon_terms.reshape(blocks, tokens // blocks, model_width), "feat", 0, 0, tiled=True
    )
    recon = jnp.sum(arrived_terms.astype(F32), axis=0)
    error_b = (recon + dec_bias[0] - tok_local.astype(F32)).astype(BF16)
    whole_errors = gather_tokens(error_b)

    def enc_rows(starts):
        return jnp.concatenate([rows_of(whole_tokens, start, quarter) for start in starts])

    own_rows = (mine, of_chip)
    other_rows = (of_core, of_both)
    errors_other = jnp.concatenate([rows_of(whole_errors, start, quarter) for start in other_rows])
    errors_own = jnp.concatenate([rows_of(whole_errors, start, quarter) for start in own_rows])
    grad_other = dot_transposed(errors_other, dec_local).astype(BF16)
    grad_from_core = to_core(grad_other).astype(F32)
    grad_pair = dot_transposed(errors_own, dec_local) + grad_from_core
    grad_pair_b = grad_pair.astype(BF16)
    from_chip = to_chip(grad_pair_b).astype(F32)
    from_chip = jnp.concatenate([from_chip[quarter:], from_chip[:quarter]])
    grad_act = dec_scale * (grad_pair + from_chip)
    active_own = jnp.concatenate([active_mine, active_of_chip])
    grad_pre_own = jnp.where(active_own > 0, grad_act, 0.0).astype(BF16)
    grad_pre_other = to_core(grad_pre_own)

    active_all = jnp.concatenate([active for _, active in pieces])
    errors_all = jnp.concatenate([rows_of(whole_errors, start, quarter) for start, _ in pieces])
    grad_dec = contract_rows(active_all, errors_all)
    grad_enc = contract_rows(enc_rows(own_rows + other_rows), jnp.concatenate([grad_pre_own, grad_pre_other]))
    enc_step = (-LEARN_RATE * enc_scale * grad_enc).astype(BF16)[None]
    dec_step = (-LEARN_RATE * dec_scale * grad_dec).astype(BF16)[None]
    return (enc_step, dec_step)


def solution(mesh):
    in_specs = (
        P("layer", "feat", None),
        P("layer", None, "feat"),
        P("layer", "feat", None),
        P("feat"),
        P("layer", None),
    )
    out_specs = (P("layer", None, "feat"), P("layer", "feat", None))
    return jax.shard_map(body, mesh=mesh, in_specs=in_specs, out_specs=out_specs, check_vma=False)
```

time: 1120 us -> 194 us (0.17)
  waiting for transfers between devices: 671 us -> 92.7 us
  blocking collectives: 410 us -> 23.8 us
  starting transfers between devices: 0.08 us -> 38.4 us
  between operations: 14.8 us -> 0.95 us
  local copies, waits for them, and re-layouts: 1.53 us -> 12.8 us
    unnamed x3 -> x0, waiting for transfers between devices: 551 us -> none
    all_gather x2 -> x0, blocking collectives: 266 us -> none  [the longest x1 136 us: body(): tokens_later = lax.all_gather(tok_local, 'feat', axis=0, tiled=True)]
    psum x1 -> x0, blocking collectives: 144 us -> none  [body(): grad_act = lax.psum(act_terms, 'layer')]
    psum x1 -> x0, waiting for transfers between devices: 121 us -> none  [body(): preact = enc_scale * lax.psum(partial_value, 'layer') + enc_bias]
    ppermute x0 -> x9, waiting for transfers between devices: none -> 56.5 us  [the longest x3 52.7 us: to_chip(): return lax.ppermute(value, 'layer', ACROSS_CHIPS)]
    all_to_all x0 -> x2, waiting for transfers between devices: none -> 36.2 us  [the longest x1 18.3 us: body(): lax.all_to_all(recon_terms.reshape(blocks, tokens // blocks, model_width)...]
    all_to_all x0 -> x1, blocking collectives: none -> 23.8 us  [gather_tokens(): lax.all_to_all(copies, 'feat', 0, 0, tiled=True)]
    ppermute x0 -> x9, starting transfers between devices: none -> 19.5 us  [the longest x6 11.9 us: to_core(): return lax.ppermute(value, 'layer', ACROSS_CORES)]
  transfers between devices with their start and end apart: 2 -> 11, of which waited for: 2 -> 7; matrix products, arithmetic and copies ran while one was open for 0% -> 10% of each run, Pallas kernels for 0% -> 0%
where the time goes in v1:
time: 194 us; the launch traced here: 193 us
  waiting for transfers between devices  92.7 us (48%)
  starting transfers between devices  38.4 us (20%)
  blocking collectives  23.8 us (12%)
  matrix products  21.7 us (11%)
  local copies, waits for them, and re-layouts  12.8 us (7%)
  other arithmetic  2.56 us (1%)
    ppermute x3, waiting for transfers between devices, to_chip(): return lax.ppermute(value, 'layer', ACROSS_CHIPS)  52.7 us
    all_to_all x1, blocking collectives, gather_tokens(): lax.all_to_all(copies, 'feat', 0, 0, tiled=True)  23.8 us
    all_to_all x1, waiting for transfers between devices, body(): lax.all_to_all(recon_terms.reshape(blocks, tokens // blocks, model_width)...  18.3 us
    all_to_all x1, waiting for transfers between devices, gather_tokens(): lax.all_to_all(copies, 'feat', 0, 0, tiled=True)  17.9 us
    all_to_all x1, starting transfers between devices, gather_tokens(): lax.all_to_all(copies, 'feat', 0, 0, tiled=True)  13.6 us
    dot_general x8, matrix products, dot(): return jnp.dot(left, right, preferred_element_type=F32)  12.7 us
    ppermute x6, starting transfers between devices, to_core(): return lax.ppermute(value, 'layer', ACROSS_CORES)  11.9 us
    ppermute x3, starting transfers between devices, to_chip(): return lax.ppermute(value, 'layer', ACROSS_CHIPS)  7.53 us
  transfers between devices with their start and end apart: 11, of which 7 were waited for; matrix products, arithmetic and copies ran while one was open for 10% of the time, Pallas kernels for 0%

profile of v1, /device:TPU:1, one launch (start us, length us, event | category | flops | bytes accessed | tf_op | source)
XLA Modules:
  0.0 193.0 jit_solution(13048173471397381703)
XLA Ops:
  0.6 1.7 broadcast_in_dim.30
  2.4 13.6 %all-to-all-start = ((bf16[64,8,576]{2,1,0:T(8,128)(2,1)}), bf16[64,8,576]{2,1,0:T(8,128)(2,1)S(1)}, u32[]{:S(2)}, u32[]{:S(2)}) async-start(bf16[64,8,576]{2,1,0:T(8,128)(2,1)} %broadcast_in_dim.30), calls=%async_computation | async-start | bytes 1310720 | tf_op jit(solution)/shard_map/all_to_all | solution.py:25
  16.0 17.9 %all-to-all-done = bf16[64,8,576]{2,1,0:T(8,128)(2,1)S(1)} async-done(((bf16[64,8,576]{2,1,0:T(8,128)(2,1)}), bf16[64,8,576]{2,1,0:T(8,128)(2,1)S(1)}, u32[]{:S(2)}, u32[]{:S(2)}) %all-to-all-start) | async-done | bytes 589856 | tf_op jit(solution)/shard_map/all_to_all | solution.py:25
  34.0 2.5 %fusion.18 = f32[128,2048]{1,0:T(8,128)S(1)} fusion(bf16[128,576]{1,0:T(8,128)(2,1)S(1)} %get-tuple-element.9, bf16[1,576,2048]{2,1,0:T(8,128)(2,1)} %param.6), kind=kOutput, calls=%fused_computation.23 | convolution fusion | flops 301989888 | bytes 3555328 | tf_op jit(solution)/shard_map/dot_general | solution.py:33
  36.6 3.8 %collective-permute-start.1 = (f32[128,2048]{1,0:T(8,128)S(1)}, f32[128,2048]{1,0:T(8,128)S(1)}, u32[]{:S(2)}, u32[]{:S(2)}) collective-permute-start(f32[128,2048]{1,0:T(8,128)S(1)} %fusion.18), channel_id=1, source_target_pairs={{0,64},{64,0},{128,192},{192,128},{1,65},{65,1},{129,193},{193,129... | collective-permute-start | bytes 3145736 | tf_op jit(solution)/shard_map/ppermute | solution.py:14
  41.1 1.5 collective-permute-done.1
  43.2 2.5 %collective-permute-start.2 = (f32[128,2048]{1,0:T(8,128)S(1)}, f32[128,2048]{1,0:T(8,128)S(1)}, u32[]{:S(2)}, u32[]{:S(2)}) collective-permute-start(f32[128,2048]{1,0:T(8,128)S(1)} %convolution_add_fusion), channel_id=1, source_target_pairs={{0,128},{64,192},{128,0},{192,64},{1,129},{65,193},{129,1},{193,65... | collective-permute-start | bytes 3145736 | tf_op jit(solution)/shard_map/ppermute | solution.py:18
  45.8 23.4 %collective-permute-done.2 = f32[128,2048]{1,0:T(8,128)S(1)} collective-permute-done((f32[128,2048]{1,0:T(8,128)S(1)}, f32[128,2048]{1,0:T(8,128)S(1)}, u32[]{:S(2)}, u32[]{:S(2)}) %collective-permute-start.2) | collective-permute-done | bytes 1048608 | tf_op jit(solution)/shard_map/ppermute | solution.py:18
  69.9 1.3 collective-permute-start.4
  71.2 2.5 %collective-permute-start.3 = (bf16[128,2048]{1,0:T(8,128)(2,1)S(1)}, bf16[128,2048]{1,0:T(8,128)(2,1)}, u32[]{:S(2)}, u32[]{:S(2)}) collective-permute-start(bf16[128,2048]{1,0:T(8,128)(2,1)S(1)} %fusion.6), channel_id=1, source_target_pairs={{0,128},{64,192},{128,0},{192,64},{1,129},{65,193},{129,1},{193,65... | collective-permute-start | bytes 1572872 | tf_op jit(solution)/shard_map/ppermute | solution.py:18
  75.3 0.9 constant_dynamic-update-slice_fusion.3
  76.3 2.5 %fusion.56 = bf16[128,576]{0,1:T(8,128)(2,1)} fusion(bf16[128,2048]{1,0:T(8,128)(2,1)} %collective-permute-done.4, bf16[1,2048,576]{1,2,0:T(8,128)(2,1)S(1)} %copy-done), kind=kOutput, calls=%fused_computation.52 | convolution fusion | flops 302137344 | bytes 3031040 | tf_op jit(solution)/shard_map/dot_general | solution.py:33
  78.8 1.7 copy.8
  80.5 5.8 %collective-permute-done.3 = bf16[128,2048]{1,0:T(8,128)(2,1)} collective-permute-done((bf16[128,2048]{1,0:T(8,128)(2,1)S(1)}, bf16[128,2048]{1,0:T(8,128)(2,1)}, u32[]{:S(2)}, u32[]{:S(2)}) %collective-permute-start.3) | collective-permute-done | bytes 524320 | tf_op jit(solution)/shard_map/ppermute | solution.py:18
  87.2 2.5 %fusion.53 = bf16[128,576]{0,1:T(8,128)(2,1)} fusion(bf16[128,2048]{1,0:T(8,128)(2,1)} %collective-permute-done.3, bf16[1,2048,576]{1,2,0:T(8,128)(2,1)S(1)} %copy-done), kind=kOutput, calls=%fused_computation.51 | convolution fusion | flops 302137344 | bytes 3031040 | tf_op jit(solution)/shard_map/dot_general | solution.py:33
  89.7 1.7 copy.9
  92.3 0.9 constant_dynamic-update-slice_fusion.1
  93.3 2.5 %fusion.50 = bf16[128,576]{0,1:T(8,128)(2,1)} fusion(bf16[128,2048]{1,0:T(8,128)(2,1)} %collective-permute-done.5, bf16[1,2048,576]{1,2,0:T(8,128)(2,1)S(1)} %copy-done), kind=kOutput, calls=%fused_computation.50 | convolution fusion | flops 302137344 | bytes 3031040 | tf_op jit(solution)/shard_map/dot_general | solution.py:33
  95.8 1.7 copy.10
  99.2 5.4 %all-to-all-start.1 = ((bf16[64,8,576]{2,1,0:T(8,128)(2,1)}), bf16[64,8,576]{2,1,0:T(8,128)(2,1)S(1)}, u32[]{:S(2)}, u32[]{:S(2)}) async-start(bf16[64,8,576]{2,1,0:T(8,128)(2,1)} %bitcast.68), calls=%async_computation.1 | async-start | bytes 1310720 | tf_op jit(solution)/shard_map/all_to_all | solution.py:90
  105.3 18.3 %all-to-all-done.1 = bf16[64,8,576]{2,1,0:T(8,128)(2,1)S(1)} async-done(((bf16[64,8,576]{2,1,0:T(8,128)(2,1)}), bf16[64,8,576]{2,1,0:T(8,128)(2,1)S(1)}, u32[]{:S(2)}, u32[]{:S(2)}) %all-to-all-start.1) | async-done | bytes 589856 | tf_op jit(solution)/shard_map/all_to_all | solution.py:90
  123.8 23.8 %all_to_all.15 = bf16[64,8,576]{2,1,0:T(8,128)(2,1)S(1)} all-to-all(bf16[64,8,576]{2,1,0:T(8,128)(2,1)S(1)} %broadcast_in_dim.33), channel_id=1, replica_groups=mesh['layer'=4,'feat'=64] {'feat'}, dimensions={0} | all-to-all | bytes 1179648 | tf_op jit(solution)/shard_map/all_to_all | solution.py:25
  147.7 1.0 convolution_convert_fusion
  148.7 4.6 %collective-permute-start.6 = (bf16[256,2048]{1,0:T(8,128)(2,1)S(1)}, bf16[256,2048]{1,0:T(8,128)(2,1)S(1)}, u32[]{:S(2)}, u32[]{:S(2)}) collective-permute-start(bf16[256,2048]{1,0:T(8,128)(2,1)S(1)} %convolution_convert_fusion), channel_id=1, source_target_pairs={{0,64},{64,0},{128,192},{192,128},{1,65},{65,1},{129,193},{193,129... | collective-permute-start | bytes 3145736 | tf_op jit(solution)/shard_map/ppermute | solution.py:14
  153.3 2.3 %collective-permute-done.6 = bf16[256,2048]{1,0:T(8,128)(2,1)S(1)} collective-permute-done((bf16[256,2048]{1,0:T(8,128)(2,1)S(1)}, bf16[256,2048]{1,0:T(8,128)(2,1)S(1)}, u32[]{:S(2)}, u32[]{:S(2)}) %collective-permute-start.6) | collective-permute-done | bytes 1048608 | tf_op jit(solution)/shard_map/ppermute | solution.py:14
  155.6 1.0 fusion.37
  156.6 2.5 %collective-permute-start.7 = (bf16[256,2048]{1,0:T(8,128)(2,1)S(1)}, bf16[256,2048]{1,0:T(8,128)(2,1)S(1)}, u32[]{:S(2)}, u32[]{:S(2)}) collective-permute-start(bf16[256,2048]{1,0:T(8,128)(2,1)S(1)} %get-tuple-element.12), channel_id=1, source_target_pairs={{0,128},{64,192},{128,0},{192,64},{1,129},{65,193},{129,1},{193,65... | collective-permute-start | bytes 3145736 | tf_op jit(solution)/shard_map/ppermute | solution.py:18
  159.1 23.4 %collective-permute-done.7 = bf16[256,2048]{1,0:T(8,128)(2,1)S(1)} collective-permute-done((bf16[256,2048]{1,0:T(8,128)(2,1)S(1)}, bf16[256,2048]{1,0:T(8,128)(2,1)S(1)}, u32[]{:S(2)}, u32[]{:S(2)}) %collective-permute-start.7) | collective-permute-done | bytes 1048608 | tf_op jit(solution)/shard_map/ppermute | solution.py:18
  182.8 1.7 fusion.26
  184.6 1.3 collective-permute-start.8
  185.9 4.2 %fusion.1 = bf16[1,2048,576]{1,2,0:T(8,128)(2,1)} fusion(bf16[128,2048]{1,0:T(8,128)(2,1)} %collective-permute-done.5, bf16[128,2048]{1,0:T(8,128)(2,1)} %collective-permute-done.3, bf16[128,2048]{1,0:T(8,128)(2,1)} %collective-permute-done.4, bf16[128,2048]{1,0:T(8,128)(2,1)S(1)} %fusion.6, bf16[128,576]{1,0:T(8,128)(2,1)S(1)} %get-tuple-element.5, ...), kind=kOutput, calls=%fused_computation.3 | convolution fusion | flops 1221066752 | bytes 5046272 | tf_op jit(solution)/shard_map/dot_general | solution.py:41
  190.1 2.8 %fusion = bf16[1,576,2048]{2,1,0:T(8,128)(2,1)} fusion(bf16[256,2048]{1,0:T(8,128)(2,1)S(1)} %collective-permute-done.8, bf16[256,2048]{1,0:T(8,128)(2,1)S(1)} %fusion.26, bf16[128,576]{1,0:T(8,128)(2,1)S(1)} %copy-done.4, bf16[128,576]{1,0:T(8,128)(2,1)S(1)} %copy-done.6, bf16[128,576]{1,0:T(8,128)(2,1)S(1)} %copy-done.10, bf16[128,576]{1,0:T(8,128)(2,1)S(1)} %copy-done.8), kind=kOutput, calls=%fused_computation.2 | convolution fusion | flops 1216872448 | bytes 5046272 | tf_op jit(solution)/shard_map/dot_general | solution.py:41
  (47 shorter events, 8.6 us)
Async XLA Ops:
  0.6 73.1 %copy-start = (bf16[1,2048,576]{1,2,0:T(8,128)(2,1)S(1)}, bf16[1,2048,576]{1,2,0:T(8,128)(2,1)}, u32[]{:S(2)}) copy-start(bf16[1,2048,576]{1,2,0:T(8,128)(2,1)} %param.7) | copy-start | bytes 7077892
  2.4 31.5 %all-to-all-start = ((bf16[64,8,576]{2,1,0:T(8,128)(2,1)}), bf16[64,8,576]{2,1,0:T(8,128)(2,1)S(1)}, u32[]{:S(2)}, u32[]{:S(2)}) async-start(bf16[64,8,576]{2,1,0:T(8,128)(2,1)} %broadcast_in_dim.30), calls=%async_computation | async-start | bytes 1310720 | tf_op jit(solution)/shard_map/all_to_all | solution.py:25
  33.9 6.4 %copy-start.1 = (bf16[1,576,2048]{2,1,0:T(8,128)(2,1)S(1)}, bf16[1,576,2048]{2,1,0:T(8,128)(2,1)}, u32[]{:S(2)}) copy-start(bf16[1,576,2048]{2,1,0:T(8,128)(2,1)} %param.6) | copy-start | bytes 7077892
  34.0 7.0 %copy-start.3 = (bf16[128,576]{1,0:T(8,128)(2,1)}, bf16[128,576]{1,0:T(8,128)(2,1)S(1)}, u32[]{:S(2)}) copy-start(bf16[128,576]{1,0:T(8,128)(2,1)S(1)} %get-tuple-element.9) | copy-start | bytes 442372
  34.0 7.0 %copy-start.5 = (bf16[128,576]{1,0:T(8,128)(2,1)}, bf16[128,576]{1,0:T(8,128)(2,1)S(1)}, u32[]{:S(2)}) copy-start(bf16[128,576]{1,0:T(8,128)(2,1)S(1)} %get-tuple-element.10) | copy-start | bytes 442372
  34.0 8.6 %copy-start.9 = (bf16[128,576]{1,0:T(8,128)(2,1)}, bf16[128,576]{1,0:T(8,128)(2,1)S(1)}, u32[]{:S(2)}) copy-start(bf16[128,576]{1,0:T(8,128)(2,1)S(1)} %get-tuple-element.11) | copy-start | bytes 442372
  34.0 35.2 %copy-start.7 = (bf16[128,576]{1,0:T(8,128)(2,1)}, bf16[128,576]{1,0:T(8,128)(2,1)S(1)}, u32[]{:S(2)}) copy-start(bf16[128,576]{1,0:T(8,128)(2,1)S(1)} %get-tuple-element.8) | copy-start | bytes 442372
  36.6 6.1 %collective-permute-start.1 = (f32[128,2048]{1,0:T(8,128)S(1)}, f32[128,2048]{1,0:T(8,128)S(1)}, u32[]{:S(2)}, u32[]{:S(2)}) collective-permute-start(f32[128,2048]{1,0:T(8,128)S(1)} %fusion.18), channel_id=1, source_target_pairs={{0,64},{64,0},{128,192},{192,128},{1,65},{65,1},{129,193},{193,129... | collective-permute-start | bytes 3145736 | tf_op jit(solution)/shard_map/ppermute | solution.py:14
  41.0 28.2 %copy-start.12 = (f32[2048]{0:T(1024)S(1)}, f32[2048]{0:T(1024)}, u32[]{:S(2)}) copy-start(f32[2048]{0:T(1024)} %param.8) | copy-start | bytes 24580
  41.0 4.8 %collective-permute-start = (f32[128,2048]{1,0:T(8,128)S(1)}, f32[128,2048]{1,0:T(8,128)S(1)}, u32[]{:S(2)}, u32[]{:S(2)}) collective-permute-start(f32[128,2048]{1,0:T(8,128)S(1)} %fusion.21), channel_id=1, source_target_pairs={{0,64},{64,0},{128,192},{192,128},{1,65},{65,1},{129,193},{193,129... | collective-permute-start | bytes 3145736 | tf_op jit(solution)/shard_map/ppermute | solution.py:14
  43.2 26.0 %collective-permute-start.2 = (f32[128,2048]{1,0:T(8,128)S(1)}, f32[128,2048]{1,0:T(8,128)S(1)}, u32[]{:S(2)}, u32[]{:S(2)}) collective-permute-start(f32[128,2048]{1,0:T(8,128)S(1)} %convolution_add_fusion), channel_id=1, source_target_pairs={{0,128},{64,192},{128,0},{192,64},{1,129},{65,193},{129,1},{193,65... | collective-permute-start | bytes 3145736 | tf_op jit(solution)/shard_map/ppermute | solution.py:18
  69.9 6.4 %collective-permute-start.4 = (bf16[128,2048]{1,0:T(8,128)(2,1)S(1)}, bf16[128,2048]{1,0:T(8,128)(2,1)}, u32[]{:S(2)}, u32[]{:S(2)}) collective-permute-start(bf16[128,2048]{1,0:T(8,128)(2,1)S(1)} %fusion.6), channel_id=1, source_target_pairs={{0,64},{64,0},{128,192},{192,128},{1,65},{65,1},{129,193},{193,129... | collective-permute-start | bytes 1572872 | tf_op jit(solution)/shard_map/ppermute | solution.py:14
  71.2 15.1 %collective-permute-start.3 = (bf16[128,2048]{1,0:T(8,128)(2,1)S(1)}, bf16[128,2048]{1,0:T(8,128)(2,1)}, u32[]{:S(2)}, u32[]{:S(2)}) collective-permute-start(bf16[128,2048]{1,0:T(8,128)(2,1)S(1)} %fusion.6), channel_id=1, source_target_pairs={{0,128},{64,192},{128,0},{192,64},{1,129},{65,193},{129,1},{193,65... | collective-permute-start | bytes 1572872 | tf_op jit(solution)/shard_map/ppermute | solution.py:18
  86.3 6.9 %collective-permute-start.5 = (bf16[128,2048]{1,0:T(8,128)(2,1)}, bf16[128,2048]{1,0:T(8,128)(2,1)}, u32[]{:S(2)}, u32[]{:S(2)}) collective-permute-start(bf16[128,2048]{1,0:T(8,128)(2,1)} %collective-permute-done.3), channel_id=1, source_target_pairs={{0,64},{64,0},{128,192},{192,128},{1,65},{65,1},{129,193},{193,129... | collective-permute-start | bytes 1572872 | tf_op jit(solution)/shard_map/ppermute | solution.py:14
  93.2 30.5 %copy-start.11 = (bf16[1,8,576]{2,1,0:T(8,128)(2,1)S(1)}, bf16[1,8,576]{2,1,0:T(8,128)(2,1)}, u32[]{:S(2)}) copy-start(bf16[1,8,576]{2,1,0:T(8,128)(2,1)} %param.5) | copy-start | bytes 27652
  98.4 0.8 copy-start.2
  99.2 24.4 %all-to-all-start.1 = ((bf16[64,8,576]{2,1,0:T(8,128)(2,1)}), bf16[64,8,576]{2,1,0:T(8,128)(2,1)S(1)}, u32[]{:S(2)}, u32[]{:S(2)}) async-start(bf16[64,8,576]{2,1,0:T(8,128)(2,1)} %bitcast.68), calls=%async_computation.1 | async-start | bytes 1310720 | tf_op jit(solution)/shard_map/all_to_all | solution.py:90
  148.7 6.9 %collective-permute-start.6 = (bf16[256,2048]{1,0:T(8,128)(2,1)S(1)}, bf16[256,2048]{1,0:T(8,128)(2,1)S(1)}, u32[]{:S(2)}, u32[]{:S(2)}) collective-permute-start(bf16[256,2048]{1,0:T(8,128)(2,1)S(1)} %convolution_convert_fusion), channel_id=1, source_target_pairs={{0,64},{64,0},{128,192},{192,128},{1,65},{65,1},{129,193},{193,129... | collective-permute-start | bytes 3145736 | tf_op jit(solution)/shard_map/ppermute | solution.py:14
  156.6 26.0 %collective-permute-start.7 = (bf16[256,2048]{1,0:T(8,128)(2,1)S(1)}, bf16[256,2048]{1,0:T(8,128)(2,1)S(1)}, u32[]{:S(2)}, u32[]{:S(2)}) collective-permute-start(bf16[256,2048]{1,0:T(8,128)(2,1)S(1)} %get-tuple-element.12), channel_id=1, source_target_pairs={{0,128},{64,192},{128,0},{192,64},{1,129},{65,193},{129,1},{193,65... | collective-permute-start | bytes 3145736 | tf_op jit(solution)/shard_map/ppermute | solution.py:18
  184.5 5.6 %copy-start.4 = (bf16[128,576]{1,0:T(8,128)(2,1)S(1)}, bf16[128,576]{1,0:T(8,128)(2,1)}, u32[]{:S(2)}) copy-start(bf16[128,576]{1,0:T(8,128)(2,1)} %copy-done.3) | copy-start | bytes 442372
  184.5 5.6 %copy-start.6 = (bf16[128,576]{1,0:T(8,128)(2,1)S(1)}, bf16[128,576]{1,0:T(8,128)(2,1)}, u32[]{:S(2)}) copy-start(bf16[128,576]{1,0:T(8,128)(2,1)} %copy-done.5) | copy-start | bytes 442372
  184.6 5.5 %copy-start.8 = (bf16[128,576]{1,0:T(8,128)(2,1)S(1)}, bf16[128,576]{1,0:T(8,128)(2,1)}, u32[]{:S(2)}) copy-start(bf16[128,576]{1,0:T(8,128)(2,1)} %copy-done.7) | copy-start | bytes 442372
  184.6 5.5 %copy-start.10 = (bf16[128,576]{1,0:T(8,128)(2,1)S(1)}, bf16[128,576]{1,0:T(8,128)(2,1)}, u32[]{:S(2)}) copy-start(bf16[128,576]{1,0:T(8,128)(2,1)} %copy-done.9) | copy-start | bytes 442372
  184.6 5.5 %collective-permute-start.8 = (bf16[256,2048]{1,0:T(8,128)(2,1)S(1)}, bf16[256,2048]{1,0:T(8,128)(2,1)S(1)}, u32[]{:S(2)}, u32[]{:S(2)}) collective-permute-start(bf16[256,2048]{1,0:T(8,128)(2,1)S(1)} %fusion.26), channel_id=1, source_target_pairs={{0,64},{64,0},{128,192},{192,128},{1,65},{65,1},{129,193},{193,129... | collective-permute-start | bytes 3145736 | tf_op jit(solution)/shard_map/ppermute | solution.py:14

commit v2 on v1

--- a/solution.py
+++ b/solution.py
@@ -1,6 +1,10 @@
+import functools
+
 import jax
 import jax.numpy as jnp
 from jax import lax
+from jax.experimental import pallas as pl
+from jax.experimental.pallas import tpu as pltpu
 from jax.sharding import PartitionSpec as P
 
 LEARN_RATE = 4.0
@@ -41,6 +45,36 @@
     return lax.dot_general(left, right, (((0,), (0,)), ((), ())), preferred_element_type=F32)
 
 
+def decode_kernel(scale, starts_ref, *refs):
+    *active_refs, dec_ref, out_ref = refs
+    rows = active_refs[0].shape[0]
+    for index, active_ref in enumerate(active_refs):
+        term = lax.dot_general(
+            active_ref[...], dec_ref[...], (((1,), (1,)), ((), ())), preferred_element_type=F32
+        )
+        start = pl.multiple_of(starts_ref[index], rows)
+        out_ref[pl.ds(start, rows), :] = (scale * term).astype(out_ref.dtype)
+
+
+def decode(starts, actives, dec_by_width, scale):
+    rows, slab_width = actives[0].shape
+    model_width = dec_by_width.shape[0]
+    count = len(actives)
+    in_vmem = pl.BlockSpec(memory_space=pltpu.VMEM)
+    return pl.pallas_call(
+        functools.partial(decode_kernel, scale),
+        out_shape=jax.ShapeDtypeStruct((count * rows, model_width), BF16),
+        in_specs=[pl.BlockSpec(memory_space=pltpu.SMEM)] + [in_vmem] * (count + 1),
+        out_specs=in_vmem,
+        compiler_params=pltpu.CompilerParams(vmem_limit_bytes=24 * 1024 * 1024),
+        cost_estimate=pl.CostEstimate(
+            flops=2 * count * rows * slab_width * model_width,
+            bytes_accessed=2 * (count * rows + model_width) * slab_width,
+            transcendentals=0,
+        ),
+    )(jnp.stack(starts), *actives, dec_by_width)
+
+
 def body(layer_acts, enc_weight, dec_weight, enc_bias, dec_bias):
     tok_local = layer_acts[0]
     enc_local = enc_weight[0]
@@ -69,30 +103,33 @@
         return dot(rows_of(whole_tokens, start, quarter), enc_local)
 
     sum_of_chip = encode(of_chip) + to_core(encode(of_both))
-    arrived = to_chip(sum_of_chip)
+    leading = lax.reduce_precision(sum_of_chip, 8, 7)
+    remainder = (sum_of_chip - leading).astype(BF16)
+    arrived = to_chip(leading.astype(BF16)).astype(F32)
     sum_mine = encode(mine) + to_core(encode(of_core))
-    preact = enc_scale * (sum_mine + arrived) + bias
-    active_mine = jnp.maximum(preact, 0.0).astype(BF16)
+
+    def activate(preact):
+        return jnp.maximum(preact, 0.0).astype(BF16)
+
+    active_mine = activate(enc_scale * (sum_mine + arrived) + bias)
     active_of_chip = to_chip(active_mine)
     active_of_core = to_core(active_mine)
     active_of_both = to_core(active_of_chip)
+    remainder, active_of_both = lax.optimization_barrier((remainder, active_of_both))
 
-    pieces = (
-        (mine, active_mine),
-        (of_core, active_of_core),
-        (of_chip, active_of_chip),
-        (of_both, active_of_both),
-    )
-    recon_terms = jnp.zeros((tokens, model_width), BF16)
-    for start, active in pieces:
-        term = (dec_scale * dot(active, dec_local)).astype(BF16)
-        recon_terms = lax.dynamic_update_slice_in_dim(recon_terms, term, start, axis=0)
+    starts = (mine, of_core, of_chip, of_both)
+    actives = (active_mine, active_of_core, active_of_chip, active_of_both)
+    recon_terms = decode(starts, actives, dec_local.T, dec_scale)
+    arrived_later = to_chip(remainder).astype(F32)
+    exact_mine = activate(enc_scale * (sum_mine + (arrived + arrived_later)) + bias)
     arrived_terms = lax.all_to_all(
         recon_terms.reshape(blocks, tokens // blocks, model_width), "feat", 0, 0, tiled=True
     )
     recon = jnp.sum(arrived_terms.astype(F32), axis=0)
     error_b = (recon + dec_bias[0] - tok_local.astype(F32)).astype(BF16)
-    whole_errors = gather_tokens(error_b)
+    error_b, exact_mine = lax.optimization_barrier((error_b, exact_mine))
+    exact_of_chip = to_chip(exact_mine)
+    whole_errors, exact_of_chip = lax.optimization_barrier((gather_tokens(error_b), exact_of_chip))
 
     def enc_rows(starts):
         return jnp.concatenate([rows_of(whole_tokens, start, quarter) for start in starts])
@@ -105,19 +142,19 @@
     grad_from_core = to_core(grad_other).astype(F32)
     grad_pair = dot_transposed(errors_own, dec_local) + grad_from_core
     grad_pair_b = grad_pair.astype(BF16)
-    from_chip = to_chip(grad_pair_b).astype(F32)
+    from_chip = to_chip(grad_pair_b)
+    errors_all = jnp.concatenate([rows_of(whole_errors, start, quarter) for start in starts])
+    grad_dec = contract_rows(jnp.concatenate(actives), errors_all)
+    dec_step = (-LEARN_RATE * dec_scale * grad_dec).astype(BF16)[None]
+    from_chip, dec_step = lax.optimization_barrier((from_chip, dec_step))
+    from_chip = from_chip.astype(F32)
     from_chip = jnp.concatenate([from_chip[quarter:], from_chip[:quarter]])
     grad_act = dec_scale * (grad_pair + from_chip)
-    active_own = jnp.concatenate([active_mine, active_of_chip])
-    grad_pre_own = jnp.where(active_own > 0, grad_act, 0.0).astype(BF16)
+    exact_own = jnp.concatenate([exact_mine, exact_of_chip])
+    grad_pre_own = jnp.where(exact_own > 0, grad_act, 0.0).astype(BF16)
     grad_pre_other = to_core(grad_pre_own)
-
-    active_all = jnp.concatenate([active for _, active in pieces])
-    errors_all = jnp.concatenate([rows_of(whole_errors, start, quarter) for start, _ in pieces])
-    grad_dec = contract_rows(active_all, errors_all)
     grad_enc = contract_rows(enc_rows(own_rows + other_rows), jnp.concatenate([grad_pre_own, grad_pre_other]))
     enc_step = (-LEARN_RATE * enc_scale * grad_enc).astype(BF16)[None]
-    dec_step = (-LEARN_RATE * dec_scale * grad_dec).astype(BF16)[None]
     return (enc_step, dec_step)
 
 

time: 194 us -> 188 us (0.969)
  blocking collectives: 23.8 us -> 0 us
  waiting for transfers between devices: 92.7 us -> 110 us
  starting transfers between devices: 38.4 us -> 48.6 us
  local copies, waits for them, and re-layouts: 12.8 us -> 4.22 us
  matrix products: 21.7 us -> 13.7 us
  Pallas kernels: 0 us -> 4.69 us
  other arithmetic: 2.56 us -> 5.66 us
    ppermute x3 -> x5, waiting for transfers between devices: 52.7 us -> 84 us  [to_chip(): return lax.ppermute(value, 'layer', ACROSS_CHIPS)]
    all_to_all x1 -> x0, blocking collectives: 23.8 us -> none  [gather_tokens(): lax.all_to_all(copies, 'feat', 0, 0, tiled=True)]
    all_to_all x1, waiting for transfers between devices: 18.3 us -> 0.01 us  [body(): lax.all_to_all(recon_terms.reshape(blocks, tokens // blocks, model_width)...]
    all_to_all x1 -> x2, starting transfers between devices: 13.6 us -> 23.6 us  [gather_tokens(): lax.all_to_all(copies, 'feat', 0, 0, tiled=True)]
    dot_general x8 -> x4, matrix products: 12.7 us -> 4.32 us  [dot(): return jnp.dot(left, right, preferred_element_type=F32)]
    convert_element_type x4 -> x0, local copies, waits for them, and re-layouts: 5.95 us -> none  [body(): term = (dec_scale * dot(active, dec_local)).astype(BF16)]
    pallas_call x0 -> x1, Pallas kernels: none -> 4.69 us  [decode(): pl.pallas_call(functools.partial(decode_kernel, scale), out_shape=jax.Sha...]
    ppermute x6, waiting for transfers between devices: 3.84 us -> 8.37 us  [to_core(): return lax.ppermute(value, 'layer', ACROSS_CORES)]
  transfers between devices with their start and end apart: 11 -> 14, of which waited for: 7 -> 11; matrix products, arithmetic and copies ran while one was open for 10% -> 4% of each run, Pallas kernels for 0% -> 0%
where the time goes in v2:
time: 188 us
  waiting for transfers between devices  110 us (59%)
  starting transfers between devices  48.6 us (26%)
  matrix products  13.7 us (7%)
  other arithmetic  5.66 us (3%)
  Pallas kernels  4.69 us (2%)
  local copies, waits for them, and re-layouts  4.22 us (2%)
    ppermute x5, waiting for transfers between devices, to_chip(): return lax.ppermute(value, 'layer', ACROSS_CHIPS)  84 us
    all_to_all x2, starting transfers between devices, gather_tokens(): lax.all_to_all(copies, 'feat', 0, 0, tiled=True)  23.6 us
    all_to_all x2, waiting for transfers between devices, gather_tokens(): lax.all_to_all(copies, 'feat', 0, 0, tiled=True)  17.9 us
    ppermute x5, starting transfers between devices, to_chip(): return lax.ppermute(value, 'layer', ACROSS_CHIPS)  10.8 us
    ppermute x6, waiting for transfers between devices, to_core(): return lax.ppermute(value, 'layer', ACROSS_CORES)  8.37 us
    ppermute x6, starting transfers between devices, to_core(): return lax.ppermute(value, 'layer', ACROSS_CORES)  8.36 us
    all_to_all x1, starting transfers between devices, body(): lax.all_to_all(recon_terms.reshape(blocks, tokens // blocks, model_width)...  5.74 us
    dot_general x2, matrix products, contract_rows(): lax.dot_general(left, right, (((0,), (0,)), ((), ())), preferred_element_...  5.56 us
  transfers between devices with their start and end apart: 14, of which 11 were waited for; matrix products, arithmetic and copies ran while one was open for 4% of the time, Pallas kernels for 0%

profile of v2, /device:TPU:1, one launch (start us, length us, event | category | flops | bytes accessed | tf_op | source)
XLA Modules:
  0.0 188.0 jit_solution(4874633716254290729)
XLA Ops:
  0.6 1.7 broadcast_in_dim.25
  2.4 13.6 %all-to-all-start = ((bf16[64,8,576]{2,1,0:T(8,128)(2,1)}), bf16[64,8,576]{2,1,0:T(8,128)(2,1)S(1)}, u32[]{:S(2)}, u32[]{:S(2)}) async-start(bf16[64,8,576]{2,1,0:T(8,128)(2,1)} %broadcast_in_dim.25), calls=%async_computation | async-start | bytes 1310720 | tf_op jit(solution)/shard_map/all_to_all | solution.py:29
  16.0 17.9 %all-to-all-done = bf16[64,8,576]{2,1,0:T(8,128)(2,1)S(1)} async-done(((bf16[64,8,576]{2,1,0:T(8,128)(2,1)}), bf16[64,8,576]{2,1,0:T(8,128)(2,1)S(1)}, u32[]{:S(2)}, u32[]{:S(2)}) %all-to-all-start) | async-done | bytes 589856 | tf_op jit(solution)/shard_map/all_to_all | solution.py:29
  34.6 3.8 %collective-permute-start.1 = (f32[128,2048]{1,0:T(8,128)S(1)}, f32[128,2048]{1,0:T(8,128)S(1)}, u32[]{:S(2)}, u32[]{:S(2)}) collective-permute-start(f32[128,2048]{1,0:T(8,128)S(1)} %fusion.5), channel_id=1, source_target_pairs={{0,64},{64,0},{128,192},{192,128},{1,65},{65,1},{129,193},{193,129... | collective-permute-start | bytes 3145736 | tf_op jit(solution)/shard_map/ppermute | solution.py:18
  39.1 1.6 collective-permute-done.1
  40.7 1.5 fusion.34
  42.1 2.5 %collective-permute-start.2 = (bf16[128,2048]{1,0:T(8,128)(2,1)S(1)}, bf16[128,2048]{1,0:T(8,128)(2,1)S(1)}, u32[]{:S(2)}, u32[]{:S(2)}) collective-permute-start(bf16[128,2048]{1,0:T(8,128)(2,1)S(1)} %get-tuple-element.21), channel_id=1, source_target_pairs={{0,128},{64,192},{128,0},{192,64},{1,129},{65,193},{129,1},{193,65... | collective-permute-start | bytes 1572872 | tf_op jit(solution)/shard_map/ppermute | solution.py:22
  44.6 12.2 %collective-permute-done.2 = bf16[128,2048]{1,0:T(8,128)(2,1)S(1)} collective-permute-done((bf16[128,2048]{1,0:T(8,128)(2,1)S(1)}, bf16[128,2048]{1,0:T(8,128)(2,1)S(1)}, u32[]{:S(2)}, u32[]{:S(2)}) %collective-permute-start.2) | collective-permute-done | bytes 524320 | tf_op jit(solution)/shard_map/ppermute | solution.py:22
  56.8 1.7 fusion.28
  58.5 2.5 %collective-permute-start.4 = (bf16[128,2048]{1,0:T(8,128)(2,1)S(1)}, bf16[128,2048]{1,0:T(8,128)(2,1)S(1)}, u32[]{:S(2)}, u32[]{:S(2)}) collective-permute-start(bf16[128,2048]{1,0:T(8,128)(2,1)S(1)} %get-tuple-element.30.refs_0_), channel_id=1, source_target_pairs={{0,128},{64,192},{128,0},{192,64},{1,129},{65,193},{129,1},{193,65... | collective-permute-start | bytes 1572872 | tf_op jit(solution)/shard_map/ppermute | solution.py:22
  61.0 11.2 %collective-permute-done.4.refs_2_ = bf16[128,2048]{1,0:T(8,128)(2,1)S(1)} collective-permute-done((bf16[128,2048]{1,0:T(8,128)(2,1)S(1)}, bf16[128,2048]{1,0:T(8,128)(2,1)S(1)}, u32[]{:S(2)}, u32[]{:S(2)}) %collective-permute-start.4) | collective-permute-done | bytes 524320 | tf_op jit(solution)/shard_map/ppermute | solution.py:22
  72.2 2.1 %collective-permute-start.5 = (bf16[128,2048]{1,0:T(8,128)(2,1)S(1)}, bf16[128,2048]{1,0:T(8,128)(2,1)S(1)}, u32[]{:S(2)}, u32[]{:S(2)}) collective-permute-start(bf16[128,2048]{1,0:T(8,128)(2,1)S(1)} %collective-permute-done.4.refs_2_), channel_id=1, source_target_pairs={{0,64},{64,0},{128,192},{192,128},{1,65},{65,1},{129,193},{193,129... | collective-permute-start | bytes 1572872 | tf_op jit(solution)/shard_map/ppermute | solution.py:18
  74.4 1.5 collective-permute-done.5.refs_3_
  76.7 4.7 %shard_map.68 = bf16[512,576]{1,0:T(8,128)(2,1)} custom-call(s32[4]{0:T(128)S(1)} %pad_add_fusion.starts_ref, bf16[128,2048]{1,0:T(8,128)(2,1)S(1)} %get-tuple-element.30.refs_0_, bf16[128,2048]{1,0:T(8,128)(2,1)S(1)} %collective-permute-done.3.refs_1_, bf16[128,2048]{1,0:T(8,128)(2,1)S(1)} %collective-permute-done.4.refs_2_, ...), custom_call_target="tpu_custom_call" | custom-call | flops 1207959552 | bytes 4456448 | tf_op jit(solution)/shard_map/pallas_call | solution.py:64
  81.4 5.7 %all-to-all-start.1 = ((bf16[64,8,576]{2,1,0:T(8,128)(2,1)}), bf16[64,8,576]{2,1,0:T(8,128)(2,1)}, u32[]{:S(2)}, u32[]{:S(2)}) async-start(bf16[64,8,576]{2,1,0:T(8,128)(2,1)} %bitcast.9), calls=%async_computation.1 | async-start | bytes 1310720 | tf_op jit(solution)/shard_map/all_to_all | solution.py:125
  87.1 2.5 %collective-permute-start.6 = (bf16[128,2048]{1,0:T(8,128)(2,1)}, bf16[128,2048]{1,0:T(8,128)(2,1)}, u32[]{:S(2)}, u32[]{:S(2)}) collective-permute-start(bf16[128,2048]{1,0:T(8,128)(2,1)} %get-tuple-element.11), channel_id=1, source_target_pairs={{0,128},{64,192},{128,0},{192,64},{1,129},{65,193},{129,1},{193,65... | collective-permute-start | bytes 1572872 | tf_op jit(solution)/shard_map/ppermute | solution.py:22
  89.6 18.9 %collective-permute-done.6 = bf16[128,2048]{1,0:T(8,128)(2,1)} collective-permute-done((bf16[128,2048]{1,0:T(8,128)(2,1)}, bf16[128,2048]{1,0:T(8,128)(2,1)}, u32[]{:S(2)}, u32[]{:S(2)}) %collective-permute-start.6) | collective-permute-done | bytes 524320 | tf_op jit(solution)/shard_map/ppermute | solution.py:22
  108.5 2.6 %fusion.33 = bf16[128,2048]{1,0:T(8,128)(2,1)} fusion(f32[128,2048]{1,0:T(8,128)} %get-tuple-element.31, bf16[128,2048]{1,0:T(8,128)(2,1)} %copy-done.8, bf16[128,2048]{1,0:T(8,128)(2,1)} %collective-permute-done.6, f32[2048]{0:T(1024)S(1)} %copy-done.18), kind=kLoop, calls=%fused_computation.45 | loop fusion | flops 2097152 | bytes 2629632 | tf_op jit(solution)/shard_map/convert_element_type | solution.py:112
  111.1 1.2 convert_reduce_fusion
  113.2 10.1 %all-to-all-start.2 = ((bf16[64,8,576]{2,1,0:T(8,128)(2,1)}), bf16[64,8,576]{2,1,0:T(8,128)(2,1)}, u32[]{:S(2)}, u32[]{:S(2)}) async-start(bf16[64,8,576]{2,1,0:T(8,128)(2,1)} %broadcast_in_dim.26), calls=%async_computation.2 | async-start | bytes 1310720 | tf_op jit(solution)/shard_map/all_to_all | solution.py:29
  123.3 2.1 %collective-permute-start.7 = (bf16[128,2048]{1,0:T(8,128)(2,1)}, bf16[128,2048]{1,0:T(8,128)(2,1)}, u32[]{:S(2)}, u32[]{:S(2)}) collective-permute-start(bf16[128,2048]{1,0:T(8,128)(2,1)} %fusion.33), channel_id=1, source_target_pairs={{0,128},{64,192},{128,0},{192,64},{1,129},{65,193},{129,1},{193,65... | collective-permute-start | bytes 1572872 | tf_op jit(solution)/shard_map/ppermute | solution.py:22
  125.4 19.8 %collective-permute-done.7 = bf16[128,2048]{1,0:T(8,128)(2,1)} collective-permute-done((bf16[128,2048]{1,0:T(8,128)(2,1)}, bf16[128,2048]{1,0:T(8,128)(2,1)}, u32[]{:S(2)}, u32[]{:S(2)}) %collective-permute-start.7) | collective-permute-done | bytes 524320 | tf_op jit(solution)/shard_map/ppermute | solution.py:22
  145.1 1.2 constant_dynamic-slice_fusion.1
  146.4 2.8 %convolution_convert_fusion = bf16[256,2048]{1,0:T(8,128)(2,1)S(1)} fusion(bf16[1,2048,576]{1,2,0:T(8,128)(2,1)} %param.7, bf16[128,576]{1,0:T(8,128)(2,1)S(1)} %get-tuple-element.23, bf16[128,576]{1,0:T(8,128)(2,1)S(1)} %get-tuple-element.22), kind=kOutput, calls=%fused_computation.4 | convolution fusion | flops 605093888 | bytes 3702784 | tf_op jit(solution)/shard_map/dot_general | solution.py:41
  150.2 2.3 %collective-permute-done.8 = bf16[256,2048]{1,0:T(8,128)(2,1)S(1)} collective-permute-done((bf16[256,2048]{1,0:T(8,128)(2,1)S(1)}, bf16[256,2048]{1,0:T(8,128)(2,1)S(1)}, u32[]{:S(2)}, u32[]{:S(2)}) %collective-permute-start.8) | collective-permute-done | bytes 1048608 | tf_op jit(solution)/shard_map/ppermute | solution.py:18
  153.5 1.3 collective-permute-start.9
  154.8 2.7 %fusion = bf16[1,2048,576]{1,2,0:T(8,128)(2,1)} fusion(bf16[128,2048]{1,0:T(8,128)(2,1)S(1)} %copy-done.4, bf16[128,2048]{1,0:T(8,128)(2,1)S(1)} %collective-permute-done.4.refs_2_, bf16[128,2048]{1,0:T(8,128)(2,1)S(1)} %copy-done.6, bf16[128,2048]{1,0:T(8,128)(2,1)S(1)} %get-tuple-element.30.refs_0_, bf16[128,576]{1,0:T(8,128)(2,1)S(1)} %get-tuple-element.23, ...), kind=kOutput, calls=%fused_computation.2 | convolution fusion | flops 1221066752 | bytes 5046272 | tf_op jit(solution)/shard_map/dot_general | solution.py:45
  157.5 21.9 %collective-permute-done.9 = bf16[256,2048]{1,0:T(8,128)(2,1)S(1)} collective-permute-done((bf16[256,2048]{1,0:T(8,128)(2,1)S(1)}, bf16[256,2048]{1,0:T(8,128)(2,1)S(1)}, u32[]{:S(2)}, u32[]{:S(2)}) %collective-permute-start.9) | collective-permute-done | bytes 1048608 | tf_op jit(solution)/shard_map/ppermute | solution.py:22
  179.8 1.8 fusion.20
  181.5 1.3 collective-permute-start.10
  182.8 2.3 %collective-permute-done.10 = bf16[256,2048]{1,0:T(8,128)(2,1)S(1)} collective-permute-done((bf16[256,2048]{1,0:T(8,128)(2,1)S(1)}, bf16[256,2048]{1,0:T(8,128)(2,1)S(1)}, u32[]{:S(2)}, u32[]{:S(2)}) %collective-permute-start.10) | collective-permute-done | bytes 1048608 | tf_op jit(solution)/shard_map/ppermute | solution.py:18
  185.1 2.8 %fusion.1 = bf16[1,576,2048]{2,1,0:T(8,128)(2,1)} fusion(bf16[256,2048]{1,0:T(8,128)(2,1)S(1)} %collective-permute-done.10, bf16[256,2048]{1,0:T(8,128)(2,1)S(1)} %fusion.20, bf16[128,576]{1,0:T(8,128)(2,1)S(1)} %copy-done.10, bf16[128,576]{1,0:T(8,128)(2,1)S(1)} %copy-done.12, bf16[128,576]{1,0:T(8,128)(2,1)S(1)} %copy-done.14, ...), kind=kOutput, calls=%fused_computation.3 | convolution fusion | flops 1216872448 | bytes 5046272 | tf_op jit(solution)/shard_map/dot_general | solution.py:45
  (56 shorter events, 5.4 us)
Async XLA Ops:
  0.6 33.4 %copy-start = (bf16[1,576,2048]{2,1,0:T(8,128)(2,1)S(1)}, bf16[1,576,2048]{2,1,0:T(8,128)(2,1)}, u32[]{:S(2)}) copy-start(bf16[1,576,2048]{2,1,0:T(8,128)(2,1)} %param.6) | copy-start | bytes 7077892
  2.4 31.5 %all-to-all-start = ((bf16[64,8,576]{2,1,0:T(8,128)(2,1)}), bf16[64,8,576]{2,1,0:T(8,128)(2,1)S(1)}, u32[]{:S(2)}, u32[]{:S(2)}) async-start(bf16[64,8,576]{2,1,0:T(8,128)(2,1)} %broadcast_in_dim.25), calls=%async_computation | async-start | bytes 1310720 | tf_op jit(solution)/shard_map/all_to_all | solution.py:29
  34.0 5.0 %copy-start.9 = (bf16[128,576]{1,0:T(8,128)(2,1)}, bf16[128,576]{1,0:T(8,128)(2,1)S(1)}, u32[]{:S(2)}) copy-start(bf16[128,576]{1,0:T(8,128)(2,1)S(1)} %get-tuple-element.27) | copy-start | bytes 442372
  34.0 5.0 %copy-start.11 = (bf16[128,576]{1,0:T(8,128)(2,1)}, bf16[128,576]{1,0:T(8,128)(2,1)S(1)}, u32[]{:S(2)}) copy-start(bf16[128,576]{1,0:T(8,128)(2,1)S(1)} %get-tuple-element.28) | copy-start | bytes 442372
  34.0 6.7 %copy-start.13 = (bf16[128,576]{1,0:T(8,128)(2,1)}, bf16[128,576]{1,0:T(8,128)(2,1)S(1)}, u32[]{:S(2)}) copy-start(bf16[128,576]{1,0:T(8,128)(2,1)S(1)} %get-tuple-element.26) | copy-start | bytes 442372
  34.0 22.8 %copy-start.15 = (bf16[128,576]{1,0:T(8,128)(2,1)}, bf16[128,576]{1,0:T(8,128)(2,1)S(1)}, u32[]{:S(2)}) copy-start(bf16[128,576]{1,0:T(8,128)(2,1)S(1)} %get-tuple-element.29) | copy-start | bytes 442372
  34.6 6.1 %collective-permute-start.1 = (f32[128,2048]{1,0:T(8,128)S(1)}, f32[128,2048]{1,0:T(8,128)S(1)}, u32[]{:S(2)}, u32[]{:S(2)}) collective-permute-start(f32[128,2048]{1,0:T(8,128)S(1)} %fusion.5), channel_id=1, source_target_pairs={{0,64},{64,0},{128,192},{192,128},{1,65},{65,1},{129,193},{193,129... | collective-permute-start | bytes 3145736 | tf_op jit(solution)/shard_map/ppermute | solution.py:18
  39.0 5.6 %collective-permute-start = (f32[128,2048]{1,0:T(8,128)S(1)}, f32[128,2048]{1,0:T(8,128)S(1)}, u32[]{:S(2)}, u32[]{:S(2)}) collective-permute-start(f32[128,2048]{1,0:T(8,128)S(1)} %fusion.8), channel_id=1, source_target_pairs={{0,64},{64,0},{128,192},{192,128},{1,65},{65,1},{129,193},{193,129... | collective-permute-start | bytes 3145736 | tf_op jit(solution)/shard_map/ppermute | solution.py:18
  40.7 16.1 %copy-start.18 = (f32[2048]{0:T(1024)S(1)}, f32[2048]{0:T(1024)}, u32[]{:S(2)}) copy-start(f32[2048]{0:T(1024)} %param.8) | copy-start | bytes 24580
  42.1 14.6 %collective-permute-start.2 = (bf16[128,2048]{1,0:T(8,128)(2,1)S(1)}, bf16[128,2048]{1,0:T(8,128)(2,1)S(1)}, u32[]{:S(2)}, u32[]{:S(2)}) collective-permute-start(bf16[128,2048]{1,0:T(8,128)(2,1)S(1)} %get-tuple-element.21), channel_id=1, source_target_pairs={{0,128},{64,192},{128,0},{192,64},{1,129},{65,193},{129,1},{193,65... | collective-permute-start | bytes 1572872 | tf_op jit(solution)/shard_map/ppermute | solution.py:22
  56.8 19.9 %copy-start.1 = (bf16[1,2048,576]{1,2,0:T(8,128)(2,1)S(1)}, bf16[1,2048,576]{1,2,0:T(8,128)(2,1)}, u32[]{:S(2)}) copy-start(bf16[1,2048,576]{1,2,0:T(8,128)(2,1)} %param.7) | copy-start | bytes 7077892
  58.5 13.7 %collective-permute-start.4 = (bf16[128,2048]{1,0:T(8,128)(2,1)S(1)}, bf16[128,2048]{1,0:T(8,128)(2,1)S(1)}, u32[]{:S(2)}, u32[]{:S(2)}) collective-permute-start(bf16[128,2048]{1,0:T(8,128)(2,1)S(1)} %get-tuple-element.30.refs_0_), channel_id=1, source_target_pairs={{0,128},{64,192},{128,0},{192,64},{1,129},{65,193},{129,1},{193,65... | collective-permute-start | bytes 1572872 | tf_op jit(solution)/shard_map/ppermute | solution.py:22
  72.2 3.7 %collective-permute-start.5 = (bf16[128,2048]{1,0:T(8,128)(2,1)S(1)}, bf16[128,2048]{1,0:T(8,128)(2,1)S(1)}, u32[]{:S(2)}, u32[]{:S(2)}) collective-permute-start(bf16[128,2048]{1,0:T(8,128)(2,1)S(1)} %collective-permute-done.4.refs_2_), channel_id=1, source_target_pairs={{0,64},{64,0},{128,192},{192,128},{1,65},{65,1},{129,193},{193,129... | collective-permute-start | bytes 1572872 | tf_op jit(solution)/shard_map/ppermute | solution.py:18
  74.4 2.3 %collective-permute-start.3 = (bf16[128,2048]{1,0:T(8,128)(2,1)S(1)}, bf16[128,2048]{1,0:T(8,128)(2,1)S(1)}, u32[]{:S(2)}, u32[]{:S(2)}) collective-permute-start(bf16[128,2048]{1,0:T(8,128)(2,1)S(1)} %get-tuple-element.30.refs_0_), channel_id=1, source_target_pairs={{0,64},{64,0},{128,192},{192,128},{1,65},{65,1},{129,193},{193,129... | collective-permute-start | bytes 1572872 | tf_op jit(solution)/shard_map/ppermute | solution.py:18
  75.9 5.5 %copy-start.3 = (bf16[128,2048]{1,0:T(8,128)(2,1)}, bf16[128,2048]{1,0:T(8,128)(2,1)S(1)}, u32[]{:S(2)}) copy-start(bf16[128,2048]{1,0:T(8,128)(2,1)S(1)} %collective-permute-done.5.refs_3_) | copy-start | bytes 1572868
  76.6 4.7 %copy-start.5 = (bf16[128,2048]{1,0:T(8,128)(2,1)}, bf16[128,2048]{1,0:T(8,128)(2,1)S(1)}, u32[]{:S(2)}) copy-start(bf16[128,2048]{1,0:T(8,128)(2,1)S(1)} %collective-permute-done.3.refs_1_) | copy-start | bytes 1572868
  76.6 13.0 %copy-start.19 = (f32[1,576]{1,0:T(1,128)S(1)}, f32[1,576]{1,0:T(1,128)}, u32[]{:S(2)}) copy-start(f32[1,576]{1,0:T(1,128)} %param.9) | copy-start | bytes 6916
  81.3 31.0 %copy-start.17 = (bf16[1,8,576]{2,1,0:T(8,128)(2,1)S(1)}, bf16[1,8,576]{2,1,0:T(8,128)(2,1)}, u32[]{:S(2)}) copy-start(bf16[1,8,576]{2,1,0:T(8,128)(2,1)} %param.5) | copy-start | bytes 27652
  81.4 29.8 %all-to-all-start.1 = ((bf16[64,8,576]{2,1,0:T(8,128)(2,1)}), bf16[64,8,576]{2,1,0:T(8,128)(2,1)}, u32[]{:S(2)}, u32[]{:S(2)}) async-start(bf16[64,8,576]{2,1,0:T(8,128)(2,1)} %bitcast.9), calls=%async_computation.1 | async-start | bytes 1310720 | tf_op jit(solution)/shard_map/all_to_all | solution.py:125
  87.1 21.4 %collective-permute-start.6 = (bf16[128,2048]{1,0:T(8,128)(2,1)}, bf16[128,2048]{1,0:T(8,128)(2,1)}, u32[]{:S(2)}, u32[]{:S(2)}) collective-permute-start(bf16[128,2048]{1,0:T(8,128)(2,1)} %get-tuple-element.11), channel_id=1, source_target_pairs={{0,128},{64,192},{128,0},{192,64},{1,129},{65,193},{129,1},{193,65... | collective-permute-start | bytes 1572872 | tf_op jit(solution)/shard_map/ppermute | solution.py:22
  113.2 31.9 %all-to-all-start.2 = ((bf16[64,8,576]{2,1,0:T(8,128)(2,1)}), bf16[64,8,576]{2,1,0:T(8,128)(2,1)}, u32[]{:S(2)}, u32[]{:S(2)}) async-start(bf16[64,8,576]{2,1,0:T(8,128)(2,1)} %broadcast_in_dim.26), calls=%async_computation.2 | async-start | bytes 1310720 | tf_op jit(solution)/shard_map/all_to_all | solution.py:29
  123.3 21.8 %collective-permute-start.7 = (bf16[128,2048]{1,0:T(8,128)(2,1)}, bf16[128,2048]{1,0:T(8,128)(2,1)}, u32[]{:S(2)}, u32[]{:S(2)}) collective-permute-start(bf16[128,2048]{1,0:T(8,128)(2,1)} %fusion.33), channel_id=1, source_target_pairs={{0,128},{64,192},{128,0},{192,64},{1,129},{65,193},{129,1},{193,65... | collective-permute-start | bytes 1572872 | tf_op jit(solution)/shard_map/ppermute | solution.py:22
  146.3 6.2 %copy-start.2 = (bf16[1,2048,576]{1,2,0:T(8,128)(2,1)S(1)}, bf16[1,2048,576]{1,2,0:T(8,128)(2,1)}, u32[]{:S(2)}) copy-start(bf16[1,2048,576]{1,2,0:T(8,128)(2,1)} %param.7) | copy-start | bytes 7077892
  149.2 3.3 %collective-permute-start.8 = (bf16[256,2048]{1,0:T(8,128)(2,1)S(1)}, bf16[256,2048]{1,0:T(8,128)(2,1)S(1)}, u32[]{:S(2)}, u32[]{:S(2)}) collective-permute-start(bf16[256,2048]{1,0:T(8,128)(2,1)S(1)} %convolution_convert_fusion), channel_id=1, source_target_pairs={{0,64},{64,0},{128,192},{192,128},{1,65},{65,1},{129,193},{193,129... | collective-permute-start | bytes 3145736 | tf_op jit(solution)/shard_map/ppermute | solution.py:18
  152.5 2.3 %copy-start.6 = (bf16[128,2048]{1,0:T(8,128)(2,1)S(1)}, bf16[128,2048]{1,0:T(8,128)(2,1)}, u32[]{:S(2)}) copy-start(bf16[128,2048]{1,0:T(8,128)(2,1)} %copy-done.5) | copy-start | bytes 1572868
  153.5 26.0 %collective-permute-start.9 = (bf16[256,2048]{1,0:T(8,128)(2,1)S(1)}, bf16[256,2048]{1,0:T(8,128)(2,1)S(1)}, u32[]{:S(2)}, u32[]{:S(2)}) collective-permute-start(bf16[256,2048]{1,0:T(8,128)(2,1)S(1)} %get-tuple-element.32), channel_id=1, source_target_pairs={{0,128},{64,192},{128,0},{192,64},{1,129},{65,193},{129,1},{193,65... | collective-permute-start | bytes 3145736 | tf_op jit(solution)/shard_map/ppermute | solution.py:22
  157.5 22.2 %copy-start.7 = (bf16[128,2048]{1,0:T(8,128)(2,1)S(1)}, bf16[128,2048]{1,0:T(8,128)(2,1)}, u32[]{:S(2)}) copy-start(bf16[128,2048]{1,0:T(8,128)(2,1)} %fusion.33) | copy-start | bytes 1572868
  179.7 5.4 %copy-start.10 = (bf16[128,576]{1,0:T(8,128)(2,1)S(1)}, bf16[128,576]{1,0:T(8,128)(2,1)}, u32[]{:S(2)}) copy-start(bf16[128,576]{1,0:T(8,128)(2,1)} %copy-done.9) | copy-start | bytes 442372
  179.7 5.4 %copy-start.12 = (bf16[128,576]{1,0:T(8,128)(2,1)S(1)}, bf16[128,576]{1,0:T(8,128)(2,1)}, u32[]{:S(2)}) copy-start(bf16[128,576]{1,0:T(8,128)(2,1)} %copy-done.11) | copy-start | bytes 442372
  179.7 5.4 %copy-start.14 = (bf16[128,576]{1,0:T(8,128)(2,1)S(1)}, bf16[128,576]{1,0:T(8,128)(2,1)}, u32[]{:S(2)}) copy-start(bf16[128,576]{1,0:T(8,128)(2,1)} %copy-done.13) | copy-start | bytes 442372
  179.8 5.4 %copy-start.16 = (bf16[128,576]{1,0:T(8,128)(2,1)S(1)}, bf16[128,576]{1,0:T(8,128)(2,1)}, u32[]{:S(2)}) copy-start(bf16[128,576]{1,0:T(8,128)(2,1)} %copy-done.15) | copy-start | bytes 442372
  181.5 3.6 %collective-permute-start.10 = (bf16[256,2048]{1,0:T(8,128)(2,1)S(1)}, bf16[256,2048]{1,0:T(8,128)(2,1)S(1)}, u32[]{:S(2)}, u32[]{:S(2)}) collective-permute-start(bf16[256,2048]{1,0:T(8,128)(2,1)S(1)} %fusion.20), channel_id=1, source_target_pairs={{0,64},{64,0},{128,192},{192,128},{1,65},{65,1},{129,193},{193,129... | collective-permute-start | bytes 3145736 | tf_op jit(solution)/shard_map/ppermute | solution.py:18
  (2 other events, 4.0 us)

commit v3 on v1

v3 whole, which is shorter than its diff:
```python
import functools

import jax
import jax.numpy as jnp
from jax import lax
from jax.experimental import pallas as pl
from jax.experimental.pallas import tpu as pltpu
from jax.sharding import PartitionSpec as P

LEARN_RATE = 4.0
BF16 = jnp.bfloat16
F32 = jnp.float32
PARTS = 2
STEP_BLOCKS = 1
ACROSS_CORES = [(0, 1), (1, 0), (2, 3), (3, 2)]
ACROSS_CHIPS = [(0, 2), (1, 3), (2, 0), (3, 1)]


def to_core(value):
    return lax.ppermute(value, "layer", ACROSS_CORES)


def to_chip(value):
    return lax.ppermute(value, "layer", ACROSS_CHIPS)


def gather_tokens(value):
    blocks = lax.axis_size("feat")
    rows, width = value.shape
    copies = jnp.broadcast_to(value[None], (blocks, rows, width))
    return lax.all_to_all(copies, "feat", 0, 0, tiled=True).reshape(blocks * rows, width)


def rows_of(value, start, count):
    return lax.dynamic_slice_in_dim(value, start, count, axis=0)


def dot(left, right):
    return jnp.dot(left, right, preferred_element_type=F32)


def dot_transposed(left, right):
    return lax.dot_general(left, right, (((1,), (1,)), ((), ())), preferred_element_type=F32)


def contract_rows(left, right):
    return lax.dot_general(left, right, (((0,), (0,)), ((), ())), preferred_element_type=F32)


VMEM = pl.BlockSpec(memory_space=pltpu.VMEM)
SMEM = pl.BlockSpec(memory_space=pltpu.SMEM)


def local_call(kernel, out_shape, operands, flops):
    moved = sum(operand.size * operand.dtype.itemsize for operand in operands)
    return pl.pallas_call(
        kernel,
        out_shape=out_shape,
        in_specs=[SMEM] + [VMEM] * (len(operands) - 1),
        out_specs=jax.tree.map(lambda _: VMEM, out_shape),
        compiler_params=pltpu.CompilerParams(vmem_limit_bytes=24 * 1024 * 1024),
        cost_estimate=pl.CostEstimate(flops=flops, bytes_accessed=moved, transcendentals=0),
    )(*operands)


def decode_kernel(places, part_count, has_before, scale, starts_ref, *refs):
    piece_refs = refs[: len(places)]
    dec_refs = refs[len(places) : len(places) + part_count]
    before_ref = refs[-2] if has_before else None
    out_ref = refs[-1]
    rows = piece_refs[0].shape[0]
    for row in range(out_ref.shape[0] // rows):
        where = pl.ds(pl.multiple_of(starts_ref[row], rows), rows)
        total = before_ref[where, :] if has_before else None
        for (row_of_piece, part), piece_ref in zip(places, piece_refs):
            if row_of_piece == row:
                term = dot_transposed(piece_ref[...], dec_refs[part][...])
                total = term if total is None else total + term
        out_ref[where, :] = (scale * total).astype(out_ref.dtype)


def decode(starts, pieces, dec_parts, before, scale, dtype):
    places, arrays = list(pieces), list(pieces.values())
    rows, part_width = arrays[0].shape
    model_width = dec_parts[0].shape[0]
    operands = [starts, *arrays, *dec_parts] + ([] if before is None else [before])
    kernel = functools.partial(decode_kernel, places, len(dec_parts), before is not None, scale)
    out_shape = jax.ShapeDtypeStruct((starts.shape[0] * rows, model_width), dtype)
    return local_call(kernel, out_shape, operands, 2 * len(places) * rows * part_width * model_width)


def back_kernel(row, rows, part_count, has_terms, starts_ref, errors_ref, *refs):
    dec_refs, refs = refs[:part_count], refs[part_count:]
    term_refs, out_refs = (refs[:part_count], refs[part_count:]) if has_terms else (None, refs)
    errors = errors_ref[pl.ds(pl.multiple_of(starts_ref[row], rows), rows), :]
    for part in range(part_count):
        total = dot(errors, dec_refs[part][...])
        if has_terms:
            total += term_refs[part][...].astype(F32)
        out_refs[part][...] = total.astype(out_refs[part].dtype)


def back(starts, row, errors, dec_parts, terms, dtype):
    rows = errors.shape[0] // starts.shape[0]
    model_width, part_width = dec_parts[0].shape
    operands = [starts, errors, *dec_parts] + ([] if terms is None else terms)
    kernel = functools.partial(back_kernel, row, rows, len(dec_parts), terms is not None)
    out_shape = [jax.ShapeDtypeStruct((rows, part_width), dtype)] * len(dec_parts)
    return local_call(kernel, out_shape, operands, 2 * rows * part_width * model_width * len(dec_parts))


def step_kernel(scale, left_ref, *refs):
    *piece_refs, _, out_ref = refs
    rows = jnp.concatenate([piece_ref[...] for piece_ref in piece_refs], axis=0)
    out_ref[...] = (scale * contract_rows(left_ref[...], rows)).astype(out_ref.dtype)


def first_step_kernel(scale, *refs):
    step_kernel(scale, *refs[:-1], None, refs[-1])


def write_step(left, pieces, before, part_index, scale):
    rows, part_width = pieces[0].shape
    tokens, model_width = left.shape
    block = part_width // STEP_BLOCKS
    operands = [left, *pieces]
    in_specs = [pl.BlockSpec((tokens, model_width), lambda index: (0, 0))]
    in_specs += [pl.BlockSpec((rows, block), lambda index: (0, index))] * len(pieces)
    kernel, aliases = first_step_kernel, {}
    if before is not None:
        aliases = {len(operands): 0}
        operands.append(before)
        in_specs.append(pl.BlockSpec(memory_space=pl.ANY))
        kernel = step_kernel
    first_block = part_index * STEP_BLOCKS
    return pl.pallas_call(
        functools.partial(kernel, scale),
        grid=(STEP_BLOCKS,),
        out_shape=jax.ShapeDtypeStruct((model_width, part_width * PARTS), BF16),
        in_specs=in_specs,
        out_specs=pl.BlockSpec((model_width, block), lambda index: (0, first_block + index)),
        input_output_aliases=aliases,
        compiler_params=pltpu.CompilerParams(vmem_limit_bytes=16 * 1024 * 1024),
        cost_estimate=pl.CostEstimate(
            flops=2 * tokens * part_width * model_width,
            bytes_accessed=2 * (tokens + model_width) * part_width,
            transcendentals=0,
        ),
    )(*operands)


def body(layer_acts, enc_weight, dec_weight, enc_bias, dec_bias):
    tok_local = layer_acts[0]
    enc_local = enc_weight[0]
    dec_local = dec_weight[0]
    bias = enc_bias[None, :]
    model_width, slab_width = enc_local.shape
    blocks = lax.axis_size("feat")
    enc_scale = (layer_acts.shape[0] * lax.axis_size("layer") * model_width) ** (-0.5)
    dec_scale = (slab_width * blocks) ** (-0.5)
    tokens = tok_local.shape[0] * blocks
    half, quarter = tokens // 2, tokens // 4
    place = lax.axis_index("layer")
    chip, core = place // 2, place % 2

    def quarter_at(core_index, chip_index):
        return core_index * half + chip_index * quarter

    mine = quarter_at(core, chip)
    of_chip = quarter_at(core, 1 - chip)
    of_core = quarter_at(1 - core, chip)
    of_both = quarter_at(1 - core, 1 - chip)
    starts = (mine, of_core, of_chip, of_both)
    starts_array = jnp.stack(starts)

    whole_tokens = gather_tokens(tok_local)
    token_rows = [rows_of(whole_tokens, start, quarter) for start in starts]
    tok_mine, tok_of_core, tok_of_chip, tok_of_both = token_rows

    def activate(sums, part):
        return jnp.maximum(enc_scale * sums + bias[:, part], 0.0).astype(BF16)

    part_width = slab_width // PARTS
    parts = [slice(index * part_width, (index + 1) * part_width) for index in range(PARTS)]
    remainders, sums_mine, arrived, actives = [], [], [], []
    for part in parts:
        enc_part = enc_local[:, part]
        sum_of_chip = dot(tok_of_chip, enc_part) + to_core(dot(tok_of_both, enc_part))
        leading = lax.reduce_precision(sum_of_chip, 8, 7)
        remainders.append((sum_of_chip - leading).astype(BF16))
        arrived.append(to_chip(leading.astype(BF16)))
        sums_mine.append(dot(tok_mine, enc_part) + to_core(dot(tok_of_core, enc_part)))
    dec_parts = [dec_local.T[:, part] for part in parts]
    active = {}
    for index, part in enumerate(parts):
        active[0, index] = activate(sums_mine[index] + arrived[index].astype(F32), part)
        active[1, index] = to_core(active[0, index])
        active[2, index] = to_chip(active[0, index])
    last = PARTS - 1
    for index in range(last):
        active[3, index] = to_core(active[2, index])
    early = {place: value for place, value in active.items() if place != (2, last)}
    recon_early = decode(starts_array, early, dec_parts, None, 1.0, F32)
    active[2, last], recon_early = lax.optimization_barrier((active[2, last], recon_early))
    active[3, last] = to_core(active[2, last])
    late = {(2, last): active[2, last], (3, last): active[3, last]}
    recon_terms = decode(starts_array, late, dec_parts, recon_early, dec_scale, BF16)
    remainders, recon_terms = lax.optimization_barrier((remainders, recon_terms))
    arrived_later = [to_chip(remainder) for remainder in remainders]
    arrived_terms = lax.all_to_all(
        recon_terms.reshape(blocks, tokens // blocks, model_width), "feat", 0, 0, tiled=True
    )
    recon = jnp.sum(arrived_terms.astype(F32), axis=0)
    error_b = (recon + dec_bias[0] - tok_local.astype(F32)).astype(BF16)
    error_b, arrived_later[0] = lax.optimization_barrier((error_b, arrived_later[0]))
    whole_errors, arrived_later = lax.optimization_barrier((gather_tokens(error_b), arrived_later))
    of_both_b = back(starts_array, 3, whole_errors, dec_parts, None, BF16)
    whole_errors, of_both_b = lax.optimization_barrier((whole_errors, of_both_b))
    of_core_b = back(starts_array, 1, whole_errors, dec_parts, None, BF16)
    pair_b = back(starts_array, 2, whole_errors, dec_parts, [to_core(term) for term in of_both_b], BF16)
    whole_errors, pair_b = lax.optimization_barrier((whole_errors, pair_b))
    grads_arrived = [to_chip(term) for term in pair_b]
    grads_mine = back(starts_array, 0, whole_errors, dec_parts, [to_core(term) for term in of_core_b], F32)

    whole_errors, arrived_later, grads_mine = lax.optimization_barrier((whole_errors, arrived_later, grads_mine))
    alive = []
    for index, part in enumerate(parts):
        terms = arrived[index].astype(F32) + arrived_later[index].astype(F32)
        exact = enc_scale * (sums_mine[index] + terms) + bias[:, part]
        alive.append((exact > 0.0).astype(F32))
    errors = jnp.concatenate([rows_of(whole_errors, start, quarter) for start in starts])
    dec_step = enc_step = None
    for index in range(PARTS):
        pieces = [active[row, index] for row in range(4)]
        dec_step = write_step(errors, pieces, dec_step, index, -LEARN_RATE * dec_scale)
    grads_arrived[0], dec_step, alive = lax.optimization_barrier((grads_arrived[0], dec_step, alive))

    pres = []
    for index in range(PARTS):
        grad_arrived = grads_arrived[index]
        if index:
            grad_arrived, pres[-1][1] = lax.optimization_barrier((grad_arrived, pres[-1][1]))
        grad_act = dec_scale * (grads_mine[index] + grad_arrived.astype(F32))
        pre_mine = jnp.where(alive[index] > 0.0, grad_act, 0.0).astype(BF16)
        pres.append([pre_mine, to_core(pre_mine), to_chip(pre_mine)])
        if index:
            pres[0][2], pres[1][2] = lax.optimization_barrier((pres[0][2], pres[1][2]))
    all_tokens = jnp.concatenate(token_rows)
    for index in range(PARTS):
        pre_mine, pre_of_core, pre_of_chip = pres[index]
        pieces = [pre_mine, pre_of_core, pre_of_chip, to_core(pre_of_chip)]
        enc_step = write_step(all_tokens, pieces, enc_step, index, -LEARN_RATE * enc_scale)
    return (enc_step[None], dec_step.T[None])


def solution(mesh):
    in_specs = (
        P("layer", "feat", None),
        P("layer", None, "feat"),
        P("layer", "feat", None),
        P("feat"),
        P("layer", None),
    )
    out_specs = (P("layer", None, "feat"), P("layer", "feat", None))
    return jax.shard_map(body, mesh=mesh, in_specs=in_specs, out_specs=out_specs, check_vma=False)
```

time: 194 us -> 165 us (0.85)
  starting transfers between devices: 38.4 us -> 65.8 us
  waiting for transfers between devices: 92.7 us -> 66.8 us
  blocking collectives: 23.8 us -> 0 us
  Pallas kernels: 0 us -> 17.2 us
  matrix products: 21.7 us -> 6.06 us
  local copies, waits for them, and re-layouts: 12.8 us -> 3.88 us
    ppermute x3 -> x10, waiting for transfers between devices: 52.7 us -> 26.7 us  [to_chip(): return lax.ppermute(value, 'layer', ACROSS_CHIPS)]
    all_to_all x1 -> x0, blocking collectives: 23.8 us -> none  [gather_tokens(): lax.all_to_all(copies, 'feat', 0, 0, tiled=True)]
    pallas_call x0 -> x10, Pallas kernels: none -> 17.2 us  [the longest x6 9.92 us: local_call(): pl.pallas_call(kernel, out_shape=out_shape, in_specs=[SMEM] + [VMEM] * (l...]
    ppermute x3 -> x10, starting transfers between devices: 7.53 us -> 21.1 us  [to_chip(): return lax.ppermute(value, 'layer', ACROSS_CHIPS)]
    dot_general x4 -> x0, matrix products: 9.07 us -> none  [the longest x2 7.06 us: contract_rows(): lax.dot_general(left, right, (((0,), (0,)), ((), ())), preferred_element_...]
    all_to_all x1 -> x2, starting transfers between devices: 13.6 us -> 21 us  [gather_tokens(): lax.all_to_all(copies, 'feat', 0, 0, tiled=True)]
    dot_general x8, matrix products: 12.7 us -> 6.06 us  [dot(): return jnp.dot(left, right, preferred_element_type=F32)]
    ppermute x6 -> x16, starting transfers between devices: 11.9 us -> 18.1 us  [to_core(): return lax.ppermute(value, 'layer', ACROSS_CORES)]
  transfers between devices with their start and end apart: 11 -> 29, of which waited for: 7 -> 13; matrix products, arithmetic and copies ran while one was open for 10% -> 6% of each run, Pallas kernels for 0% -> 7%
where the time goes in v3:
time: 165 us
  waiting for transfers between devices  66.8 us (40%)
  starting transfers between devices  65.8 us (40%)
  Pallas kernels  17.2 us (10%)
  matrix products  6.06 us (4%)
  local copies, waits for them, and re-layouts  3.88 us (2%)
  other arithmetic  3.84 us (2%)
    ppermute x10, waiting for transfers between devices, to_chip(): return lax.ppermute(value, 'layer', ACROSS_CHIPS)  26.7 us
    all_to_all x2, waiting for transfers between devices, gather_tokens(): lax.all_to_all(copies, 'feat', 0, 0, tiled=True)  22.1 us
    ppermute x10, starting transfers between devices, to_chip(): return lax.ppermute(value, 'layer', ACROSS_CHIPS)  21.1 us
    all_to_all x2, starting transfers between devices, gather_tokens(): lax.all_to_all(copies, 'feat', 0, 0, tiled=True)  21 us
    ppermute x16, starting transfers between devices, to_core(): return lax.ppermute(value, 'layer', ACROSS_CORES)  18.1 us
    all_to_all x1, waiting for transfers between devices, body(): lax.all_to_all(recon_terms.reshape(blocks, tokens // blocks, model_width)...  14.6 us
    pallas_call x6, Pallas kernels, local_call(): pl.pallas_call(kernel, out_shape=out_shape, in_specs=[SMEM] + [VMEM] * (l...  9.92 us
    pallas_call x4, Pallas kernels, write_step(): pl.pallas_call(functools.partial(kernel, scale), grid=(STEP_BLOCKS,), out...  7.3 us
  transfers between devices with their start and end apart: 29, of which 13 were waited for; matrix products, arithmetic and copies ran while one was open for 6% of the time, Pallas kernels for 7%

profile of v3, /device:TPU:1, one launch (start us, length us, event | category | flops | bytes accessed | tf_op | source)
XLA Modules:
  0.0 164.7 jit_solution(4952329501969132906)
XLA Ops:
  0.6 1.6 broadcast_in_dim.26
  2.2 13.7 %all-to-all-start = ((bf16[64,8,576]{2,1,0:T(8,128)(2,1)}), bf16[64,8,576]{2,1,0:T(8,128)(2,1)S(1)}, u32[]{:S(2)}, u32[]{:S(2)}) async-start(bf16[64,8,576]{2,1,0:T(8,128)(2,1)} %broadcast_in_dim.26), calls=%async_computation | async-start | bytes 1310720 | tf_op jit(solution)/shard_map/all_to_all | solution.py:31
  16.0 17.9 %all-to-all-done = bf16[64,8,576]{2,1,0:T(8,128)(2,1)S(1)} async-done(((bf16[64,8,576]{2,1,0:T(8,128)(2,1)}), bf16[64,8,576]{2,1,0:T(8,128)(2,1)S(1)}, u32[]{:S(2)}, u32[]{:S(2)}) %all-to-all-start) | async-done | bytes 589856 | tf_op jit(solution)/shard_map/all_to_all | solution.py:31
  34.8 3.8 %collective-permute-start.2 = (f32[128,1024]{1,0:T(8,128)S(1)}, f32[128,1024]{1,0:T(8,128)S(1)}, u32[]{:S(2)}, u32[]{:S(2)}) collective-permute-start(f32[128,1024]{1,0:T(8,128)S(1)} %fusion), channel_id=1, source_target_pairs={{0,64},{64,0},{128,192},{192,128},{1,65},{65,1},{129,193},{193,129... | collective-permute-start | bytes 1572872 | tf_op jit(solution)/shard_map/ppermute | solution.py:20
  41.9 2.5 %collective-permute-start.6 = (bf16[128,1024]{1,0:T(8,128)(2,1)S(1)}, bf16[128,1024]{1,0:T(8,128)(2,1)S(1)}, u32[]{:S(2)}, u32[]{:S(2)}) collective-permute-start(bf16[128,1024]{1,0:T(8,128)(2,1)S(1)} %get-tuple-element.86), channel_id=1, source_target_pairs={{0,128},{64,192},{128,0},{192,64},{1,129},{65,193},{129,1},{193,65... | collective-permute-start | bytes 786440 | tf_op jit(solution)/shard_map/ppermute | solution.py:24
  46.0 5.0 %collective-permute-done.6 = bf16[128,1024]{1,0:T(8,128)(2,1)S(1)} collective-permute-done((bf16[128,1024]{1,0:T(8,128)(2,1)S(1)}, bf16[128,1024]{1,0:T(8,128)(2,1)S(1)}, u32[]{:S(2)}, u32[]{:S(2)}) %collective-permute-start.6) | collective-permute-done | bytes 262176 | tf_op jit(solution)/shard_map/ppermute | solution.py:24
  52.2 2.5 %collective-permute-start.8 = (bf16[128,1024]{1,0:T(8,128)(2,1)S(1)}, bf16[128,1024]{1,0:T(8,128)(2,1)S(1)}, u32[]{:S(2)}, u32[]{:S(2)}) collective-permute-start(bf16[128,1024]{1,0:T(8,128)(2,1)S(1)} %get-tuple-element.94.refs_0_.refs_1_), channel_id=1, source_target_pairs={{0,128},{64,192},{128,0},{192,64},{1,129},{65,193},{129,1},{193,65... | collective-permute-start | bytes 786440 | tf_op jit(solution)/shard_map/ppermute | solution.py:24
  54.6 2.3 %collective-permute-start.7 = (bf16[128,1024]{1,0:T(8,128)(2,1)S(1)}, bf16[128,1024]{1,0:T(8,128)(2,1)S(1)}, u32[]{:S(2)}, u32[]{:S(2)}) collective-permute-start(bf16[128,1024]{1,0:T(8,128)(2,1)S(1)} %get-tuple-element.94.refs_0_.refs_1_), channel_id=1, source_target_pairs={{0,64},{64,0},{128,192},{192,128},{1,65},{65,1},{129,193},{193,129... | collective-permute-start | bytes 786440 | tf_op jit(solution)/shard_map/ppermute | solution.py:20
  58.1 1.6 collective-permute-start.9
  59.8 2.4 %collective-permute-start.4 = (bf16[128,1024]{1,0:T(8,128)(2,1)S(1)}, bf16[128,1024]{1,0:T(8,128)(2,1)S(1)}, u32[]{:S(2)}, u32[]{:S(2)}) collective-permute-start(bf16[128,1024]{1,0:T(8,128)(2,1)S(1)} %get-tuple-element.92.refs_3_.refs_0_), channel_id=1, source_target_pairs={{0,128},{64,192},{128,0},{192,64},{1,129},{65,193},{129,1},{193,65... | collective-permute-start | bytes 786440 | tf_op jit(solution)/shard_map/ppermute | solution.py:24
  64.5 3.0 %shard_map.68.refs_4_ = f32[512,576]{1,0:T(8,128)S(1)} custom-call(s32[4]{0:T(128)S(1)} %pad_add_fusion.starts_ref, bf16[128,1024]{1,0:T(8,128)(2,1)S(1)} %get-tuple-element.94.refs_0_.refs_1_, bf16[128,1024]{1,0:T(8,128)(2,1)S(1)} %collective-permute-done.7.refs_1_.refs_2_, bf16[128,1024]{1,0:T(8,128)(2,1)S(1)} %collective-permute-done.8.refs_2_.refs_3_, ...), custom_call_target="tpu_custom_call" | custom-call | flops 905969664 | bytes 3932176 | tf_op jit(solution)/shard_map/pallas_call | solution.py:56
  67.6 1.6 collective-permute-done.4.refs_0_.refs_2_
  71.2 2.4 %shard_map.69 = bf16[512,576]{1,0:T(8,128)(2,1)} custom-call(s32[4]{0:T(128)S(1)} %pad_add_fusion.starts_ref, bf16[128,1024]{1,0:T(8,128)(2,1)S(1)} %collective-permute-done.4.refs_0_.refs_2_, bf16[128,1024]{1,0:T(8,128)(2,1)S(1)} %collective-permute-done.11.refs_1_.refs_3_, bf16[576,1024]{1,0:T(8,128)(2,1)S(1)} %get-tuple-element.77.refs_6_.refs_2_.refs_0_, ...), custom_call_target="tpu_custom_call" | custom-call | flops 301989888 | bytes 4063248 | tf_op jit(solution)/shard_map/pallas_call | solution.py:56
  73.5 5.5 %all-to-all-start.1 = ((bf16[64,8,576]{2,1,0:T(8,128)(2,1)}), bf16[64,8,576]{2,1,0:T(8,128)(2,1)S(1)}, u32[]{:S(2)}, u32[]{:S(2)}) async-start(bf16[64,8,576]{2,1,0:T(8,128)(2,1)} %bitcast.13), calls=%async_computation.1 | async-start | bytes 1310720 | tf_op jit(solution)/shard_map/all_to_all | solution.py:210
  79.0 1.3 reduce
  80.3 2.5 %collective-permute-start.12 = (bf16[128,1024]{1,0:T(8,128)(2,1)}, bf16[128,1024]{1,0:T(8,128)(2,1)}, u32[]{:S(2)}, u32[]{:S(2)}) collective-permute-start(bf16[128,1024]{1,0:T(8,128)(2,1)} %get-tuple-element.42), channel_id=1, source_target_pairs={{0,128},{64,192},{128,0},{192,64},{1,129},{65,193},{129,1},{193,65... | collective-permute-start | bytes 786440 | tf_op jit(solution)/shard_map/ppermute | solution.py:24
  82.8 14.6 %all-to-all-done.1 = bf16[64,8,576]{2,1,0:T(8,128)(2,1)S(1)} async-done(((bf16[64,8,576]{2,1,0:T(8,128)(2,1)}), bf16[64,8,576]{2,1,0:T(8,128)(2,1)S(1)}, u32[]{:S(2)}, u32[]{:S(2)}) %all-to-all-start.1) | async-done | bytes 589856 | tf_op jit(solution)/shard_map/all_to_all | solution.py:210
  99.1 7.3 %all-to-all-start.2 = ((bf16[64,8,576]{2,1,0:T(8,128)(2,1)}), bf16[64,8,576]{2,1,0:T(8,128)(2,1)S(1)}, u32[]{:S(2)}, u32[]{:S(2)}) async-start(bf16[64,8,576]{2,1,0:T(8,128)(2,1)} %broadcast_in_dim.28), calls=%async_computation.2 | async-start | bytes 1310720 | tf_op jit(solution)/shard_map/all_to_all | solution.py:31
  106.5 2.5 %collective-permute-start.13 = (bf16[128,1024]{1,0:T(8,128)(2,1)}, bf16[128,1024]{1,0:T(8,128)(2,1)}, u32[]{:S(2)}, u32[]{:S(2)}) collective-permute-start(bf16[128,1024]{1,0:T(8,128)(2,1)} %get-tuple-element.45), channel_id=1, source_target_pairs={{0,128},{64,192},{128,0},{192,64},{1,129},{65,193},{129,1},{193,65... | collective-permute-start | bytes 786440 | tf_op jit(solution)/shard_map/ppermute | solution.py:24
  109.0 10.5 %collective-permute-done.13 = bf16[128,1024]{1,0:T(8,128)(2,1)} collective-permute-done((bf16[128,1024]{1,0:T(8,128)(2,1)}, bf16[128,1024]{1,0:T(8,128)(2,1)}, u32[]{:S(2)}, u32[]{:S(2)}) %collective-permute-start.13) | collective-permute-done | bytes 262176 | tf_op jit(solution)/shard_map/ppermute | solution.py:24
  119.5 4.3 %all-to-all-done.2 = bf16[64,8,576]{2,1,0:T(8,128)(2,1)S(1)} async-done(((bf16[64,8,576]{2,1,0:T(8,128)(2,1)}), bf16[64,8,576]{2,1,0:T(8,128)(2,1)S(1)}, u32[]{:S(2)}, u32[]{:S(2)}) %all-to-all-start.2) | async-done | bytes 589856 | tf_op jit(solution)/shard_map/all_to_all | solution.py:31
  124.9 4.5 %collective-permute-start.14 = (bf16[128,1024]{1,0:T(8,128)(2,1)S(1)}, bf16[128,1024]{1,0:T(8,128)(2,1)S(1)}, u32[]{:S(2)}, u32[]{:S(2)}) collective-permute-start(bf16[128,1024]{1,0:T(8,128)(2,1)S(1)} %get-tuple-element.50), channel_id=1, source_target_pairs={{0,64},{64,0},{128,192},{192,128},{1,65},{65,1},{129,193},{193,129... | collective-permute-start | bytes 786440 | tf_op jit(solution)/shard_map/ppermute | solution.py:20
  132.4 2.5 %collective-permute-start.16 = (bf16[128,1024]{1,0:T(8,128)(2,1)S(1)}, bf16[128,1024]{1,0:T(8,128)(2,1)S(1)}, u32[]{:S(2)}, u32[]{:S(2)}) collective-permute-start(bf16[128,1024]{1,0:T(8,128)(2,1)S(1)} %get-tuple-element.54), channel_id=1, source_target_pairs={{0,128},{64,192},{128,0},{192,64},{1,129},{65,193},{129,1},{193,65... | collective-permute-start | bytes 786440 | tf_op jit(solution)/shard_map/ppermute | solution.py:24
  137.7 1.8 %shard_map.74.refs_4_ = bf16[576,2048]{1,0:T(8,128)(2,1)} custom-call(bf16[512,576]{1,0:T(8,128)(2,1)S(1)} %pad_maximum_fusion.1.refs_0_.left_ref, bf16[128,1024]{1,0:T(8,128)(2,1)S(1)} %get-tuple-element.94.refs_0_.refs_1_, bf16[128,1024]{1,0:T(8,128)(2,1)S(1)} %copy-done.7, bf16[128,1024]{1,0:T(8,128)(2,1)S(1)} %copy-done.5, bf16[128,1024]{1,0:T(8,128)(2,1)S(1)} %copy-done.11), custom_call_target="tpu_custom_call" | custom-call | flops 603979776 | bytes 2228224 | tf_op jit(solution)/shard_map/pallas_call | solution.py:136
  139.6 1.8 %shard_map.75 = bf16[576,2048]{1,0:T(8,128)(2,1)} custom-call(bf16[512,576]{1,0:T(8,128)(2,1)S(1)} %pad_maximum_fusion.1.refs_0_.left_ref, bf16[128,1024]{1,0:T(8,128)(2,1)S(1)} %get-tuple-element.92.refs_3_.refs_0_, bf16[128,1024]{1,0:T(8,128)(2,1)S(1)} %copy-done.9, bf16[128,1024]{1,0:T(8,128)(2,1)S(1)} %copy-done.1, ...), custom_call_target="tpu_custom_call", output_to_operand_aliasing={{}: (5, {})} | custom-call | flops 603979776 | bytes 2228224 | tf_op jit(solution)/shard_map/pallas_call | solution.py:136
  141.5 1.3 fusion.30
  144.0 2.5 %collective-permute-start.22 = (bf16[128,1024]{1,0:T(8,128)(2,1)S(1)}, bf16[128,1024]{1,0:T(8,128)(2,1)S(1)}, u32[]{:S(2)}, u32[]{:S(2)}) collective-permute-start(bf16[128,1024]{1,0:T(8,128)(2,1)S(1)} %select_convert_fusion.1.refs_1_), channel_id=1, source_target_pairs={{0,128},{64,192},{128,0},{192,64},{1,129},{65,193},{129,1},{193,65... | collective-permute-start | bytes 786440 | tf_op jit(solution)/shard_map/ppermute | solution.py:24
  147.2 2.7 %collective-permute-start.23 = (bf16[128,1024]{1,0:T(8,128)(2,1)S(1)}, bf16[128,1024]{1,0:T(8,128)(2,1)S(1)}, u32[]{:S(2)}, u32[]{:S(2)}) collective-permute-start(bf16[128,1024]{1,0:T(8,128)(2,1)S(1)} %select_convert_fusion.refs_0_), channel_id=1, source_target_pairs={{0,128},{64,192},{128,0},{192,64},{1,129},{65,193},{129,1},{193,65... | collective-permute-start | bytes 786440 | tf_op jit(solution)/shard_map/ppermute | solution.py:24
  150.0 3.4 %collective-permute-done.22.refs_3_ = bf16[128,1024]{1,0:T(8,128)(2,1)S(1)} collective-permute-done((bf16[128,1024]{1,0:T(8,128)(2,1)S(1)}, bf16[128,1024]{1,0:T(8,128)(2,1)S(1)}, u32[]{:S(2)}, u32[]{:S(2)}) %collective-permute-start.22) | collective-permute-done | bytes 262176 | tf_op jit(solution)/shard_map/ppermute | solution.py:24
  153.4 5.6 %collective-permute-done.23.refs_2_ = bf16[128,1024]{1,0:T(8,128)(2,1)S(1)} collective-permute-done((bf16[128,1024]{1,0:T(8,128)(2,1)S(1)}, bf16[128,1024]{1,0:T(8,128)(2,1)S(1)}, u32[]{:S(2)}, u32[]{:S(2)}) %collective-permute-start.23) | collective-permute-done | bytes 262176 | tf_op jit(solution)/shard_map/ppermute | solution.py:24
  161.1 1.8 %shard_map.76.refs_4_ = bf16[576,2048]{1,0:T(8,128)(2,1)} custom-call(bf16[512,576]{1,0:T(8,128)(2,1)S(1)} %pad_maximum_fusion.refs_0_.left_ref, bf16[128,1024]{1,0:T(8,128)(2,1)S(1)} %select_convert_fusion.1.refs_1_, bf16[128,1024]{1,0:T(8,128)(2,1)S(1)} %collective-permute-done.20.refs_2_, bf16[128,1024]{1,0:T(8,128)(2,1)S(1)} %collective-permute-done.22.refs_3_, ...), custom_call_target="tpu_custom_call" | custom-call | flops 603979776 | bytes 2228224 | tf_op jit(solution)/shard_map/pallas_call | solution.py:136
  162.9 1.8 %shard_map.77 = bf16[576,2048]{1,0:T(8,128)(2,1)} custom-call(bf16[512,576]{1,0:T(8,128)(2,1)S(1)} %pad_maximum_fusion.refs_0_.left_ref, bf16[128,1024]{1,0:T(8,128)(2,1)S(1)} %select_convert_fusion.refs_0_, bf16[128,1024]{1,0:T(8,128)(2,1)S(1)} %collective-permute-done.21.refs_1_, ...), custom_call_target="tpu_custom_call", output_to_operand_aliasing={{}: (5, {})} | custom-call | flops 603979776 | bytes 2228224 | tf_op jit(solution)/shard_map/pallas_call | solution.py:136
  (127 shorter events, 25.0 us)
Async XLA Ops:
  2.2 31.8 %copy-start.12 = (bf16[1,576,2048]{2,1,0:T(8,128)(2,1)S(1)}, bf16[1,576,2048]{2,1,0:T(8,128)(2,1)}, u32[]{:S(2)}) copy-start(bf16[1,576,2048]{2,1,0:T(8,128)(2,1)} %param.6) | copy-start | bytes 7077892
  2.2 31.7 %all-to-all-start = ((bf16[64,8,576]{2,1,0:T(8,128)(2,1)}), bf16[64,8,576]{2,1,0:T(8,128)(2,1)S(1)}, u32[]{:S(2)}, u32[]{:S(2)}) async-start(bf16[64,8,576]{2,1,0:T(8,128)(2,1)} %broadcast_in_dim.26), calls=%async_computation | async-start | bytes 1310720 | tf_op jit(solution)/shard_map/all_to_all | solution.py:31
  16.0 34.9 %copy-start.29 = (f32[1,1024]{1,0:T(1,128)}, f32[1,1024]{1,0:T(1,128)S(1)}, u32[]{:S(2)}) copy-start(f32[1,1024]{1,0:T(1,128)S(1)} %get-tuple-element.90) | copy-start | bytes 12292
  16.0 40.9 %copy-start.31 = (f32[1,1024]{1,0:T(1,128)}, f32[1,1024]{1,0:T(1,128)S(1)}, u32[]{:S(2)}) copy-start(f32[1,1024]{1,0:T(1,128)S(1)} %get-tuple-element.91) | copy-start | bytes 12292
  34.8 22.1 %collective-permute-start.2 = (f32[128,1024]{1,0:T(8,128)S(1)}, f32[128,1024]{1,0:T(8,128)S(1)}, u32[]{:S(2)}, u32[]{:S(2)}) collective-permute-start(f32[128,1024]{1,0:T(8,128)S(1)} %fusion), channel_id=1, source_target_pairs={{0,64},{64,0},{128,192},{192,128},{1,65},{65,1},{129,193},{193,129... | collective-permute-start | bytes 1572872 | tf_op jit(solution)/shard_map/ppermute | solution.py:20
  38.6 2.3 %collective-permute-start = (f32[128,1024]{1,0:T(8,128)S(1)}, f32[128,1024]{1,0:T(8,128)S(1)}, u32[]{:S(2)}, u32[]{:S(2)}) collective-permute-start(f32[128,1024]{1,0:T(8,128)S(1)} %fusion.9), channel_id=1, source_target_pairs={{0,64},{64,0},{128,192},{192,128},{1,65},{65,1},{129,193},{193,129... | collective-permute-start | bytes 1572872 | tf_op jit(solution)/shard_map/ppermute | solution.py:20
  39.0 5.3 %collective-permute-start.1 = (f32[128,1024]{1,0:T(8,128)S(1)}, f32[128,1024]{1,0:T(8,128)S(1)}, u32[]{:S(2)}, u32[]{:S(2)}) collective-permute-start(f32[128,1024]{1,0:T(8,128)S(1)} %fusion.3), channel_id=1, source_target_pairs={{0,64},{64,0},{128,192},{192,128},{1,65},{65,1},{129,193},{193,129... | collective-permute-start | bytes 1572872 | tf_op jit(solution)/shard_map/ppermute | solution.py:20
  39.9 6.1 %collective-permute-start.5 = (f32[128,1024]{1,0:T(8,128)S(1)}, f32[128,1024]{1,0:T(8,128)S(1)}, u32[]{:S(2)}, u32[]{:S(2)}) collective-permute-start(f32[128,1024]{1,0:T(8,128)S(1)} %fusion.6), channel_id=1, source_target_pairs={{0,64},{64,0},{128,192},{192,128},{1,65},{65,1},{129,193},{193,129... | collective-permute-start | bytes 1572872 | tf_op jit(solution)/shard_map/ppermute | solution.py:20
  41.9 9.0 %collective-permute-start.6 = (bf16[128,1024]{1,0:T(8,128)(2,1)S(1)}, bf16[128,1024]{1,0:T(8,128)(2,1)S(1)}, u32[]{:S(2)}, u32[]{:S(2)}) collective-permute-start(bf16[128,1024]{1,0:T(8,128)(2,1)S(1)} %get-tuple-element.86), channel_id=1, source_target_pairs={{0,128},{64,192},{128,0},{192,64},{1,129},{65,193},{129,1},{193,65... | collective-permute-start | bytes 786440 | tf_op jit(solution)/shard_map/ppermute | solution.py:24
  45.5 11.5 %collective-permute-start.3 = (bf16[128,1024]{1,0:T(8,128)(2,1)S(1)}, bf16[128,1024]{1,0:T(8,128)(2,1)S(1)}, u32[]{:S(2)}, u32[]{:S(2)}) collective-permute-start(bf16[128,1024]{1,0:T(8,128)(2,1)S(1)} %get-tuple-element.88), channel_id=1, source_target_pairs={{0,128},{64,192},{128,0},{192,64},{1,129},{65,193},{129,1},{193,65... | collective-permute-start | bytes 786440 | tf_op jit(solution)/shard_map/ppermute | solution.py:24
  52.2 10.1 %collective-permute-start.8 = (bf16[128,1024]{1,0:T(8,128)(2,1)S(1)}, bf16[128,1024]{1,0:T(8,128)(2,1)S(1)}, u32[]{:S(2)}, u32[]{:S(2)}) collective-permute-start(bf16[128,1024]{1,0:T(8,128)(2,1)S(1)} %get-tuple-element.94.refs_0_.refs_1_), channel_id=1, source_target_pairs={{0,128},{64,192},{128,0},{192,64},{1,129},{65,193},{129,1},{193,65... | collective-permute-start | bytes 786440 | tf_op jit(solution)/shard_map/ppermute | solution.py:24
  54.6 9.1 %collective-permute-start.7 = (bf16[128,1024]{1,0:T(8,128)(2,1)S(1)}, bf16[128,1024]{1,0:T(8,128)(2,1)S(1)}, u32[]{:S(2)}, u32[]{:S(2)}) collective-permute-start(bf16[128,1024]{1,0:T(8,128)(2,1)S(1)} %get-tuple-element.94.refs_0_.refs_1_), channel_id=1, source_target_pairs={{0,64},{64,0},{128,192},{192,128},{1,65},{65,1},{129,193},{193,129... | collective-permute-start | bytes 786440 | tf_op jit(solution)/shard_map/ppermute | solution.py:20
  58.1 5.5 %collective-permute-start.9 = (bf16[128,1024]{1,0:T(8,128)(2,1)S(1)}, bf16[128,1024]{1,0:T(8,128)(2,1)S(1)}, u32[]{:S(2)}, u32[]{:S(2)}) collective-permute-start(bf16[128,1024]{1,0:T(8,128)(2,1)S(1)} %get-tuple-element.92.refs_3_.refs_0_), channel_id=1, source_target_pairs={{0,64},{64,0},{128,192},{192,128},{1,65},{65,1},{129,193},{193,129... | collective-permute-start | bytes 786440 | tf_op jit(solution)/shard_map/ppermute | solution.py:20
  59.8 9.4 %collective-permute-start.4 = (bf16[128,1024]{1,0:T(8,128)(2,1)S(1)}, bf16[128,1024]{1,0:T(8,128)(2,1)S(1)}, u32[]{:S(2)}, u32[]{:S(2)}) collective-permute-start(bf16[128,1024]{1,0:T(8,128)(2,1)S(1)} %get-tuple-element.92.refs_3_.refs_0_), channel_id=1, source_target_pairs={{0,128},{64,192},{128,0},{192,64},{1,129},{65,193},{129,1},{193,65... | collective-permute-start | bytes 786440 | tf_op jit(solution)/shard_map/ppermute | solution.py:24
  62.2 2.3 %collective-permute-start.10 = (bf16[128,1024]{1,0:T(8,128)(2,1)S(1)}, bf16[128,1024]{1,0:T(8,128)(2,1)S(1)}, u32[]{:S(2)}, u32[]{:S(2)}) collective-permute-start(bf16[128,1024]{1,0:T(8,128)(2,1)S(1)} %collective-permute-done.8.refs_2_.refs_3_), channel_id=1, source_target_pairs={{0,64},{64,0},{128,192},{192,128},{1,65},{65,1},{129,193},{193,129... | collective-permute-start | bytes 786440 | tf_op jit(solution)/shard_map/ppermute | solution.py:20
  69.2 1.9 %collective-permute-start.11 = (bf16[128,1024]{1,0:T(8,128)(2,1)S(1)}, bf16[128,1024]{1,0:T(8,128)(2,1)S(1)}, u32[]{:S(2)}, u32[]{:S(2)}) collective-permute-start(bf16[128,1024]{1,0:T(8,128)(2,1)S(1)} %collective-permute-done.4.refs_0_.refs_2_), channel_id=1, source_target_pairs={{0,64},{64,0},{128,192},{192,128},{1,65},{65,1},{129,193},{193,129... | collective-permute-start | bytes 786440 | tf_op jit(solution)/shard_map/ppermute | solution.py:20
  73.5 23.9 %all-to-all-start.1 = ((bf16[64,8,576]{2,1,0:T(8,128)(2,1)}), bf16[64,8,576]{2,1,0:T(8,128)(2,1)S(1)}, u32[]{:S(2)}, u32[]{:S(2)}) async-start(bf16[64,8,576]{2,1,0:T(8,128)(2,1)} %bitcast.13), calls=%async_computation.1 | async-start | bytes 1310720 | tf_op jit(solution)/shard_map/all_to_all | solution.py:210
  80.3 17.9 %collective-permute-start.12 = (bf16[128,1024]{1,0:T(8,128)(2,1)}, bf16[128,1024]{1,0:T(8,128)(2,1)}, u32[]{:S(2)}, u32[]{:S(2)}) collective-permute-start(bf16[128,1024]{1,0:T(8,128)(2,1)} %get-tuple-element.42), channel_id=1, source_target_pairs={{0,128},{64,192},{128,0},{192,64},{1,129},{65,193},{129,1},{193,65... | collective-permute-start | bytes 786440 | tf_op jit(solution)/shard_map/ppermute | solution.py:24
  99.1 24.6 %all-to-all-start.2 = ((bf16[64,8,576]{2,1,0:T(8,128)(2,1)}), bf16[64,8,576]{2,1,0:T(8,128)(2,1)S(1)}, u32[]{:S(2)}, u32[]{:S(2)}) async-start(bf16[64,8,576]{2,1,0:T(8,128)(2,1)} %broadcast_in_dim.28), calls=%async_computation.2 | async-start | bytes 1310720 | tf_op jit(solution)/shard_map/all_to_all | solution.py:31
  106.5 13.0 %collective-permute-start.13 = (bf16[128,1024]{1,0:T(8,128)(2,1)}, bf16[128,1024]{1,0:T(8,128)(2,1)}, u32[]{:S(2)}, u32[]{:S(2)}) collective-permute-start(bf16[128,1024]{1,0:T(8,128)(2,1)} %get-tuple-element.45), channel_id=1, source_target_pairs={{0,128},{64,192},{128,0},{192,64},{1,129},{65,193},{129,1},{193,65... | collective-permute-start | bytes 786440 | tf_op jit(solution)/shard_map/ppermute | solution.py:24
  124.9 6.4 %collective-permute-start.14 = (bf16[128,1024]{1,0:T(8,128)(2,1)S(1)}, bf16[128,1024]{1,0:T(8,128)(2,1)S(1)}, u32[]{:S(2)}, u32[]{:S(2)}) collective-permute-start(bf16[128,1024]{1,0:T(8,128)(2,1)S(1)} %get-tuple-element.50), channel_id=1, source_target_pairs={{0,64},{64,0},{128,192},{192,128},{1,65},{65,1},{129,193},{193,129... | collective-permute-start | bytes 786440 | tf_op jit(solution)/shard_map/ppermute | solution.py:20
  129.4 1.8 %collective-permute-start.15 = (bf16[128,1024]{1,0:T(8,128)(2,1)S(1)}, bf16[128,1024]{1,0:T(8,128)(2,1)S(1)}, u32[]{:S(2)}, u32[]{:S(2)}) collective-permute-start(bf16[128,1024]{1,0:T(8,128)(2,1)S(1)} %get-tuple-element.51), channel_id=1, source_target_pairs={{0,64},{64,0},{128,192},{192,128},{1,65},{65,1},{129,193},{193,129... | collective-permute-start | bytes 786440 | tf_op jit(solution)/shard_map/ppermute | solution.py:20
  130.7 4.8 %collective-permute-start.17 = (bf16[128,1024]{1,0:T(8,128)(2,1)S(1)}, bf16[128,1024]{1,0:T(8,128)(2,1)S(1)}, u32[]{:S(2)}, u32[]{:S(2)}) collective-permute-start(bf16[128,1024]{1,0:T(8,128)(2,1)S(1)} %get-tuple-element.58), channel_id=1, source_target_pairs={{0,64},{64,0},{128,192},{192,128},{1,65},{65,1},{129,193},{193,129... | collective-permute-start | bytes 786440 | tf_op jit(solution)/shard_map/ppermute | solution.py:20
  131.2 4.3 %collective-permute-start.18 = (bf16[128,1024]{1,0:T(8,128)(2,1)S(1)}, bf16[128,1024]{1,0:T(8,128)(2,1)S(1)}, u32[]{:S(2)}, u32[]{:S(2)}) collective-permute-start(bf16[128,1024]{1,0:T(8,128)(2,1)S(1)} %get-tuple-element.59), channel_id=1, source_target_pairs={{0,64},{64,0},{128,192},{192,128},{1,65},{65,1},{129,193},{193,129... | collective-permute-start | bytes 786440 | tf_op jit(solution)/shard_map/ppermute | solution.py:20
  132.4 10.4 %collective-permute-start.16 = (bf16[128,1024]{1,0:T(8,128)(2,1)S(1)}, bf16[128,1024]{1,0:T(8,128)(2,1)S(1)}, u32[]{:S(2)}, u32[]{:S(2)}) collective-permute-start(bf16[128,1024]{1,0:T(8,128)(2,1)S(1)} %get-tuple-element.54), channel_id=1, source_target_pairs={{0,128},{64,192},{128,0},{192,64},{1,129},{65,193},{129,1},{193,65... | collective-permute-start | bytes 786440 | tf_op jit(solution)/shard_map/ppermute | solution.py:24
  134.9 12.2 %collective-permute-start.19 = (bf16[128,1024]{1,0:T(8,128)(2,1)S(1)}, bf16[128,1024]{1,0:T(8,128)(2,1)S(1)}, u32[]{:S(2)}, u32[]{:S(2)}) collective-permute-start(bf16[128,1024]{1,0:T(8,128)(2,1)S(1)} %get-tuple-element.67), channel_id=1, source_target_pairs={{0,128},{64,192},{128,0},{192,64},{1,129},{65,193},{129,1},{193,65... | collective-permute-start | bytes 786440 | tf_op jit(solution)/shard_map/ppermute | solution.py:24
  143.0 4.1 %collective-permute-start.20 = (bf16[128,1024]{1,0:T(8,128)(2,1)S(1)}, bf16[128,1024]{1,0:T(8,128)(2,1)S(1)}, u32[]{:S(2)}, u32[]{:S(2)}) collective-permute-start(bf16[128,1024]{1,0:T(8,128)(2,1)S(1)} %select_convert_fusion.1.refs_1_), channel_id=1, source_target_pairs={{0,64},{64,0},{128,192},{192,128},{1,65},{65,1},{129,193},{193,129... | collective-permute-start | bytes 786440 | tf_op jit(solution)/shard_map/ppermute | solution.py:20
  144.0 9.4 %collective-permute-start.22 = (bf16[128,1024]{1,0:T(8,128)(2,1)S(1)}, bf16[128,1024]{1,0:T(8,128)(2,1)S(1)}, u32[]{:S(2)}, u32[]{:S(2)}) collective-permute-start(bf16[128,1024]{1,0:T(8,128)(2,1)S(1)} %select_convert_fusion.1.refs_1_), channel_id=1, source_target_pairs={{0,128},{64,192},{128,0},{192,64},{1,129},{65,193},{129,1},{193,65... | collective-permute-start | bytes 786440 | tf_op jit(solution)/shard_map/ppermute | solution.py:24
  147.2 11.8 %collective-permute-start.23 = (bf16[128,1024]{1,0:T(8,128)(2,1)S(1)}, bf16[128,1024]{1,0:T(8,128)(2,1)S(1)}, u32[]{:S(2)}, u32[]{:S(2)}) collective-permute-start(bf16[128,1024]{1,0:T(8,128)(2,1)S(1)} %select_convert_fusion.refs_0_), channel_id=1, source_target_pairs={{0,128},{64,192},{128,0},{192,64},{1,129},{65,193},{129,1},{193,65... | collective-permute-start | bytes 786440 | tf_op jit(solution)/shard_map/ppermute | solution.py:24
  159.0 2.0 %collective-permute-start.25 = (bf16[128,1024]{1,0:T(8,128)(2,1)S(1)}, bf16[128,1024]{1,0:T(8,128)(2,1)S(1)}, u32[]{:S(2)}, u32[]{:S(2)}) collective-permute-start(bf16[128,1024]{1,0:T(8,128)(2,1)S(1)} %collective-permute-done.22.refs_3_), channel_id=1, source_target_pairs={{0,64},{64,0},{128,192},{192,128},{1,65},{65,1},{129,193},{193,129... | collective-permute-start | bytes 786440 | tf_op jit(solution)/shard_map/ppermute | solution.py:20
  159.9 3.0 %collective-permute-start.21 = (bf16[128,1024]{1,0:T(8,128)(2,1)S(1)}, bf16[128,1024]{1,0:T(8,128)(2,1)S(1)}, u32[]{:S(2)}, u32[]{:S(2)}) collective-permute-start(bf16[128,1024]{1,0:T(8,128)(2,1)S(1)} %select_convert_fusion.refs_0_), channel_id=1, source_target_pairs={{0,64},{64,0},{128,192},{192,128},{1,65},{65,1},{129,193},{193,129... | collective-permute-start | bytes 786440 | tf_op jit(solution)/shard_map/ppermute | solution.py:20
  159.9 3.0 %collective-permute-start.24 = (bf16[128,1024]{1,0:T(8,128)(2,1)S(1)}, bf16[128,1024]{1,0:T(8,128)(2,1)S(1)}, u32[]{:S(2)}, u32[]{:S(2)}) collective-permute-start(bf16[128,1024]{1,0:T(8,128)(2,1)S(1)} %collective-permute-done.23.refs_2_), channel_id=1, source_target_pairs={{0,64},{64,0},{128,192},{192,128},{1,65},{65,1},{129,193},{193,129... | collective-permute-start | bytes 786440 | tf_op jit(solution)/shard_map/ppermute | solution.py:20
  (31 other events, 201.9 us)

commit v4 on v3

--- a/solution.py
+++ b/solution.py
@@ -11,7 +11,6 @@
 BF16 = jnp.bfloat16
 F32 = jnp.float32
 PARTS = 2
-STEP_BLOCKS = 1
 ACROSS_CORES = [(0, 1), (1, 0), (2, 3), (3, 2)]
 ACROSS_CHIPS = [(0, 2), (1, 3), (2, 0), (3, 1)]
 
@@ -69,14 +68,19 @@
     before_ref = refs[-2] if has_before else None
     out_ref = refs[-1]
     rows = piece_refs[0].shape[0]
+    terms = {}
+    for part in range(part_count):
+        owners = [row for row, part_of_piece in places if part_of_piece == part]
+        pieces = [ref[...] for (_, part_of_piece), ref in zip(places, piece_refs) if part_of_piece == part]
+        if not pieces:
+            continue
+        product = dot_transposed(jnp.concatenate(pieces, axis=0), dec_refs[part][...])
+        for index, row in enumerate(owners):
+            terms.setdefault(row, []).append(product[index * rows : (index + 1) * rows])
     for row in range(out_ref.shape[0] // rows):
         where = pl.ds(pl.multiple_of(starts_ref[row], rows), rows)
-        total = before_ref[where, :] if has_before else None
-        for (row_of_piece, part), piece_ref in zip(places, piece_refs):
-            if row_of_piece == row:
-                term = dot_transposed(piece_ref[...], dec_refs[part][...])
-                total = term if total is None else total + term
-        out_ref[where, :] = (scale * total).astype(out_ref.dtype)
+        summands = terms.get(row, []) + ([before_ref[where, :]] if has_before else [])
+        out_ref[where, :] = (scale * sum(summands[1:], summands[0])).astype(out_ref.dtype)
 
 
 def decode(starts, pieces, dec_parts, before, scale, dtype):
@@ -109,41 +113,32 @@
     return local_call(kernel, out_shape, operands, 2 * rows * part_width * model_width * len(dec_parts))
 
 
-def step_kernel(scale, left_ref, *refs):
-    *piece_refs, _, out_ref = refs
-    rows = jnp.concatenate([piece_ref[...] for piece_ref in piece_refs], axis=0)
-    out_ref[...] = (scale * contract_rows(left_ref[...], rows)).astype(out_ref.dtype)
-
-
-def first_step_kernel(scale, *refs):
-    step_kernel(scale, *refs[:-1], None, refs[-1])
-
-
-def write_step(left, pieces, before, part_index, scale):
-    rows, part_width = pieces[0].shape
-    tokens, model_width = left.shape
-    block = part_width // STEP_BLOCKS
-    operands = [left, *pieces]
-    in_specs = [pl.BlockSpec((tokens, model_width), lambda index: (0, 0))]
-    in_specs += [pl.BlockSpec((rows, block), lambda index: (0, index))] * len(pieces)
-    kernel, aliases = first_step_kernel, {}
-    if before is not None:
-        aliases = {len(operands): 0}
-        operands.append(before)
-        in_specs.append(pl.BlockSpec(memory_space=pl.ANY))
-        kernel = step_kernel
-    first_block = part_index * STEP_BLOCKS
+def step_kernel(scale, part_count, piece_count, left_ref, *refs):
+    out_ref = refs[-1]
+    for part in range(part_count):
+
+        @pl.when(pl.program_id(0) == part)
+        def _(part=part):
+            pieces = [ref[...] for ref in refs[piece_count * part : piece_count * (part + 1)]]
+            total = contract_rows(left_ref[...], jnp.concatenate(pieces, axis=0))
+            out_ref[...] = (scale * total).astype(out_ref.dtype)
+
+
+def write_step(left, pieces, scale):
+    part_count, piece_count = len(pieces), len(pieces[0])
+    part_width = pieces[0][0].shape[1]
+    model_width = left.shape[1]
+    operands = [left, *(piece for part in pieces for piece in part)]
     return pl.pallas_call(
-        functools.partial(kernel, scale),
-        grid=(STEP_BLOCKS,),
-        out_shape=jax.ShapeDtypeStruct((model_width, part_width * PARTS), BF16),
-        in_specs=in_specs,
-        out_specs=pl.BlockSpec((model_width, block), lambda index: (0, first_block + index)),
-        input_output_aliases=aliases,
-        compiler_params=pltpu.CompilerParams(vmem_limit_bytes=16 * 1024 * 1024),
+        functools.partial(step_kernel, scale, part_count, piece_count),
+        grid=(part_count,),
+        out_shape=jax.ShapeDtypeStruct((model_width, part_width * part_count), BF16),
+        in_specs=[VMEM] * len(operands),
+        out_specs=pl.BlockSpec((model_width, part_width), lambda index: (0, index)),
+        compiler_params=pltpu.CompilerParams(vmem_limit_bytes=24 * 1024 * 1024),
         cost_estimate=pl.CostEstimate(
-            flops=2 * tokens * part_width * model_width,
-            bytes_accessed=2 * (tokens + model_width) * part_width,
+            flops=2 * left.size * part_width * part_count,
+            bytes_accessed=2 * (left.shape[0] + model_width) * part_width * part_count,
             transcendentals=0,
         ),
     )(*operands)
@@ -182,14 +177,19 @@
 
     part_width = slab_width // PARTS
     parts = [slice(index * part_width, (index + 1) * part_width) for index in range(PARTS)]
-    remainders, sums_mine, arrived, actives = [], [], [], []
+    remainders, leading_b, sums_mine = [], [], []
     for part in parts:
         enc_part = enc_local[:, part]
         sum_of_chip = dot(tok_of_chip, enc_part) + to_core(dot(tok_of_both, enc_part))
         leading = lax.reduce_precision(sum_of_chip, 8, 7)
         remainders.append((sum_of_chip - leading).astype(BF16))
-        arrived.append(to_chip(leading.astype(BF16)))
-        sums_mine.append(dot(tok_mine, enc_part) + to_core(dot(tok_of_core, enc_part)))
+        leading_b.append(leading.astype(BF16))
+    arrived = [to_chip(piece) for piece in leading_b]
+    ties = [leading_b[0]] * PARTS
+    for index, part in enumerate(parts):
+        enc_part = enc_local[:, part]
+        near, cross, _ = lax.optimization_barrier((tok_mine, tok_of_core, ties[index]))
+        sums_mine.append(dot(near, enc_part) + to_core(dot(cross, enc_part)))
     dec_parts = [dec_local.T[:, part] for part in parts]
     active = {}
     for index, part in enumerate(parts):
@@ -229,27 +229,25 @@
         exact = enc_scale * (sums_mine[index] + terms) + bias[:, part]
         alive.append((exact > 0.0).astype(F32))
     errors = jnp.concatenate([rows_of(whole_errors, start, quarter) for start in starts])
-    dec_step = enc_step = None
-    for index in range(PARTS):
-        pieces = [active[row, index] for row in range(4)]
-        dec_step = write_step(errors, pieces, dec_step, index, -LEARN_RATE * dec_scale)
+    pieces = [[active[row, index] for row in range(4)] for index in range(PARTS)]
+    dec_step = write_step(errors, pieces, -LEARN_RATE * dec_scale)
     grads_arrived[0], dec_step, alive = lax.optimization_barrier((grads_arrived[0], dec_step, alive))
 
-    pres = []
+    pres_mine, pres_of_core, pres_of_chip = [], [], []
     for index in range(PARTS):
         grad_arrived = grads_arrived[index]
         if index:
-            grad_arrived, pres[-1][1] = lax.optimization_barrier((grad_arrived, pres[-1][1]))
+            grad_arrived, pres_of_core[-1] = lax.optimization_barrier((grad_arrived, pres_of_core[-1]))
         grad_act = dec_scale * (grads_mine[index] + grad_arrived.astype(F32))
         pre_mine = jnp.where(alive[index] > 0.0, grad_act, 0.0).astype(BF16)
-        pres.append([pre_mine, to_core(pre_mine), to_chip(pre_mine)])
-        if index:
-            pres[0][2], pres[1][2] = lax.optimization_barrier((pres[0][2], pres[1][2]))
-    all_tokens = jnp.concatenate(token_rows)
-    for index in range(PARTS):
-        pre_mine, pre_of_core, pre_of_chip = pres[index]
-        pieces = [pre_mine, pre_of_core, pre_of_chip, to_core(pre_of_chip)]
-        enc_step = write_step(all_tokens, pieces, enc_step, index, -LEARN_RATE * enc_scale)
+        pres_mine.append(pre_mine)
+        pres_of_core.append(to_core(pre_mine))
+        pres_of_chip.append(to_chip(pre_mine))
+    pres_of_chip = lax.optimization_barrier(pres_of_chip)
+    pieces = [
+        [mine, near, far, to_core(far)] for mine, near, far in zip(pres_mine, pres_of_core, pres_of_chip)
+    ]
+    enc_step = write_step(jnp.concatenate(token_rows), pieces, -LEARN_RATE * enc_scale)
     return (enc_step[None], dec_step.T[None])
 
 

time: 165 us -> 163 us (0.988)
  Pallas kernels: 17.2 us -> 13.9 us
  starting transfers between devices: 65.8 us -> 68.2 us
    ppermute x10, waiting for transfers between devices: 26.7 us -> 23.8 us  [to_chip(): return lax.ppermute(value, 'layer', ACROSS_CHIPS)]
    pallas_call x4 -> x2, Pallas kernels: 7.3 us -> 5.34 us  [write_step(): pl.pallas_call(functools.partial(step_kernel, scale, part_count, piece_co...]
  transfers between devices with their start and end apart: 29 -> 29, of which waited for: 13 -> 14; matrix products, arithmetic and copies ran while one was open for 6% -> 6% of each run, Pallas kernels for 7% -> 5%
where the time goes in v4:
time: 163 us; the launch traced here: 162 us
  starting transfers between devices  68.2 us (42%)
  waiting for transfers between devices  65.2 us (40%)
  Pallas kernels  13.9 us (9%)
  matrix products  6.05 us (4%)
  local copies, waits for them, and re-layouts  4.08 us (3%)
  other arithmetic  3.88 us (2%)
    ppermute x10, waiting for transfers between devices, to_chip(): return lax.ppermute(value, 'layer', ACROSS_CHIPS)  23.8 us
    all_to_all x2, waiting for transfers between devices, gather_tokens(): lax.all_to_all(copies, 'feat', 0, 0, tiled=True)  22.5 us
    ppermute x10, starting transfers between devices, to_chip(): return lax.ppermute(value, 'layer', ACROSS_CHIPS)  21.8 us
    all_to_all x2, starting transfers between devices, gather_tokens(): lax.all_to_all(copies, 'feat', 0, 0, tiled=True)  21.1 us
    ppermute x16, starting transfers between devices, to_core(): return lax.ppermute(value, 'layer', ACROSS_CORES)  19.5 us
    all_to_all x1, waiting for transfers between devices, body(): lax.all_to_all(recon_terms.reshape(blocks, tokens // blocks, model_width)...  14.5 us
    pallas_call x6, Pallas kernels, local_call(): pl.pallas_call(kernel, out_shape=out_shape, in_specs=[SMEM] + [VMEM] * (l...  8.54 us
    dot_general x8, matrix products, dot(): return jnp.dot(left, right, preferred_element_type=F32)  6.05 us
  transfers between devices with their start and end apart: 29, of which 14 were waited for; matrix products, arithmetic and copies ran while one was open for 6% of the time, Pallas kernels for 5%

profile of v4, /device:TPU:1, one launch (start us, length us, event | category | flops | bytes accessed | tf_op | source)
XLA Modules:
  0.0 162.4 jit_solution(17528460044075718364)
XLA Ops:
  0.6 1.6 broadcast_in_dim.26
  2.2 13.7 %all-to-all-start = ((bf16[64,8,576]{2,1,0:T(8,128)(2,1)}), bf16[64,8,576]{2,1,0:T(8,128)(2,1)S(1)}, u32[]{:S(2)}, u32[]{:S(2)}) async-start(bf16[64,8,576]{2,1,0:T(8,128)(2,1)} %broadcast_in_dim.26), calls=%async_computation | async-start | bytes 1310720 | tf_op jit(solution)/shard_map/all_to_all | solution.py:30
  16.0 17.9 %all-to-all-done = bf16[64,8,576]{2,1,0:T(8,128)(2,1)S(1)} async-done(((bf16[64,8,576]{2,1,0:T(8,128)(2,1)}), bf16[64,8,576]{2,1,0:T(8,128)(2,1)S(1)}, u32[]{:S(2)}, u32[]{:S(2)}) %all-to-all-start) | async-done | bytes 589856 | tf_op jit(solution)/shard_map/all_to_all | solution.py:30
  34.4 3.8 %collective-permute-start = (f32[128,1024]{1,0:T(8,128)S(1)}, f32[128,1024]{1,0:T(8,128)S(1)}, u32[]{:S(2)}, u32[]{:S(2)}) collective-permute-start(f32[128,1024]{1,0:T(8,128)S(1)} %fusion.9), channel_id=1, source_target_pairs={{0,64},{64,0},{128,192},{192,128},{1,65},{65,1},{129,193},{193,129... | collective-permute-start | bytes 1572872 | tf_op jit(solution)/shard_map/ppermute | solution.py:19
  40.8 2.4 %collective-permute-start.6 = (bf16[128,1024]{1,0:T(8,128)(2,1)S(1)}, bf16[128,1024]{1,0:T(8,128)(2,1)S(1)}, u32[]{:S(2)}, u32[]{:S(2)}) collective-permute-start(bf16[128,1024]{1,0:T(8,128)(2,1)S(1)} %get-tuple-element.92), channel_id=1, source_target_pairs={{0,128},{64,192},{128,0},{192,64},{1,129},{65,193},{129,1},{193,65... | collective-permute-start | bytes 786440 | tf_op jit(solution)/shard_map/ppermute | solution.py:23
  46.4 3.4 %collective-permute-done.6 = bf16[128,1024]{1,0:T(8,128)(2,1)S(1)} collective-permute-done((bf16[128,1024]{1,0:T(8,128)(2,1)S(1)}, bf16[128,1024]{1,0:T(8,128)(2,1)S(1)}, u32[]{:S(2)}, u32[]{:S(2)}) %collective-permute-start.6) | collective-permute-done | bytes 262176 | tf_op jit(solution)/shard_map/ppermute | solution.py:23
  51.0 2.4 %collective-permute-start.8 = (bf16[128,1024]{1,0:T(8,128)(2,1)S(1)}, bf16[128,1024]{1,0:T(8,128)(2,1)S(1)}, u32[]{:S(2)}, u32[]{:S(2)}) collective-permute-start(bf16[128,1024]{1,0:T(8,128)(2,1)S(1)} %get-tuple-element.98.refs_0_), channel_id=1, source_target_pairs={{0,128},{64,192},{128,0},{192,64},{1,129},{65,193},{129,1},{193,65... | collective-permute-start | bytes 786440 | tf_op jit(solution)/shard_map/ppermute | solution.py:23
  53.5 2.3 %collective-permute-start.7 = (bf16[128,1024]{1,0:T(8,128)(2,1)S(1)}, bf16[128,1024]{1,0:T(8,128)(2,1)S(1)}, u32[]{:S(2)}, u32[]{:S(2)}) collective-permute-start(bf16[128,1024]{1,0:T(8,128)(2,1)S(1)} %get-tuple-element.98.refs_0_), channel_id=1, source_target_pairs={{0,64},{64,0},{128,192},{192,128},{1,65},{65,1},{129,193},{193,129... | collective-permute-start | bytes 786440 | tf_op jit(solution)/shard_map/ppermute | solution.py:19
  57.0 1.3 collective-permute-start.9
  58.3 2.8 %collective-permute-start.4 = (bf16[128,1024]{1,0:T(8,128)(2,1)S(1)}, bf16[128,1024]{1,0:T(8,128)(2,1)S(1)}, u32[]{:S(2)}, u32[]{:S(2)}) collective-permute-start(bf16[128,1024]{1,0:T(8,128)(2,1)S(1)} %get-tuple-element.96.refs_3_.refs_4_), channel_id=1, source_target_pairs={{0,128},{64,192},{128,0},{192,64},{1,129},{65,193},{129,1},{193,65... | collective-permute-start | bytes 786440 | tf_op jit(solution)/shard_map/ppermute | solution.py:23
  63.4 2.0 %shard_map.68.refs_4_ = f32[512,576]{1,0:T(8,128)S(1)} custom-call(s32[4]{0:T(128)S(1)} %pad_add_fusion.starts_ref, bf16[128,1024]{1,0:T(8,128)(2,1)S(1)} %get-tuple-element.98.refs_0_, bf16[128,1024]{1,0:T(8,128)(2,1)S(1)} %collective-permute-done.7.refs_1_, bf16[128,1024]{1,0:T(8,128)(2,1)S(1)} %collective-permute-done.8.refs_2_, ...), custom_call_target="tpu_custom_call" | custom-call | flops 905969664 | bytes 3932176 | tf_op jit(solution)/shard_map/pallas_call | solution.py:55
  65.5 2.3 %collective-permute-done.4.refs_0_.refs_6_ = bf16[128,1024]{1,0:T(8,128)(2,1)S(1)} collective-permute-done((bf16[128,1024]{1,0:T(8,128)(2,1)S(1)}, bf16[128,1024]{1,0:T(8,128)(2,1)S(1)}, u32[]{:S(2)}, u32[]{:S(2)}) %collective-permute-start.4) | collective-permute-done | bytes 262176 | tf_op jit(solution)/shard_map/ppermute | solution.py:23
  69.7 2.0 %shard_map.69 = bf16[512,576]{1,0:T(8,128)(2,1)} custom-call(s32[4]{0:T(128)S(1)} %pad_add_fusion.starts_ref, bf16[128,1024]{1,0:T(8,128)(2,1)S(1)} %collective-permute-done.4.refs_0_.refs_6_, bf16[128,1024]{1,0:T(8,128)(2,1)S(1)} %collective-permute-done.11.refs_1_.refs_7_, bf16[576,1024]{1,0:T(8,128)(2,1)S(1)} %get-tuple-element.81.refs_6_.refs_2_.refs_0_, ...), custom_call_target="tpu_custom_call" | custom-call | flops 301989888 | bytes 4063248 | tf_op jit(solution)/shard_map/pallas_call | solution.py:55
  71.7 5.9 %all-to-all-start.1 = ((bf16[64,8,576]{2,1,0:T(8,128)(2,1)}), bf16[64,8,576]{2,1,0:T(8,128)(2,1)S(1)}, u32[]{:S(2)}, u32[]{:S(2)}) async-start(bf16[64,8,576]{2,1,0:T(8,128)(2,1)} %bitcast.13), calls=%async_computation.1 | async-start | bytes 1310720 | tf_op jit(solution)/shard_map/all_to_all | solution.py:210
  77.6 1.3 reduce
  78.9 2.6 %collective-permute-start.12 = (bf16[128,1024]{1,0:T(8,128)(2,1)}, bf16[128,1024]{1,0:T(8,128)(2,1)}, u32[]{:S(2)}, u32[]{:S(2)}) collective-permute-start(bf16[128,1024]{1,0:T(8,128)(2,1)} %get-tuple-element.46), channel_id=1, source_target_pairs={{0,128},{64,192},{128,0},{192,64},{1,129},{65,193},{129,1},{193,65... | collective-permute-start | bytes 786440 | tf_op jit(solution)/shard_map/ppermute | solution.py:23
  81.5 14.5 %all-to-all-done.1 = bf16[64,8,576]{2,1,0:T(8,128)(2,1)S(1)} async-done(((bf16[64,8,576]{2,1,0:T(8,128)(2,1)}), bf16[64,8,576]{2,1,0:T(8,128)(2,1)S(1)}, u32[]{:S(2)}, u32[]{:S(2)}) %all-to-all-start.1) | async-done | bytes 589856 | tf_op jit(solution)/shard_map/all_to_all | solution.py:210
  97.7 7.3 %all-to-all-start.2 = ((bf16[64,8,576]{2,1,0:T(8,128)(2,1)}), bf16[64,8,576]{2,1,0:T(8,128)(2,1)S(1)}, u32[]{:S(2)}, u32[]{:S(2)}) async-start(bf16[64,8,576]{2,1,0:T(8,128)(2,1)} %broadcast_in_dim.28), calls=%async_computation.2 | async-start | bytes 1310720 | tf_op jit(solution)/shard_map/all_to_all | solution.py:30
  105.0 2.7 %collective-permute-start.13 = (bf16[128,1024]{1,0:T(8,128)(2,1)}, bf16[128,1024]{1,0:T(8,128)(2,1)}, u32[]{:S(2)}, u32[]{:S(2)}) collective-permute-start(bf16[128,1024]{1,0:T(8,128)(2,1)} %get-tuple-element.49), channel_id=1, source_target_pairs={{0,128},{64,192},{128,0},{192,64},{1,129},{65,193},{129,1},{193,65... | collective-permute-start | bytes 786440 | tf_op jit(solution)/shard_map/ppermute | solution.py:23
  107.7 10.0 %collective-permute-done.13 = bf16[128,1024]{1,0:T(8,128)(2,1)} collective-permute-done((bf16[128,1024]{1,0:T(8,128)(2,1)}, bf16[128,1024]{1,0:T(8,128)(2,1)}, u32[]{:S(2)}, u32[]{:S(2)}) %collective-permute-start.13) | collective-permute-done | bytes 262176 | tf_op jit(solution)/shard_map/ppermute | solution.py:23
  117.7 4.6 %all-to-all-done.2 = bf16[64,8,576]{2,1,0:T(8,128)(2,1)S(1)} async-done(((bf16[64,8,576]{2,1,0:T(8,128)(2,1)}), bf16[64,8,576]{2,1,0:T(8,128)(2,1)S(1)}, u32[]{:S(2)}, u32[]{:S(2)}) %all-to-all-start.2) | async-done | bytes 589856 | tf_op jit(solution)/shard_map/all_to_all | solution.py:30
  123.4 4.5 %collective-permute-start.14 = (bf16[128,1024]{1,0:T(8,128)(2,1)S(1)}, bf16[128,1024]{1,0:T(8,128)(2,1)S(1)}, u32[]{:S(2)}, u32[]{:S(2)}) collective-permute-start(bf16[128,1024]{1,0:T(8,128)(2,1)S(1)} %get-tuple-element.54), channel_id=1, source_target_pairs={{0,64},{64,0},{128,192},{192,128},{1,65},{65,1},{129,193},{193,129... | collective-permute-start | bytes 786440 | tf_op jit(solution)/shard_map/ppermute | solution.py:19
  131.0 2.7 %collective-permute-start.16 = (bf16[128,1024]{1,0:T(8,128)(2,1)S(1)}, bf16[128,1024]{1,0:T(8,128)(2,1)S(1)}, u32[]{:S(2)}, u32[]{:S(2)}) collective-permute-start(bf16[128,1024]{1,0:T(8,128)(2,1)S(1)} %get-tuple-element.58), channel_id=1, source_target_pairs={{0,128},{64,192},{128,0},{192,64},{1,129},{65,193},{129,1},{193,65... | collective-permute-start | bytes 786440 | tf_op jit(solution)/shard_map/ppermute | solution.py:23
  136.6 2.7 %shard_map.74 = bf16[576,2048]{1,0:T(8,128)(2,1)} custom-call(bf16[512,576]{1,0:T(8,128)(2,1)S(1)} %pad_maximum_fusion.1.left_ref, bf16[128,1024]{1,0:T(8,128)(2,1)S(1)} %get-tuple-element.98.refs_0_, bf16[128,1024]{1,0:T(8,128)(2,1)S(1)} %copy-done.7, bf16[128,1024]{1,0:T(8,128)(2,1)S(1)} %copy-done.5, bf16[128,1024]{1,0:T(8,128)(2,1)S(1)} %copy-done.11, ...), custom_call_target="tpu_custom_call" | custom-call | flops 1207959552 | bytes 4456448 | tf_op jit(solution)/shard_map/pallas_call | solution.py:132
  139.3 1.3 fusion.30
  140.8 1.5 collective-permute-start.20
  142.4 2.6 %collective-permute-start.21 = (bf16[128,1024]{1,0:T(8,128)(2,1)S(1)}, bf16[128,1024]{1,0:T(8,128)(2,1)S(1)}, u32[]{:S(2)}, u32[]{:S(2)}) collective-permute-start(bf16[128,1024]{1,0:T(8,128)(2,1)S(1)} %select_convert_fusion.1.refs_0_), channel_id=1, source_target_pairs={{0,128},{64,192},{128,0},{192,64},{1,129},{65,193},{129,1},{193,65... | collective-permute-start | bytes 786440 | tf_op jit(solution)/shard_map/ppermute | solution.py:23
  145.8 2.7 %collective-permute-start.22 = (bf16[128,1024]{1,0:T(8,128)(2,1)S(1)}, bf16[128,1024]{1,0:T(8,128)(2,1)S(1)}, u32[]{:S(2)}, u32[]{:S(2)}) collective-permute-start(bf16[128,1024]{1,0:T(8,128)(2,1)S(1)} %select_convert_fusion.refs_4_), channel_id=1, source_target_pairs={{0,128},{64,192},{128,0},{192,64},{1,129},{65,193},{129,1},{193,65... | collective-permute-start | bytes 786440 | tf_op jit(solution)/shard_map/ppermute | solution.py:23
  148.5 1.5 collective-permute-start.24
  150.0 1.7 %collective-permute-done.21.refs_2_ = bf16[128,1024]{1,0:T(8,128)(2,1)S(1)} collective-permute-done((bf16[128,1024]{1,0:T(8,128)(2,1)S(1)}, bf16[128,1024]{1,0:T(8,128)(2,1)S(1)}, u32[]{:S(2)}, u32[]{:S(2)}) %collective-permute-start.21) | collective-permute-done | bytes 262176 | tf_op jit(solution)/shard_map/ppermute | solution.py:23
  151.7 5.6 %collective-permute-done.22.refs_6_ = bf16[128,1024]{1,0:T(8,128)(2,1)S(1)} collective-permute-done((bf16[128,1024]{1,0:T(8,128)(2,1)S(1)}, bf16[128,1024]{1,0:T(8,128)(2,1)S(1)}, u32[]{:S(2)}, u32[]{:S(2)}) %collective-permute-start.22) | collective-permute-done | bytes 262176 | tf_op jit(solution)/shard_map/ppermute | solution.py:23
  159.8 2.7 %shard_map.75 = bf16[576,2048]{1,0:T(8,128)(2,1)} custom-call(bf16[512,576]{1,0:T(8,128)(2,1)S(1)} %pad_maximum_fusion.left_ref, bf16[128,1024]{1,0:T(8,128)(2,1)S(1)} %select_convert_fusion.1.refs_0_, bf16[128,1024]{1,0:T(8,128)(2,1)S(1)} %collective-permute-done.20.refs_1_, bf16[128,1024]{1,0:T(8,128)(2,1)S(1)} %collective-permute-done.21.refs_2_, ...), custom_call_target="tpu_custom_call" | custom-call | flops 1207959552 | bytes 4456448 | tf_op jit(solution)/shard_map/pallas_call | solution.py:132
  (125 shorter events, 24.9 us)
Async XLA Ops:
  2.2 31.8 %copy-start.12 = (bf16[1,576,2048]{2,1,0:T(8,128)(2,1)S(1)}, bf16[1,576,2048]{2,1,0:T(8,128)(2,1)}, u32[]{:S(2)}) copy-start(bf16[1,576,2048]{2,1,0:T(8,128)(2,1)} %param.6) | copy-start | bytes 7077892
  2.2 31.7 %all-to-all-start = ((bf16[64,8,576]{2,1,0:T(8,128)(2,1)}), bf16[64,8,576]{2,1,0:T(8,128)(2,1)S(1)}, u32[]{:S(2)}, u32[]{:S(2)}) async-start(bf16[64,8,576]{2,1,0:T(8,128)(2,1)} %broadcast_in_dim.26), calls=%async_computation | async-start | bytes 1310720 | tf_op jit(solution)/shard_map/all_to_all | solution.py:30
  34.0 21.8 %copy-start.13 = (bf16[128,576]{1,0:T(8,128)(2,1)}, bf16[128,576]{1,0:T(8,128)(2,1)S(1)}, u32[]{:S(2)}) copy-start(bf16[128,576]{1,0:T(8,128)(2,1)S(1)} %get-tuple-element.41) | copy-start | bytes 442372
  34.4 5.3 %collective-permute-start = (f32[128,1024]{1,0:T(8,128)S(1)}, f32[128,1024]{1,0:T(8,128)S(1)}, u32[]{:S(2)}, u32[]{:S(2)}) collective-permute-start(f32[128,1024]{1,0:T(8,128)S(1)} %fusion.9), channel_id=1, source_target_pairs={{0,64},{64,0},{128,192},{192,128},{1,65},{65,1},{129,193},{193,129... | collective-permute-start | bytes 1572872 | tf_op jit(solution)/shard_map/ppermute | solution.py:19
  38.6 6.3 %collective-permute-start.1 = (f32[128,1024]{1,0:T(8,128)S(1)}, f32[128,1024]{1,0:T(8,128)S(1)}, u32[]{:S(2)}, u32[]{:S(2)}) collective-permute-start(f32[128,1024]{1,0:T(8,128)S(1)} %fusion.3), channel_id=1, source_target_pairs={{0,64},{64,0},{128,192},{192,128},{1,65},{65,1},{129,193},{193,129... | collective-permute-start | bytes 1572872 | tf_op jit(solution)/shard_map/ppermute | solution.py:19
  40.8 9.0 %collective-permute-start.6 = (bf16[128,1024]{1,0:T(8,128)(2,1)S(1)}, bf16[128,1024]{1,0:T(8,128)(2,1)S(1)}, u32[]{:S(2)}, u32[]{:S(2)}) collective-permute-start(bf16[128,1024]{1,0:T(8,128)(2,1)S(1)} %get-tuple-element.92), channel_id=1, source_target_pairs={{0,128},{64,192},{128,0},{192,64},{1,129},{65,193},{129,1},{193,65... | collective-permute-start | bytes 786440 | tf_op jit(solution)/shard_map/ppermute | solution.py:23
  43.6 6.2 %collective-permute-start.5 = (f32[128,1024]{1,0:T(8,128)S(1)}, f32[128,1024]{1,0:T(8,128)S(1)}, u32[]{:S(2)}, u32[]{:S(2)}) collective-permute-start(f32[128,1024]{1,0:T(8,128)S(1)} %fusion.6), channel_id=1, source_target_pairs={{0,64},{64,0},{128,192},{192,128},{1,65},{65,1},{129,193},{193,129... | collective-permute-start | bytes 1572872 | tf_op jit(solution)/shard_map/ppermute | solution.py:19
  44.7 11.1 %collective-permute-start.2 = (f32[128,1024]{1,0:T(8,128)S(1)}, f32[128,1024]{1,0:T(8,128)S(1)}, u32[]{:S(2)}, u32[]{:S(2)}) collective-permute-start(f32[128,1024]{1,0:T(8,128)S(1)} %fusion), channel_id=1, source_target_pairs={{0,64},{64,0},{128,192},{192,128},{1,65},{65,1},{129,193},{193,129... | collective-permute-start | bytes 1572872 | tf_op jit(solution)/shard_map/ppermute | solution.py:19
  45.9 9.9 %collective-permute-start.3 = (bf16[128,1024]{1,0:T(8,128)(2,1)S(1)}, bf16[128,1024]{1,0:T(8,128)(2,1)S(1)}, u32[]{:S(2)}, u32[]{:S(2)}) collective-permute-start(bf16[128,1024]{1,0:T(8,128)(2,1)S(1)} %get-tuple-element.90), channel_id=1, source_target_pairs={{0,128},{64,192},{128,0},{192,64},{1,129},{65,193},{129,1},{193,65... | collective-permute-start | bytes 786440 | tf_op jit(solution)/shard_map/ppermute | solution.py:23
  51.0 10.1 %collective-permute-start.8 = (bf16[128,1024]{1,0:T(8,128)(2,1)S(1)}, bf16[128,1024]{1,0:T(8,128)(2,1)S(1)}, u32[]{:S(2)}, u32[]{:S(2)}) collective-permute-start(bf16[128,1024]{1,0:T(8,128)(2,1)S(1)} %get-tuple-element.98.refs_0_), channel_id=1, source_target_pairs={{0,128},{64,192},{128,0},{192,64},{1,129},{65,193},{129,1},{193,65... | collective-permute-start | bytes 786440 | tf_op jit(solution)/shard_map/ppermute | solution.py:23
  53.5 9.1 %collective-permute-start.7 = (bf16[128,1024]{1,0:T(8,128)(2,1)S(1)}, bf16[128,1024]{1,0:T(8,128)(2,1)S(1)}, u32[]{:S(2)}, u32[]{:S(2)}) collective-permute-start(bf16[128,1024]{1,0:T(8,128)(2,1)S(1)} %get-tuple-element.98.refs_0_), channel_id=1, source_target_pairs={{0,64},{64,0},{128,192},{192,128},{1,65},{65,1},{129,193},{193,129... | collective-permute-start | bytes 786440 | tf_op jit(solution)/shard_map/ppermute | solution.py:19
  57.0 5.5 %collective-permute-start.9 = (bf16[128,1024]{1,0:T(8,128)(2,1)S(1)}, bf16[128,1024]{1,0:T(8,128)(2,1)S(1)}, u32[]{:S(2)}, u32[]{:S(2)}) collective-permute-start(bf16[128,1024]{1,0:T(8,128)(2,1)S(1)} %get-tuple-element.96.refs_3_.refs_4_), channel_id=1, source_target_pairs={{0,64},{64,0},{128,192},{192,128},{1,65},{65,1},{129,193},{193,129... | collective-permute-start | bytes 786440 | tf_op jit(solution)/shard_map/ppermute | solution.py:19
  58.3 9.4 %collective-permute-start.4 = (bf16[128,1024]{1,0:T(8,128)(2,1)S(1)}, bf16[128,1024]{1,0:T(8,128)(2,1)S(1)}, u32[]{:S(2)}, u32[]{:S(2)}) collective-permute-start(bf16[128,1024]{1,0:T(8,128)(2,1)S(1)} %get-tuple-element.96.refs_3_.refs_4_), channel_id=1, source_target_pairs={{0,128},{64,192},{128,0},{192,64},{1,129},{65,193},{129,1},{193,65... | collective-permute-start | bytes 786440 | tf_op jit(solution)/shard_map/ppermute | solution.py:23
  61.1 2.3 %collective-permute-start.10 = (bf16[128,1024]{1,0:T(8,128)(2,1)S(1)}, bf16[128,1024]{1,0:T(8,128)(2,1)S(1)}, u32[]{:S(2)}, u32[]{:S(2)}) collective-permute-start(bf16[128,1024]{1,0:T(8,128)(2,1)S(1)} %collective-permute-done.8.refs_2_), channel_id=1, source_target_pairs={{0,64},{64,0},{128,192},{192,128},{1,65},{65,1},{129,193},{193,129... | collective-permute-start | bytes 786440 | tf_op jit(solution)/shard_map/ppermute | solution.py:19
  67.7 1.9 %collective-permute-start.11 = (bf16[128,1024]{1,0:T(8,128)(2,1)S(1)}, bf16[128,1024]{1,0:T(8,128)(2,1)S(1)}, u32[]{:S(2)}, u32[]{:S(2)}) collective-permute-start(bf16[128,1024]{1,0:T(8,128)(2,1)S(1)} %collective-permute-done.4.refs_0_.refs_6_), channel_id=1, source_target_pairs={{0,64},{64,0},{128,192},{192,128},{1,65},{65,1},{129,193},{193,129... | collective-permute-start | bytes 786440 | tf_op jit(solution)/shard_map/ppermute | solution.py:19
  71.7 24.4 %copy-start.28 = (bf16[1,8,576]{2,1,0:T(8,128)(2,1)S(1)}, bf16[1,8,576]{2,1,0:T(8,128)(2,1)}, u32[]{:S(2)}) copy-start(bf16[1,8,576]{2,1,0:T(8,128)(2,1)} %param.5) | copy-start | bytes 27652
  71.7 24.3 %all-to-all-start.1 = ((bf16[64,8,576]{2,1,0:T(8,128)(2,1)}), bf16[64,8,576]{2,1,0:T(8,128)(2,1)S(1)}, u32[]{:S(2)}, u32[]{:S(2)}) async-start(bf16[64,8,576]{2,1,0:T(8,128)(2,1)} %bitcast.13), calls=%async_computation.1 | async-start | bytes 1310720 | tf_op jit(solution)/shard_map/all_to_all | solution.py:210
  78.9 17.9 %collective-permute-start.12 = (bf16[128,1024]{1,0:T(8,128)(2,1)}, bf16[128,1024]{1,0:T(8,128)(2,1)}, u32[]{:S(2)}, u32[]{:S(2)}) collective-permute-start(bf16[128,1024]{1,0:T(8,128)(2,1)} %get-tuple-element.46), channel_id=1, source_target_pairs={{0,128},{64,192},{128,0},{192,64},{1,129},{65,193},{129,1},{193,65... | collective-permute-start | bytes 786440 | tf_op jit(solution)/shard_map/ppermute | solution.py:23
  97.7 24.6 %all-to-all-start.2 = ((bf16[64,8,576]{2,1,0:T(8,128)(2,1)}), bf16[64,8,576]{2,1,0:T(8,128)(2,1)S(1)}, u32[]{:S(2)}, u32[]{:S(2)}) async-start(bf16[64,8,576]{2,1,0:T(8,128)(2,1)} %broadcast_in_dim.28), calls=%async_computation.2 | async-start | bytes 1310720 | tf_op jit(solution)/shard_map/all_to_all | solution.py:30
  105.0 12.7 %collective-permute-start.13 = (bf16[128,1024]{1,0:T(8,128)(2,1)}, bf16[128,1024]{1,0:T(8,128)(2,1)}, u32[]{:S(2)}, u32[]{:S(2)}) collective-permute-start(bf16[128,1024]{1,0:T(8,128)(2,1)} %get-tuple-element.49), channel_id=1, source_target_pairs={{0,128},{64,192},{128,0},{192,64},{1,129},{65,193},{129,1},{193,65... | collective-permute-start | bytes 786440 | tf_op jit(solution)/shard_map/ppermute | solution.py:23
  123.4 6.4 %collective-permute-start.14 = (bf16[128,1024]{1,0:T(8,128)(2,1)S(1)}, bf16[128,1024]{1,0:T(8,128)(2,1)S(1)}, u32[]{:S(2)}, u32[]{:S(2)}) collective-permute-start(bf16[128,1024]{1,0:T(8,128)(2,1)S(1)} %get-tuple-element.54), channel_id=1, source_target_pairs={{0,64},{64,0},{128,192},{192,128},{1,65},{65,1},{129,193},{193,129... | collective-permute-start | bytes 786440 | tf_op jit(solution)/shard_map/ppermute | solution.py:19
  128.0 1.8 %collective-permute-start.15 = (bf16[128,1024]{1,0:T(8,128)(2,1)S(1)}, bf16[128,1024]{1,0:T(8,128)(2,1)S(1)}, u32[]{:S(2)}, u32[]{:S(2)}) collective-permute-start(bf16[128,1024]{1,0:T(8,128)(2,1)S(1)} %get-tuple-element.55), channel_id=1, source_target_pairs={{0,64},{64,0},{128,192},{192,128},{1,65},{65,1},{129,193},{193,129... | collective-permute-start | bytes 786440 | tf_op jit(solution)/shard_map/ppermute | solution.py:19
  129.2 4.8 %collective-permute-start.17 = (bf16[128,1024]{1,0:T(8,128)(2,1)S(1)}, bf16[128,1024]{1,0:T(8,128)(2,1)S(1)}, u32[]{:S(2)}, u32[]{:S(2)}) collective-permute-start(bf16[128,1024]{1,0:T(8,128)(2,1)S(1)} %get-tuple-element.62), channel_id=1, source_target_pairs={{0,64},{64,0},{128,192},{192,128},{1,65},{65,1},{129,193},{193,129... | collective-permute-start | bytes 786440 | tf_op jit(solution)/shard_map/ppermute | solution.py:19
  129.7 4.3 %collective-permute-start.18 = (bf16[128,1024]{1,0:T(8,128)(2,1)S(1)}, bf16[128,1024]{1,0:T(8,128)(2,1)S(1)}, u32[]{:S(2)}, u32[]{:S(2)}) collective-permute-start(bf16[128,1024]{1,0:T(8,128)(2,1)S(1)} %get-tuple-element.63), channel_id=1, source_target_pairs={{0,64},{64,0},{128,192},{192,128},{1,65},{65,1},{129,193},{193,129... | collective-permute-start | bytes 786440 | tf_op jit(solution)/shard_map/ppermute | solution.py:19
  131.0 9.6 %collective-permute-start.16 = (bf16[128,1024]{1,0:T(8,128)(2,1)S(1)}, bf16[128,1024]{1,0:T(8,128)(2,1)S(1)}, u32[]{:S(2)}, u32[]{:S(2)}) collective-permute-start(bf16[128,1024]{1,0:T(8,128)(2,1)S(1)} %get-tuple-element.58), channel_id=1, source_target_pairs={{0,128},{64,192},{128,0},{192,64},{1,129},{65,193},{129,1},{193,65... | collective-permute-start | bytes 786440 | tf_op jit(solution)/shard_map/ppermute | solution.py:23
  133.6 12.0 %collective-permute-start.19 = (bf16[128,1024]{1,0:T(8,128)(2,1)S(1)}, bf16[128,1024]{1,0:T(8,128)(2,1)S(1)}, u32[]{:S(2)}, u32[]{:S(2)}) collective-permute-start(bf16[128,1024]{1,0:T(8,128)(2,1)S(1)} %get-tuple-element.72), channel_id=1, source_target_pairs={{0,128},{64,192},{128,0},{192,64},{1,129},{65,193},{129,1},{193,65... | collective-permute-start | bytes 786440 | tf_op jit(solution)/shard_map/ppermute | solution.py:23
  140.8 4.9 %collective-permute-start.20 = (bf16[128,1024]{1,0:T(8,128)(2,1)S(1)}, bf16[128,1024]{1,0:T(8,128)(2,1)S(1)}, u32[]{:S(2)}, u32[]{:S(2)}) collective-permute-start(bf16[128,1024]{1,0:T(8,128)(2,1)S(1)} %select_convert_fusion.1.refs_0_), channel_id=1, source_target_pairs={{0,64},{64,0},{128,192},{192,128},{1,65},{65,1},{129,193},{193,129... | collective-permute-start | bytes 786440 | tf_op jit(solution)/shard_map/ppermute | solution.py:19
  142.4 9.4 %collective-permute-start.21 = (bf16[128,1024]{1,0:T(8,128)(2,1)S(1)}, bf16[128,1024]{1,0:T(8,128)(2,1)S(1)}, u32[]{:S(2)}, u32[]{:S(2)}) collective-permute-start(bf16[128,1024]{1,0:T(8,128)(2,1)S(1)} %select_convert_fusion.1.refs_0_), channel_id=1, source_target_pairs={{0,128},{64,192},{128,0},{192,64},{1,129},{65,193},{129,1},{193,65... | collective-permute-start | bytes 786440 | tf_op jit(solution)/shard_map/ppermute | solution.py:23
  145.8 11.5 %collective-permute-start.22 = (bf16[128,1024]{1,0:T(8,128)(2,1)S(1)}, bf16[128,1024]{1,0:T(8,128)(2,1)S(1)}, u32[]{:S(2)}, u32[]{:S(2)}) collective-permute-start(bf16[128,1024]{1,0:T(8,128)(2,1)S(1)} %select_convert_fusion.refs_4_), channel_id=1, source_target_pairs={{0,128},{64,192},{128,0},{192,64},{1,129},{65,193},{129,1},{193,65... | collective-permute-start | bytes 786440 | tf_op jit(solution)/shard_map/ppermute | solution.py:23
  148.5 9.8 %collective-permute-start.24 = (bf16[128,1024]{1,0:T(8,128)(2,1)S(1)}, bf16[128,1024]{1,0:T(8,128)(2,1)S(1)}, u32[]{:S(2)}, u32[]{:S(2)}) collective-permute-start(bf16[128,1024]{1,0:T(8,128)(2,1)S(1)} %select_convert_fusion.refs_4_), channel_id=1, source_target_pairs={{0,64},{64,0},{128,192},{192,128},{1,65},{65,1},{129,193},{193,129... | collective-permute-start | bytes 786440 | tf_op jit(solution)/shard_map/ppermute | solution.py:19
  157.3 2.0 %collective-permute-start.23 = (bf16[128,1024]{1,0:T(8,128)(2,1)S(1)}, bf16[128,1024]{1,0:T(8,128)(2,1)S(1)}, u32[]{:S(2)}, u32[]{:S(2)}) collective-permute-start(bf16[128,1024]{1,0:T(8,128)(2,1)S(1)} %collective-permute-done.21.refs_2_), channel_id=1, source_target_pairs={{0,64},{64,0},{128,192},{192,128},{1,65},{65,1},{129,193},{193,129... | collective-permute-start | bytes 786440 | tf_op jit(solution)/shard_map/ppermute | solution.py:19
  158.2 1.5 collective-permute-start.25
  (31 other events, 177.8 us)

commit v5 on v4

--- a/solution.py
+++ b/solution.py
@@ -102,6 +102,27 @@
         if has_terms:
             total += term_refs[part][...].astype(F32)
         out_refs[part][...] = total.astype(out_refs[part].dtype)
+
+
+def back_rows_kernel(rows_of_outputs, rows, part_count, starts_ref, errors_ref, *refs):
+    dec_refs, out_refs = refs[:part_count], refs[part_count:]
+    errors = [errors_ref[pl.ds(pl.multiple_of(starts_ref[row], rows), rows), :] for row in rows_of_outputs]
+    errors = jnp.concatenate(errors, axis=0)
+    for part in range(part_count):
+        total = dot(errors, dec_refs[part][...])
+        for index in range(len(rows_of_outputs)):
+            out_ref = out_refs[index * part_count + part]
+            out_ref[...] = total[index * rows : (index + 1) * rows].astype(out_ref.dtype)
+
+
+def back_rows(starts, rows_of_outputs, errors, dec_parts):
+    rows, count = errors.shape[0] // starts.shape[0], len(dec_parts)
+    model_width, part_width = dec_parts[0].shape
+    kernel = functools.partial(back_rows_kernel, rows_of_outputs, rows, count)
+    out_shape = [jax.ShapeDtypeStruct((rows, part_width), BF16)] * (count * len(rows_of_outputs))
+    flops = 2 * rows * part_width * model_width * len(out_shape)
+    outs = local_call(kernel, out_shape, [starts, errors, *dec_parts], flops)
+    return [outs[index * count : (index + 1) * count] for index in range(len(rows_of_outputs))]
 
 
 def back(starts, row, errors, dec_parts, terms, dtype):
@@ -214,9 +235,7 @@
     error_b = (recon + dec_bias[0] - tok_local.astype(F32)).astype(BF16)
     error_b, arrived_later[0] = lax.optimization_barrier((error_b, arrived_later[0]))
     whole_errors, arrived_later = lax.optimization_barrier((gather_tokens(error_b), arrived_later))
-    of_both_b = back(starts_array, 3, whole_errors, dec_parts, None, BF16)
-    whole_errors, of_both_b = lax.optimization_barrier((whole_errors, of_both_b))
-    of_core_b = back(starts_array, 1, whole_errors, dec_parts, None, BF16)
+    of_both_b, of_core_b = back_rows(starts_array, (3, 1), whole_errors, dec_parts)
     pair_b = back(starts_array, 2, whole_errors, dec_parts, [to_core(term) for term in of_both_b], BF16)
     whole_errors, pair_b = lax.optimization_barrier((whole_errors, pair_b))
     grads_arrived = [to_chip(term) for term in pair_b]

time: 163 us -> 163 us (level)
    pallas_call x6 -> x5, Pallas kernels: 8.54 us -> 7.79 us  [local_call(): pl.pallas_call(kernel, out_shape=out_shape, in_specs=[SMEM] + [VMEM] * (l...]
  transfers between devices with their start and end apart: 29 -> 29, of which waited for: 14 -> 16; matrix products, arithmetic and copies ran while one was open for 6% -> 6% of each run, Pallas kernels for 5% -> 4%
where the time goes in v5:
time: 163 us; the launch traced here: 162 us
  starting transfers between devices  68 us (42%)
  waiting for transfers between devices  66.2 us (41%)
  Pallas kernels  13.1 us (8%)
  matrix products  6.04 us (4%)
  local copies, waits for them, and re-layouts  4.08 us (3%)
  other arithmetic  3.9 us (2%)
    ppermute x10, waiting for transfers between devices, to_chip(): return lax.ppermute(value, 'layer', ACROSS_CHIPS)  23.8 us
    all_to_all x2, waiting for transfers between devices, gather_tokens(): lax.all_to_all(copies, 'feat', 0, 0, tiled=True)  22.5 us
    ppermute x10, starting transfers between devices, to_chip(): return lax.ppermute(value, 'layer', ACROSS_CHIPS)  21.7 us
    all_to_all x2, starting transfers between devices, gather_tokens(): lax.all_to_all(copies, 'feat', 0, 0, tiled=True)  21.1 us
    ppermute x16, starting transfers between devices, to_core(): return lax.ppermute(value, 'layer', ACROSS_CORES)  19.4 us
    all_to_all x1, waiting for transfers between devices, body(): lax.all_to_all(recon_terms.reshape(blocks, tokens // blocks, model_width)...  14.5 us
    pallas_call x5, Pallas kernels, local_call(): pl.pallas_call(kernel, out_shape=out_shape, in_specs=[SMEM] + [VMEM] * (l...  7.79 us
    dot_general x8, matrix products, dot(): return jnp.dot(left, right, preferred_element_type=F32)  6.04 us
  transfers between devices with their start and end apart: 29, of which 16 were waited for; matrix products, arithmetic and copies ran while one was open for 6% of the time, Pallas kernels for 4%

profile of v5, /device:TPU:1, one launch (start us, length us, event | category | flops | bytes accessed | tf_op | source)
XLA Modules:
  0.0 162.5 jit_solution(3542448990475748006)
XLA Ops:
  0.6 1.6 broadcast_in_dim.26
  2.2 13.7 %all-to-all-start = ((bf16[64,8,576]{2,1,0:T(8,128)(2,1)}), bf16[64,8,576]{2,1,0:T(8,128)(2,1)S(1)}, u32[]{:S(2)}, u32[]{:S(2)}) async-start(bf16[64,8,576]{2,1,0:T(8,128)(2,1)} %broadcast_in_dim.26), calls=%async_computation | async-start | bytes 1310720 | tf_op jit(solution)/shard_map/all_to_all | solution.py:30
  16.0 17.9 %all-to-all-done = bf16[64,8,576]{2,1,0:T(8,128)(2,1)S(1)} async-done(((bf16[64,8,576]{2,1,0:T(8,128)(2,1)}), bf16[64,8,576]{2,1,0:T(8,128)(2,1)S(1)}, u32[]{:S(2)}, u32[]{:S(2)}) %all-to-all-start) | async-done | bytes 589856 | tf_op jit(solution)/shard_map/all_to_all | solution.py:30
  34.4 3.8 %collective-permute-start = (f32[128,1024]{1,0:T(8,128)S(1)}, f32[128,1024]{1,0:T(8,128)S(1)}, u32[]{:S(2)}, u32[]{:S(2)}) collective-permute-start(f32[128,1024]{1,0:T(8,128)S(1)} %fusion.9), channel_id=1, source_target_pairs={{0,64},{64,0},{128,192},{192,128},{1,65},{65,1},{129,193},{193,129... | collective-permute-start | bytes 1572872 | tf_op jit(solution)/shard_map/ppermute | solution.py:19
  40.8 2.4 %collective-permute-start.6 = (bf16[128,1024]{1,0:T(8,128)(2,1)S(1)}, bf16[128,1024]{1,0:T(8,128)(2,1)S(1)}, u32[]{:S(2)}, u32[]{:S(2)}) collective-permute-start(bf16[128,1024]{1,0:T(8,128)(2,1)S(1)} %get-tuple-element.86), channel_id=1, source_target_pairs={{0,128},{64,192},{128,0},{192,64},{1,129},{65,193},{129,1},{193,65... | collective-permute-start | bytes 786440 | tf_op jit(solution)/shard_map/ppermute | solution.py:23
  46.4 3.4 %collective-permute-done.6 = bf16[128,1024]{1,0:T(8,128)(2,1)S(1)} collective-permute-done((bf16[128,1024]{1,0:T(8,128)(2,1)S(1)}, bf16[128,1024]{1,0:T(8,128)(2,1)S(1)}, u32[]{:S(2)}, u32[]{:S(2)}) %collective-permute-start.6) | collective-permute-done | bytes 262176 | tf_op jit(solution)/shard_map/ppermute | solution.py:23
  51.0 2.4 %collective-permute-start.8 = (bf16[128,1024]{1,0:T(8,128)(2,1)S(1)}, bf16[128,1024]{1,0:T(8,128)(2,1)S(1)}, u32[]{:S(2)}, u32[]{:S(2)}) collective-permute-start(bf16[128,1024]{1,0:T(8,128)(2,1)S(1)} %get-tuple-element.92.refs_0_), channel_id=1, source_target_pairs={{0,128},{64,192},{128,0},{192,64},{1,129},{65,193},{129,1},{193,65... | collective-permute-start | bytes 786440 | tf_op jit(solution)/shard_map/ppermute | solution.py:23
  53.5 2.3 %collective-permute-start.7 = (bf16[128,1024]{1,0:T(8,128)(2,1)S(1)}, bf16[128,1024]{1,0:T(8,128)(2,1)S(1)}, u32[]{:S(2)}, u32[]{:S(2)}) collective-permute-start(bf16[128,1024]{1,0:T(8,128)(2,1)S(1)} %get-tuple-element.92.refs_0_), channel_id=1, source_target_pairs={{0,64},{64,0},{128,192},{192,128},{1,65},{65,1},{129,193},{193,129... | collective-permute-start | bytes 786440 | tf_op jit(solution)/shard_map/ppermute | solution.py:19
  57.0 1.3 collective-permute-start.9
  58.3 2.8 %collective-permute-start.4 = (bf16[128,1024]{1,0:T(8,128)(2,1)S(1)}, bf16[128,1024]{1,0:T(8,128)(2,1)S(1)}, u32[]{:S(2)}, u32[]{:S(2)}) collective-permute-start(bf16[128,1024]{1,0:T(8,128)(2,1)S(1)} %get-tuple-element.90.refs_3_.refs_4_), channel_id=1, source_target_pairs={{0,128},{64,192},{128,0},{192,64},{1,129},{65,193},{129,1},{193,65... | collective-permute-start | bytes 786440 | tf_op jit(solution)/shard_map/ppermute | solution.py:23
  63.4 2.0 %shard_map.68.refs_4_ = f32[512,576]{1,0:T(8,128)S(1)} custom-call(s32[4]{0:T(128)S(1)} %pad_add_fusion.starts_ref, bf16[128,1024]{1,0:T(8,128)(2,1)S(1)} %get-tuple-element.92.refs_0_, bf16[128,1024]{1,0:T(8,128)(2,1)S(1)} %collective-permute-done.7.refs_1_, bf16[128,1024]{1,0:T(8,128)(2,1)S(1)} %collective-permute-done.8.refs_2_, ...), custom_call_target="tpu_custom_call" | custom-call | flops 905969664 | bytes 3932176 | tf_op jit(solution)/shard_map/pallas_call | solution.py:55
  65.4 2.3 %collective-permute-done.4.refs_0_.refs_6_ = bf16[128,1024]{1,0:T(8,128)(2,1)S(1)} collective-permute-done((bf16[128,1024]{1,0:T(8,128)(2,1)S(1)}, bf16[128,1024]{1,0:T(8,128)(2,1)S(1)}, u32[]{:S(2)}, u32[]{:S(2)}) %collective-permute-start.4) | collective-permute-done | bytes 262176 | tf_op jit(solution)/shard_map/ppermute | solution.py:23
  69.7 2.0 %shard_map.69 = bf16[512,576]{1,0:T(8,128)(2,1)} custom-call(s32[4]{0:T(128)S(1)} %pad_add_fusion.starts_ref, bf16[128,1024]{1,0:T(8,128)(2,1)S(1)} %collective-permute-done.4.refs_0_.refs_6_, bf16[128,1024]{1,0:T(8,128)(2,1)S(1)} %collective-permute-done.11.refs_1_.refs_7_, bf16[576,1024]{1,0:T(8,128)(2,1)S(1)} %get-tuple-element.75.refs_6_.refs_2_.refs_0_, ...), custom_call_target="tpu_custom_call" | custom-call | flops 301989888 | bytes 4063248 | tf_op jit(solution)/shard_map/pallas_call | solution.py:55
  71.7 5.9 %all-to-all-start.1 = ((bf16[64,8,576]{2,1,0:T(8,128)(2,1)}), bf16[64,8,576]{2,1,0:T(8,128)(2,1)S(1)}, u32[]{:S(2)}, u32[]{:S(2)}) async-start(bf16[64,8,576]{2,1,0:T(8,128)(2,1)} %bitcast.13), calls=%async_computation.1 | async-start | bytes 1310720 | tf_op jit(solution)/shard_map/all_to_all | solution.py:231
  78.9 2.6 %collective-permute-start.12 = (bf16[128,1024]{1,0:T(8,128)(2,1)}, bf16[128,1024]{1,0:T(8,128)(2,1)}, u32[]{:S(2)}, u32[]{:S(2)}) collective-permute-start(bf16[128,1024]{1,0:T(8,128)(2,1)} %get-tuple-element.43), channel_id=1, source_target_pairs={{0,128},{64,192},{128,0},{192,64},{1,129},{65,193},{129,1},{193,65... | collective-permute-start | bytes 786440 | tf_op jit(solution)/shard_map/ppermute | solution.py:23
  81.5 14.5 %all-to-all-done.1 = bf16[64,8,576]{2,1,0:T(8,128)(2,1)S(1)} async-done(((bf16[64,8,576]{2,1,0:T(8,128)(2,1)}), bf16[64,8,576]{2,1,0:T(8,128)(2,1)S(1)}, u32[]{:S(2)}, u32[]{:S(2)}) %all-to-all-start.1) | async-done | bytes 589856 | tf_op jit(solution)/shard_map/all_to_all | solution.py:231
  97.7 7.3 %all-to-all-start.2 = ((bf16[64,8,576]{2,1,0:T(8,128)(2,1)}), bf16[64,8,576]{2,1,0:T(8,128)(2,1)S(1)}, u32[]{:S(2)}, u32[]{:S(2)}) async-start(bf16[64,8,576]{2,1,0:T(8,128)(2,1)} %broadcast_in_dim.28), calls=%async_computation.2 | async-start | bytes 1310720 | tf_op jit(solution)/shard_map/all_to_all | solution.py:30
  105.0 2.7 %collective-permute-start.13 = (bf16[128,1024]{1,0:T(8,128)(2,1)}, bf16[128,1024]{1,0:T(8,128)(2,1)}, u32[]{:S(2)}, u32[]{:S(2)}) collective-permute-start(bf16[128,1024]{1,0:T(8,128)(2,1)} %get-tuple-element.46), channel_id=1, source_target_pairs={{0,128},{64,192},{128,0},{192,64},{1,129},{65,193},{129,1},{193,65... | collective-permute-start | bytes 786440 | tf_op jit(solution)/shard_map/ppermute | solution.py:23
  107.7 10.0 %collective-permute-done.13 = bf16[128,1024]{1,0:T(8,128)(2,1)} collective-permute-done((bf16[128,1024]{1,0:T(8,128)(2,1)}, bf16[128,1024]{1,0:T(8,128)(2,1)}, u32[]{:S(2)}, u32[]{:S(2)}) %collective-permute-start.13) | collective-permute-done | bytes 262176 | tf_op jit(solution)/shard_map/ppermute | solution.py:23
  117.7 4.6 %all-to-all-done.2 = bf16[64,8,576]{2,1,0:T(8,128)(2,1)S(1)} async-done(((bf16[64,8,576]{2,1,0:T(8,128)(2,1)}), bf16[64,8,576]{2,1,0:T(8,128)(2,1)S(1)}, u32[]{:S(2)}, u32[]{:S(2)}) %all-to-all-start.2) | async-done | bytes 589856 | tf_op jit(solution)/shard_map/all_to_all | solution.py:30
  122.3 1.5 shard_map.70
  123.9 4.5 %collective-permute-start.14 = (bf16[128,1024]{1,0:T(8,128)(2,1)S(1)}, bf16[128,1024]{1,0:T(8,128)(2,1)S(1)}, u32[]{:S(2)}, u32[]{:S(2)}) collective-permute-start(bf16[128,1024]{1,0:T(8,128)(2,1)S(1)} %get-tuple-element.48), channel_id=1, source_target_pairs={{0,64},{64,0},{128,192},{192,128},{1,65},{65,1},{129,193},{193,129... | collective-permute-start | bytes 786440 | tf_op jit(solution)/shard_map/ppermute | solution.py:19
  131.1 2.7 %collective-permute-start.16 = (bf16[128,1024]{1,0:T(8,128)(2,1)S(1)}, bf16[128,1024]{1,0:T(8,128)(2,1)S(1)}, u32[]{:S(2)}, u32[]{:S(2)}) collective-permute-start(bf16[128,1024]{1,0:T(8,128)(2,1)S(1)} %get-tuple-element.52), channel_id=1, source_target_pairs={{0,128},{64,192},{128,0},{192,64},{1,129},{65,193},{129,1},{193,65... | collective-permute-start | bytes 786440 | tf_op jit(solution)/shard_map/ppermute | solution.py:23
  136.7 2.7 %shard_map.73 = bf16[576,2048]{1,0:T(8,128)(2,1)} custom-call(bf16[512,576]{1,0:T(8,128)(2,1)S(1)} %pad_maximum_fusion.1.left_ref, bf16[128,1024]{1,0:T(8,128)(2,1)S(1)} %get-tuple-element.92.refs_0_, bf16[128,1024]{1,0:T(8,128)(2,1)S(1)} %copy-done.7, bf16[128,1024]{1,0:T(8,128)(2,1)S(1)} %copy-done.5, bf16[128,1024]{1,0:T(8,128)(2,1)S(1)} %copy-done.11, ...), custom_call_target="tpu_custom_call" | custom-call | flops 1207959552 | bytes 4456448 | tf_op jit(solution)/shard_map/pallas_call | solution.py:153
  139.4 1.3 fusion.30
  140.9 1.5 collective-permute-start.20
  142.4 2.6 %collective-permute-start.21 = (bf16[128,1024]{1,0:T(8,128)(2,1)S(1)}, bf16[128,1024]{1,0:T(8,128)(2,1)S(1)}, u32[]{:S(2)}, u32[]{:S(2)}) collective-permute-start(bf16[128,1024]{1,0:T(8,128)(2,1)S(1)} %select_convert_fusion.1.refs_0_), channel_id=1, source_target_pairs={{0,128},{64,192},{128,0},{192,64},{1,129},{65,193},{129,1},{193,65... | collective-permute-start | bytes 786440 | tf_op jit(solution)/shard_map/ppermute | solution.py:23
  145.9 2.7 %collective-permute-start.22 = (bf16[128,1024]{1,0:T(8,128)(2,1)S(1)}, bf16[128,1024]{1,0:T(8,128)(2,1)S(1)}, u32[]{:S(2)}, u32[]{:S(2)}) collective-permute-start(bf16[128,1024]{1,0:T(8,128)(2,1)S(1)} %select_convert_fusion.refs_4_), channel_id=1, source_target_pairs={{0,128},{64,192},{128,0},{192,64},{1,129},{65,193},{129,1},{193,65... | collective-permute-start | bytes 786440 | tf_op jit(solution)/shard_map/ppermute | solution.py:23
  148.6 1.5 collective-permute-start.24
  150.1 1.7 %collective-permute-done.21.refs_2_ = bf16[128,1024]{1,0:T(8,128)(2,1)S(1)} collective-permute-done((bf16[128,1024]{1,0:T(8,128)(2,1)S(1)}, bf16[128,1024]{1,0:T(8,128)(2,1)S(1)}, u32[]{:S(2)}, u32[]{:S(2)}) %collective-permute-start.21) | collective-permute-done | bytes 262176 | tf_op jit(solution)/shard_map/ppermute | solution.py:23
  151.8 5.6 %collective-permute-done.22.refs_6_ = bf16[128,1024]{1,0:T(8,128)(2,1)S(1)} collective-permute-done((bf16[128,1024]{1,0:T(8,128)(2,1)S(1)}, bf16[128,1024]{1,0:T(8,128)(2,1)S(1)}, u32[]{:S(2)}, u32[]{:S(2)}) %collective-permute-start.22) | collective-permute-done | bytes 262176 | tf_op jit(solution)/shard_map/ppermute | solution.py:23
  159.8 2.7 %shard_map.74 = bf16[576,2048]{1,0:T(8,128)(2,1)} custom-call(bf16[512,576]{1,0:T(8,128)(2,1)S(1)} %pad_maximum_fusion.left_ref, bf16[128,1024]{1,0:T(8,128)(2,1)S(1)} %select_convert_fusion.1.refs_0_, bf16[128,1024]{1,0:T(8,128)(2,1)S(1)} %collective-permute-done.20.refs_1_, bf16[128,1024]{1,0:T(8,128)(2,1)S(1)} %collective-permute-done.21.refs_2_, ...), custom_call_target="tpu_custom_call" | custom-call | flops 1207959552 | bytes 4456448 | tf_op jit(solution)/shard_map/pallas_call | solution.py:153
  (124 shorter events, 24.9 us)
Async XLA Ops:
  2.2 31.8 %copy-start.12 = (bf16[1,576,2048]{2,1,0:T(8,128)(2,1)S(1)}, bf16[1,576,2048]{2,1,0:T(8,128)(2,1)}, u32[]{:S(2)}) copy-start(bf16[1,576,2048]{2,1,0:T(8,128)(2,1)} %param.6) | copy-start | bytes 7077892
  2.2 31.7 %all-to-all-start = ((bf16[64,8,576]{2,1,0:T(8,128)(2,1)}), bf16[64,8,576]{2,1,0:T(8,128)(2,1)S(1)}, u32[]{:S(2)}, u32[]{:S(2)}) async-start(bf16[64,8,576]{2,1,0:T(8,128)(2,1)} %broadcast_in_dim.26), calls=%async_computation | async-start | bytes 1310720 | tf_op jit(solution)/shard_map/all_to_all | solution.py:30
  34.0 21.8 %copy-start.13 = (bf16[128,576]{1,0:T(8,128)(2,1)}, bf16[128,576]{1,0:T(8,128)(2,1)S(1)}, u32[]{:S(2)}) copy-start(bf16[128,576]{1,0:T(8,128)(2,1)S(1)} %get-tuple-element.38) | copy-start | bytes 442372
  34.4 5.3 %collective-permute-start = (f32[128,1024]{1,0:T(8,128)S(1)}, f32[128,1024]{1,0:T(8,128)S(1)}, u32[]{:S(2)}, u32[]{:S(2)}) collective-permute-start(f32[128,1024]{1,0:T(8,128)S(1)} %fusion.9), channel_id=1, source_target_pairs={{0,64},{64,0},{128,192},{192,128},{1,65},{65,1},{129,193},{193,129... | collective-permute-start | bytes 1572872 | tf_op jit(solution)/shard_map/ppermute | solution.py:19
  38.6 6.3 %collective-permute-start.1 = (f32[128,1024]{1,0:T(8,128)S(1)}, f32[128,1024]{1,0:T(8,128)S(1)}, u32[]{:S(2)}, u32[]{:S(2)}) collective-permute-start(f32[128,1024]{1,0:T(8,128)S(1)} %fusion.3), channel_id=1, source_target_pairs={{0,64},{64,0},{128,192},{192,128},{1,65},{65,1},{129,193},{193,129... | collective-permute-start | bytes 1572872 | tf_op jit(solution)/shard_map/ppermute | solution.py:19
  40.8 9.0 %collective-permute-start.6 = (bf16[128,1024]{1,0:T(8,128)(2,1)S(1)}, bf16[128,1024]{1,0:T(8,128)(2,1)S(1)}, u32[]{:S(2)}, u32[]{:S(2)}) collective-permute-start(bf16[128,1024]{1,0:T(8,128)(2,1)S(1)} %get-tuple-element.86), channel_id=1, source_target_pairs={{0,128},{64,192},{128,0},{192,64},{1,129},{65,193},{129,1},{193,65... | collective-permute-start | bytes 786440 | tf_op jit(solution)/shard_map/ppermute | solution.py:23
  43.6 6.2 %collective-permute-start.5 = (f32[128,1024]{1,0:T(8,128)S(1)}, f32[128,1024]{1,0:T(8,128)S(1)}, u32[]{:S(2)}, u32[]{:S(2)}) collective-permute-start(f32[128,1024]{1,0:T(8,128)S(1)} %fusion.6), channel_id=1, source_target_pairs={{0,64},{64,0},{128,192},{192,128},{1,65},{65,1},{129,193},{193,129... | collective-permute-start | bytes 1572872 | tf_op jit(solution)/shard_map/ppermute | solution.py:19
  44.7 11.0 %collective-permute-start.2 = (f32[128,1024]{1,0:T(8,128)S(1)}, f32[128,1024]{1,0:T(8,128)S(1)}, u32[]{:S(2)}, u32[]{:S(2)}) collective-permute-start(f32[128,1024]{1,0:T(8,128)S(1)} %fusion), channel_id=1, source_target_pairs={{0,64},{64,0},{128,192},{192,128},{1,65},{65,1},{129,193},{193,129... | collective-permute-start | bytes 1572872 | tf_op jit(solution)/shard_map/ppermute | solution.py:19
  45.9 9.8 %collective-permute-start.3 = (bf16[128,1024]{1,0:T(8,128)(2,1)S(1)}, bf16[128,1024]{1,0:T(8,128)(2,1)S(1)}, u32[]{:S(2)}, u32[]{:S(2)}) collective-permute-start(bf16[128,1024]{1,0:T(8,128)(2,1)S(1)} %get-tuple-element.84), channel_id=1, source_target_pairs={{0,128},{64,192},{128,0},{192,64},{1,129},{65,193},{129,1},{193,65... | collective-permute-start | bytes 786440 | tf_op jit(solution)/shard_map/ppermute | solution.py:23
  51.0 10.1 %collective-permute-start.8 = (bf16[128,1024]{1,0:T(8,128)(2,1)S(1)}, bf16[128,1024]{1,0:T(8,128)(2,1)S(1)}, u32[]{:S(2)}, u32[]{:S(2)}) collective-permute-start(bf16[128,1024]{1,0:T(8,128)(2,1)S(1)} %get-tuple-element.92.refs_0_), channel_id=1, source_target_pairs={{0,128},{64,192},{128,0},{192,64},{1,129},{65,193},{129,1},{193,65... | collective-permute-start | bytes 786440 | tf_op jit(solution)/shard_map/ppermute | solution.py:23
  53.5 9.1 %collective-permute-start.7 = (bf16[128,1024]{1,0:T(8,128)(2,1)S(1)}, bf16[128,1024]{1,0:T(8,128)(2,1)S(1)}, u32[]{:S(2)}, u32[]{:S(2)}) collective-permute-start(bf16[128,1024]{1,0:T(8,128)(2,1)S(1)} %get-tuple-element.92.refs_0_), channel_id=1, source_target_pairs={{0,64},{64,0},{128,192},{192,128},{1,65},{65,1},{129,193},{193,129... | collective-permute-start | bytes 786440 | tf_op jit(solution)/shard_map/ppermute | solution.py:19
  57.0 5.6 %collective-permute-start.9 = (bf16[128,1024]{1,0:T(8,128)(2,1)S(1)}, bf16[128,1024]{1,0:T(8,128)(2,1)S(1)}, u32[]{:S(2)}, u32[]{:S(2)}) collective-permute-start(bf16[128,1024]{1,0:T(8,128)(2,1)S(1)} %get-tuple-element.90.refs_3_.refs_4_), channel_id=1, source_target_pairs={{0,64},{64,0},{128,192},{192,128},{1,65},{65,1},{129,193},{193,129... | collective-permute-start | bytes 786440 | tf_op jit(solution)/shard_map/ppermute | solution.py:19
  58.3 9.4 %collective-permute-start.4 = (bf16[128,1024]{1,0:T(8,128)(2,1)S(1)}, bf16[128,1024]{1,0:T(8,128)(2,1)S(1)}, u32[]{:S(2)}, u32[]{:S(2)}) collective-permute-start(bf16[128,1024]{1,0:T(8,128)(2,1)S(1)} %get-tuple-element.90.refs_3_.refs_4_), channel_id=1, source_target_pairs={{0,128},{64,192},{128,0},{192,64},{1,129},{65,193},{129,1},{193,65... | collective-permute-start | bytes 786440 | tf_op jit(solution)/shard_map/ppermute | solution.py:23
  61.1 2.3 %collective-permute-start.10 = (bf16[128,1024]{1,0:T(8,128)(2,1)S(1)}, bf16[128,1024]{1,0:T(8,128)(2,1)S(1)}, u32[]{:S(2)}, u32[]{:S(2)}) collective-permute-start(bf16[128,1024]{1,0:T(8,128)(2,1)S(1)} %collective-permute-done.8.refs_2_), channel_id=1, source_target_pairs={{0,64},{64,0},{128,192},{192,128},{1,65},{65,1},{129,193},{193,129... | collective-permute-start | bytes 786440 | tf_op jit(solution)/shard_map/ppermute | solution.py:19
  67.8 1.9 %collective-permute-start.11 = (bf16[128,1024]{1,0:T(8,128)(2,1)S(1)}, bf16[128,1024]{1,0:T(8,128)(2,1)S(1)}, u32[]{:S(2)}, u32[]{:S(2)}) collective-permute-start(bf16[128,1024]{1,0:T(8,128)(2,1)S(1)} %collective-permute-done.4.refs_0_.refs_6_), channel_id=1, source_target_pairs={{0,64},{64,0},{128,192},{192,128},{1,65},{65,1},{129,193},{193,129... | collective-permute-start | bytes 786440 | tf_op jit(solution)/shard_map/ppermute | solution.py:19
  71.7 24.4 %copy-start.28 = (bf16[1,8,576]{2,1,0:T(8,128)(2,1)S(1)}, bf16[1,8,576]{2,1,0:T(8,128)(2,1)}, u32[]{:S(2)}) copy-start(bf16[1,8,576]{2,1,0:T(8,128)(2,1)} %param.5) | copy-start | bytes 27652
  71.7 24.3 %all-to-all-start.1 = ((bf16[64,8,576]{2,1,0:T(8,128)(2,1)}), bf16[64,8,576]{2,1,0:T(8,128)(2,1)S(1)}, u32[]{:S(2)}, u32[]{:S(2)}) async-start(bf16[64,8,576]{2,1,0:T(8,128)(2,1)} %bitcast.13), calls=%async_computation.1 | async-start | bytes 1310720 | tf_op jit(solution)/shard_map/all_to_all | solution.py:231
  78.9 17.9 %collective-permute-start.12 = (bf16[128,1024]{1,0:T(8,128)(2,1)}, bf16[128,1024]{1,0:T(8,128)(2,1)}, u32[]{:S(2)}, u32[]{:S(2)}) collective-permute-start(bf16[128,1024]{1,0:T(8,128)(2,1)} %get-tuple-element.43), channel_id=1, source_target_pairs={{0,128},{64,192},{128,0},{192,64},{1,129},{65,193},{129,1},{193,65... | collective-permute-start | bytes 786440 | tf_op jit(solution)/shard_map/ppermute | solution.py:23
  97.7 24.6 %all-to-all-start.2 = ((bf16[64,8,576]{2,1,0:T(8,128)(2,1)}), bf16[64,8,576]{2,1,0:T(8,128)(2,1)S(1)}, u32[]{:S(2)}, u32[]{:S(2)}) async-start(bf16[64,8,576]{2,1,0:T(8,128)(2,1)} %broadcast_in_dim.28), calls=%async_computation.2 | async-start | bytes 1310720 | tf_op jit(solution)/shard_map/all_to_all | solution.py:30
  105.0 12.7 %collective-permute-start.13 = (bf16[128,1024]{1,0:T(8,128)(2,1)}, bf16[128,1024]{1,0:T(8,128)(2,1)}, u32[]{:S(2)}, u32[]{:S(2)}) collective-permute-start(bf16[128,1024]{1,0:T(8,128)(2,1)} %get-tuple-element.46), channel_id=1, source_target_pairs={{0,128},{64,192},{128,0},{192,64},{1,129},{65,193},{129,1},{193,65... | collective-permute-start | bytes 786440 | tf_op jit(solution)/shard_map/ppermute | solution.py:23
  123.9 5.7 %collective-permute-start.14 = (bf16[128,1024]{1,0:T(8,128)(2,1)S(1)}, bf16[128,1024]{1,0:T(8,128)(2,1)S(1)}, u32[]{:S(2)}, u32[]{:S(2)}) collective-permute-start(bf16[128,1024]{1,0:T(8,128)(2,1)S(1)} %get-tuple-element.48), channel_id=1, source_target_pairs={{0,64},{64,0},{128,192},{192,128},{1,65},{65,1},{129,193},{193,129... | collective-permute-start | bytes 786440 | tf_op jit(solution)/shard_map/ppermute | solution.py:19
  128.4 1.5 collective-permute-start.15
  128.5 5.6 %collective-permute-start.17 = (bf16[128,1024]{1,0:T(8,128)(2,1)S(1)}, bf16[128,1024]{1,0:T(8,128)(2,1)S(1)}, u32[]{:S(2)}, u32[]{:S(2)}) collective-permute-start(bf16[128,1024]{1,0:T(8,128)(2,1)S(1)} %get-tuple-element.56), channel_id=1, source_target_pairs={{0,64},{64,0},{128,192},{192,128},{1,65},{65,1},{129,193},{193,129... | collective-permute-start | bytes 786440 | tf_op jit(solution)/shard_map/ppermute | solution.py:19
  128.9 5.2 %collective-permute-start.18 = (bf16[128,1024]{1,0:T(8,128)(2,1)S(1)}, bf16[128,1024]{1,0:T(8,128)(2,1)S(1)}, u32[]{:S(2)}, u32[]{:S(2)}) collective-permute-start(bf16[128,1024]{1,0:T(8,128)(2,1)S(1)} %get-tuple-element.57), channel_id=1, source_target_pairs={{0,64},{64,0},{128,192},{192,128},{1,65},{65,1},{129,193},{193,129... | collective-permute-start | bytes 786440 | tf_op jit(solution)/shard_map/ppermute | solution.py:19
  131.1 9.7 %collective-permute-start.16 = (bf16[128,1024]{1,0:T(8,128)(2,1)S(1)}, bf16[128,1024]{1,0:T(8,128)(2,1)S(1)}, u32[]{:S(2)}, u32[]{:S(2)}) collective-permute-start(bf16[128,1024]{1,0:T(8,128)(2,1)S(1)} %get-tuple-element.52), channel_id=1, source_target_pairs={{0,128},{64,192},{128,0},{192,64},{1,129},{65,193},{129,1},{193,65... | collective-permute-start | bytes 786440 | tf_op jit(solution)/shard_map/ppermute | solution.py:23
  133.7 12.1 %collective-permute-start.19 = (bf16[128,1024]{1,0:T(8,128)(2,1)S(1)}, bf16[128,1024]{1,0:T(8,128)(2,1)S(1)}, u32[]{:S(2)}, u32[]{:S(2)}) collective-permute-start(bf16[128,1024]{1,0:T(8,128)(2,1)S(1)} %get-tuple-element.66), channel_id=1, source_target_pairs={{0,128},{64,192},{128,0},{192,64},{1,129},{65,193},{129,1},{193,65... | collective-permute-start | bytes 786440 | tf_op jit(solution)/shard_map/ppermute | solution.py:23
  140.9 4.9 %collective-permute-start.20 = (bf16[128,1024]{1,0:T(8,128)(2,1)S(1)}, bf16[128,1024]{1,0:T(8,128)(2,1)S(1)}, u32[]{:S(2)}, u32[]{:S(2)}) collective-permute-start(bf16[128,1024]{1,0:T(8,128)(2,1)S(1)} %select_convert_fusion.1.refs_0_), channel_id=1, source_target_pairs={{0,64},{64,0},{128,192},{192,128},{1,65},{65,1},{129,193},{193,129... | collective-permute-start | bytes 786440 | tf_op jit(solution)/shard_map/ppermute | solution.py:19
  142.4 9.4 %collective-permute-start.21 = (bf16[128,1024]{1,0:T(8,128)(2,1)S(1)}, bf16[128,1024]{1,0:T(8,128)(2,1)S(1)}, u32[]{:S(2)}, u32[]{:S(2)}) collective-permute-start(bf16[128,1024]{1,0:T(8,128)(2,1)S(1)} %select_convert_fusion.1.refs_0_), channel_id=1, source_target_pairs={{0,128},{64,192},{128,0},{192,64},{1,129},{65,193},{129,1},{193,65... | collective-permute-start | bytes 786440 | tf_op jit(solution)/shard_map/ppermute | solution.py:23
  145.9 11.5 %collective-permute-start.22 = (bf16[128,1024]{1,0:T(8,128)(2,1)S(1)}, bf16[128,1024]{1,0:T(8,128)(2,1)S(1)}, u32[]{:S(2)}, u32[]{:S(2)}) collective-permute-start(bf16[128,1024]{1,0:T(8,128)(2,1)S(1)} %select_convert_fusion.refs_4_), channel_id=1, source_target_pairs={{0,128},{64,192},{128,0},{192,64},{1,129},{65,193},{129,1},{193,65... | collective-permute-start | bytes 786440 | tf_op jit(solution)/shard_map/ppermute | solution.py:23
  148.6 9.8 %collective-permute-start.24 = (bf16[128,1024]{1,0:T(8,128)(2,1)S(1)}, bf16[128,1024]{1,0:T(8,128)(2,1)S(1)}, u32[]{:S(2)}, u32[]{:S(2)}) collective-permute-start(bf16[128,1024]{1,0:T(8,128)(2,1)S(1)} %select_convert_fusion.refs_4_), channel_id=1, source_target_pairs={{0,64},{64,0},{128,192},{192,128},{1,65},{65,1},{129,193},{193,129... | collective-permute-start | bytes 786440 | tf_op jit(solution)/shard_map/ppermute | solution.py:19
  157.4 2.0 %collective-permute-start.23 = (bf16[128,1024]{1,0:T(8,128)(2,1)S(1)}, bf16[128,1024]{1,0:T(8,128)(2,1)S(1)}, u32[]{:S(2)}, u32[]{:S(2)}) collective-permute-start(bf16[128,1024]{1,0:T(8,128)(2,1)S(1)} %collective-permute-done.21.refs_2_), channel_id=1, source_target_pairs={{0,64},{64,0},{128,192},{192,128},{1,65},{65,1},{129,193},{193,129... | collective-permute-start | bytes 786440 | tf_op jit(solution)/shard_map/ppermute | solution.py:19
  158.3 1.5 collective-permute-start.25
  (31 other events, 177.6 us)
